TPU v7x, 512 devices: a whole 4x8x8 slice. The times are simulated.
512 devices in a mesh: site: 8 (over y), sector: 64 (over z, x, core).
Axes of the slice: x: 4, y: 8, z: 8, core: 2. Of those that a mesh axis runs over, the one named last changes fastest.
Arguments:
- site_blocks: bfloat16 [8, 64, 4, 256, 256], P('site', 'sector'), may hold values from -0.375 to 0.375
- operators: float32 [8, 4, 4, 4], P('site'), may hold values from -2.5 to 2.5
- op_mask: int32 [8, 4, 4, 4], P('site'), may hold values 0 or 1
- coupling: int32 [8, 64, 4], P('site', 'sector'), may hold values 0 or 1
- start_env: bfloat16 [64, 4, 256, 256], P('sector'), may hold values from -6 to 6
Outputs:
- left_envs: bfloat16 [8, 64, 4, 256, 256], P('site', 'sector')
All inputs are finite; a program needn't handle non-finite values. No bound on the sum of `op_mask` or of `coupling` on one device may be relied on, other than what follows from the above.
Results may differ from a plain program's by a relative error of at most 0.034.
Values may be sent and summed in bfloat16 or wider, within the bound.
No kernel may reach another device: no remote copies, remote signals or barrier semaphores. Data moves between devices by JAX's collectives and lax.ppermute only.
A program may use at most 64 MiB of HBM per device.

v0:
```python
import functools

import jax
import jax.numpy as jnp
from jax import lax
from jax.experimental import pallas as pl
from jax.experimental.pallas import tpu as pltpu
from jax.sharding import PartitionSpec as P

AXES = ("site", "sector")
RING = 8
ROUND = (8, 7)


def moved(x, pairs, sectors):
    flat = [(a * sectors + b, c * sectors + d) for (a, b), (c, d) in pairs]
    return lax.ppermute(x, AXES, flat)


def mix_and_multiply(env_ref, a_ref, w_ref, p, mixed_ref, half_ref):
    size = env_ref.shape[-1]
    step = 32
    for i in range(0, size, step):
        rows = [env_ref[w, i : i + step, :].astype(jnp.float32) for w in range(4)]
        for v in range(4):
            total = rows[0] * w_ref[p * 16 + v * 4]
            for w in range(1, 4):
                total = total + rows[w] * w_ref[p * 16 + v * 4 + w]
            mixed_ref[v * size + i : v * size + i + step, :] = total.astype(jnp.bfloat16)
    block = a_ref[pl.ds(pl.multiple_of(p * size, size), size), :]
    half_ref[...] = jnp.dot(
        mixed_ref[...], block, preferred_element_type=jnp.float32
    ).astype(jnp.bfloat16)
    return block


def close(block, half):
    return lax.dot_general(
        block, half, (((0,), (0,)), ((), ())), preferred_element_type=jnp.float32
    )


def one_unit(env_ref, a_ref, w_ref, p, mixed_ref, half_ref, out_ref):
    size = env_ref.shape[-1]
    block = mix_and_multiply(env_ref, a_ref, w_ref, p, mixed_ref, half_ref)
    for v in range(4):
        half = half_ref[v * size : (v + 1) * size, :]
        out_ref[v] = close(block, half).astype(jnp.bfloat16)


def unit_kernel(p_ref, w_ref, env_ref, a_ref, out_ref, mixed_ref, half_ref):
    one_unit(env_ref, a_ref, w_ref, p_ref[0], mixed_ref, half_ref, out_ref)


def pair_kernel(w_ref, env_ref, a_ref, out_ref, mixed_ref, half_ref, mixed2_ref, half2_ref):
    size = env_ref.shape[-1]
    first = mix_and_multiply(env_ref, a_ref, w_ref, 1, mixed_ref, half_ref)
    second = mix_and_multiply(env_ref, a_ref, w_ref, 2, mixed2_ref, half2_ref)
    for v in range(4):
        at = slice(v * size, (v + 1) * size)
        total = close(first, half_ref[at, :]) + close(second, half2_ref[at, :])
        out_ref[v] = total.astype(jnp.bfloat16)


def summed(turn, own_ref, over_ref, swap_ref, edge_ref, env_ref):
    size = env_ref.shape[-1]
    step = 32

    def add(one_ref):
        for v in range(4):
            for i in range(0, size, step):
                at = (v, slice(i, i + step))
                total = (
                    swap_ref[at].astype(jnp.float32)
                    + one_ref[at].astype(jnp.float32)
                    + edge_ref[at].astype(jnp.float32)
                )
                env_ref[at] = total.astype(jnp.bfloat16)

    @pl.when(turn == 1)
    def _():
        add(over_ref)

    @pl.when(turn == 0)
    def _():
        add(own_ref)


def lead_kernel(
    p_ref, w_ref, own_ref, over_ref, swap_ref, edge_ref, a_ref, env_ref, out_ref, mixed_ref, half_ref
):
    summed(p_ref[1], own_ref, over_ref, swap_ref, edge_ref, env_ref)
    one_unit(env_ref, a_ref, w_ref, p_ref[0], mixed_ref, half_ref, out_ref)


def last_kernel(p_ref, own_ref, over_ref, swap_ref, edge_ref, near_ref, far_ref, out_ref, sem):
    @pl.when(p_ref[0] == 0)
    def _():
        summed(p_ref[1], own_ref, over_ref, swap_ref, edge_ref, out_ref)

    @pl.when(p_ref[0] == 1)
    def _():
        copy = pltpu.make_async_copy(near_ref, out_ref, sem)
        copy.start()
        copy.wait()

    @pl.when(p_ref[0] == 2)
    def _():
        copy = pltpu.make_async_copy(far_ref, out_ref, sem)
        copy.start()
        copy.wait()


def pick_kernel(count, p_ref, *refs):
    out_ref, sem = refs[count], refs[count + 1]
    for i in range(count):

        @pl.when(p_ref[0] == i)
        def _():
            copy = pltpu.make_async_copy(refs[i], out_ref, sem)
            copy.start()
            copy.wait()


VMEM = pl.BlockSpec(memory_space=pltpu.VMEM)
SMEM = pl.BlockSpec(memory_space=pltpu.SMEM)
ANY = pl.BlockSpec(memory_space=pl.ANY)
PARAMS = pltpu.CompilerParams(vmem_limit_bytes=24 * 1024 * 1024)


def scratch(count, channels, size):
    return [pltpu.VMEM((channels * size, size), jnp.bfloat16)] * count


def cost(units, arrays):
    return pl.CostEstimate(
        flops=units * 8 * 2 * 256**3, bytes_accessed=arrays * 2**19, transcendentals=0
    )


def local(site_blocks, operators, op_mask, coupling, start_env):
    sites = lax.axis_size("site")
    sectors = lax.axis_size("sector")
    lines = sectors // RING
    row = lax.axis_index("site")
    place = lax.axis_index("sector")
    slot = lax.rem(place, RING)
    odd = lax.rem(place, 2)
    states, size = site_blocks.shape[2], site_blocks.shape[3]
    block_shape = jax.ShapeDtypeStruct(start_env.shape[1:], jnp.bfloat16)
    channels = start_env.shape[1]

    def at(line, slot_at):
        return line * RING + slot_at % RING

    coupled = coupling[0, 0].astype(jnp.float32)
    weights = operators[0] * op_mask[0].astype(jnp.float32) * coupled[None, None, :]
    weights = weights.transpose(2, 1, 0).reshape(-1)
    high = lax.reduce_precision(weights, *ROUND)
    middle = lax.reduce_precision(weights - high, *ROUND)
    low = lax.reduce_precision(weights - high - middle, *ROUND)
    pieces = jnp.stack([high, middle, low]).astype(jnp.bfloat16)
    pieces = jnp.pad(pieces, ((0, 13), (0, size - pieces.shape[1])))
    blocks = site_blocks[0, 0].reshape(states * size, size)
    packed = jnp.concatenate([blocks, pieces], axis=0)

    def weights_of(parcel):
        parts = parcel[states * size : states * size + 3, : weights.shape[0]].astype(jnp.float32)
        return parts[0] + parts[1] + parts[2]

    lane = [(line, u) for line in range(lines) for u in range(RING)]
    parcels = [None] * sites
    parcels[1] = moved(
        packed, [((1, at(z, u)), (0, at(z, u - 1))) for z, u in lane], sectors
    )
    turned = moved(
        packed,
        [((s, at(z, u)), (s, at(z, u - s))) for s in range(2, sites) for z, u in lane],
        sectors,
    )

    def fetch(s, after):
        held, after = lax.optimization_barrier((turned, after))
        pairs = [((s, q), (0, q)) for q in range(sectors)]
        return moved(held, pairs, sectors), after

    def edge_pairs(s):
        pairs = []
        for z, v in lane:
            u = (v + s) % RING
            if v % 2 == 0:
                pairs.append(((0, at(z, v)), (0, at(z, v - 1))))
            elif z + (u >= 6) < lines:
                pairs.append(((0, at(z, v)), (0, at(z + (u >= 6), v + 1))))
        return pairs

    def swap_pairs(s):
        pairs = []
        for z, v in lane:
            u = (v + s) % RING
            if v % 2 == 1:
                pairs.append(((0, at(z, v)), (0, at(z, v - 1))))
            elif z + (u >= 6) < lines:
                pairs.append(((0, at(z, v)), (0, at(z + (u >= 6), v + 1))))
        return pairs

    def over_pairs(s):
        v = (RING - 1 - s) % RING
        return [((0, at(z, v)), (0, at(z + 1, v))) for z in range(lines - 1)]

    edge_state = jnp.stack([3 * odd])
    swap_state = jnp.stack([3 * (1 - odd)])
    current = start_env[0]
    kept = {}
    for s in range(sites):
        if s == 0:
            parcel, scales = blocks, weights
            edge = pl.pallas_call(
                unit_kernel,
                out_shape=block_shape,
                in_specs=[SMEM, SMEM, VMEM, VMEM],
                out_specs=VMEM,
                scratch_shapes=scratch(2, channels, size),
                compiler_params=PARAMS,
                cost_estimate=cost(1, 4),
                name="first",
            )(edge_state, scales, current, parcel)
        else:
            parcel = parcels[s]
            scales = weights_of(parcel)
            turn = (lax.rem(slot + s - 1, RING) == RING - 1).astype(jnp.int32)
            current, edge = pl.pallas_call(
                lead_kernel,
                out_shape=(block_shape, block_shape),
                in_specs=[SMEM, SMEM, VMEM, VMEM, VMEM, VMEM, VMEM],
                out_specs=(VMEM, VMEM),
                scratch_shapes=scratch(2, channels, size),
                compiler_params=PARAMS,
                cost_estimate=cost(1, 6),
                name="lead",
            )(jnp.stack([3 * odd, turn]), scales, own, over, swap, edge_in, parcel)
            kept[s] = current
        edge_in = moved(edge, edge_pairs(s), sectors)
        inner = pl.pallas_call(
            unit_kernel,
            out_shape=block_shape,
            in_specs=[SMEM, SMEM, VMEM, VMEM],
            out_specs=VMEM,
            scratch_shapes=scratch(2, channels, size),
            compiler_params=PARAMS,
            cost_estimate=cost(1, 4),
            name="inner",
        )(swap_state, scales, current, parcel)
        swap = moved(inner, swap_pairs(s), sectors)
        own = pl.pallas_call(
            pair_kernel,
            out_shape=block_shape,
            in_specs=[SMEM, VMEM, VMEM],
            out_specs=VMEM,
            scratch_shapes=scratch(4, channels, size),
            compiler_params=PARAMS,
            cost_estimate=cost(2, 4),
            name="stay",
        )(scales, current, parcel)
        over = moved(own, over_pairs(s), sectors)
        for ahead in ([2, 3] if s == 0 else [s + 3]):
            if ahead < sites:
                parcels[ahead], own = fetch(ahead, own)

    near = min(6, sites)
    raised = [
        moved(kept[r], [((0, q), (r, q)) for q in range(sectors)], sectors)
        for r in range(1, near)
    ]
    picked = pl.pallas_call(
        functools.partial(pick_kernel, len(raised)),
        out_shape=block_shape,
        in_specs=[SMEM] + [ANY] * len(raised),
        out_specs=ANY,
        scratch_shapes=[pltpu.SemaphoreType.DMA],
        name="pick",
    )(jnp.stack([row - 1]), *raised)
    homeward = moved(
        picked,
        [((r, at(z, u - r)), (r, at(z, u))) for r in range(1, near) for z, u in lane],
        sectors,
    )
    direct = [
        moved(kept[r], [((0, at(z, u - r)), (r, at(z, u))) for z, u in lane], sectors)
        for r in range(near, sites)
    ]
    straight = pl.pallas_call(
        functools.partial(pick_kernel, len(direct)),
        out_shape=block_shape,
        in_specs=[SMEM] + [ANY] * len(direct),
        out_specs=ANY,
        scratch_shapes=[pltpu.SemaphoreType.DMA],
        name="pick_late",
    )(jnp.stack([row - near]), *direct)
    turn = (lax.rem(slot + sites - 1, RING) == RING - 1).astype(jnp.int32)
    kind = jnp.where(row == 0, 0, jnp.where(row < near, 1, 2))
    out = pl.pallas_call(
        last_kernel,
        out_shape=block_shape,
        in_specs=[SMEM] + [VMEM] * 4 + [ANY] * 2,
        out_specs=VMEM,
        scratch_shapes=[pltpu.SemaphoreType.DMA],
        compiler_params=PARAMS,
        name="last",
    )(jnp.stack([kind, turn]), own, over, swap, edge_in, homeward, straight)
    return out[None, None]


def solution(mesh):
    return jax.shard_map(
        local,
        mesh=mesh,
        in_specs=(
            P("site", "sector", None, None, None),
            P("site", None, None, None),
            P("site", None, None, None),
            P("site", "sector", None),
            P("sector", None, None, None),
        ),
        out_specs=P("site", "sector", None, None, None),
        check_vma=False,
    )
```

profile of v0, /device:TPU:121, one launch (start us, length us, event | category | flops | bytes accessed | tf_op | source)
XLA Modules:
  0.0 234.2 jit_solution(7234713063594745428)
XLA Ops:
  1.6 2.0 pad_maximum_fusion
  3.6 3.7 %collective-permute-start = (bf16[1040,256]{1,0:T(8,128)(2,1)}, bf16[1040,256]{1,0:T(8,128)(2,1)}, u32[]{:S(2)}, u32[]{:S(2)}) collective-permute-start(bf16[1040,256]{1,0:T(8,128)(2,1)} %pad_maximum_fusion), channel_id=1, source_target_pairs={{128,134},{129,135},{130,128},{131,129},{132,130},{133,131},{134,1... | collective-permute-start | bytes 1597448 | tf_op jit(solution)/shard_map/ppermute | solution.py:17
  8.1 2.0 inner.8
  10.8 2.0 first.1
  16.6 1.8 lead.7
  20.8 2.0 stay.9.own_ref
  25.1 1.8 lead.8
  27.0 1.7 inner.10
  29.4 2.0 stay.10.own_ref
  33.7 1.9 lead.9
  35.5 1.7 inner.11
  38.1 2.1 stay.11.own_ref
  42.4 1.8 lead.10
  46.6 2.0 stay.12.own_ref
  50.9 2.2 lead.11
  60.9 88.4 %collective-permute-start.17 = (bf16[1040,256]{1,0:T(8,128)(2,1)}, bf16[1040,256]{1,0:T(8,128)(2,1)S(1)}, u32[]{:S(2)}, u32[]{:S(2)}) collective-permute-start(bf16[1040,256]{1,0:T(8,128)(2,1)} %collective-permute-done), channel_id=1, source_target_pairs={{448,0},{449,1},{450,2},{451,3},{452,4},{453,5},{454,6},{455,7},{4... | collective-permute-start | bytes 1597448 | tf_op jit(solution)/shard_map/ppermute | solution.py:17
  149.3 2.2 lead.12
  151.4 2.5 %inner.14 = bf16[4,256,256]{2,1,0:T(8,128)(2,1)} custom-call(s32[1]{0:T(128)} %bitcast.10.p_ref, f32[64]{0:T(128)S(1)} %add_bitcast_fusion.1.w_ref, bf16[4,256,256]{2,1,0:T(8,128)(2,1)} %get-tuple-element.53.env_ref, bf16[1040,256]{1,0:T(8,128)(2,1)S(1)} %collective-permute-done.18.a_ref), custom_call_target="tpu_custom_call" | custom-call | flops 268435456 | bytes 2097152 | tf_op jit(solution)/shard_map/inner/pallas_call | solution.py:244
  153.9 2.1 stay.14.own_ref
  162.1 2.4 %lead.13 = (bf16[4,256,256]{2,1,0:T(8,128)(2,1)}, bf16[4,256,256]{2,1,0:T(8,128)(2,1)}) custom-call(s32[2]{0:T(128)S(1)} %pad_add_fusion.5.p_ref, f32[64]{0:T(128)S(1)} %add_bitcast_fusion.2.w_ref, bf16[4,256,256]{2,1,0:T(8,128)(2,1)S(1)} %stay.14.own_ref, bf16[4,256,256]{2,1,0:T(8,128)(2,1)S(1)} %collective-permute-done.26.over_ref, ...), custom_call_target="tpu_custom_call" | custom-call | flops 268435456 | bytes 3145728 | tf_op jit(solution)/shard_map/lead/pallas_call | solution.py:232
  165.8 1.7 inner.15
  168.2 2.1 stay.15.own_ref
  171.7 42.8 %collective-permute-done.39.refs_1_ = bf16[4,256,256]{2,1,0:T(8,128)(2,1)} collective-permute-done((bf16[4,256,256]{2,1,0:T(8,128)(2,1)}, bf16[4,256,256]{2,1,0:T(8,128)(2,1)}, u32[]{:S(2)}, u32[]{:S(2)}) %collective-permute-start.39) | collective-permute-done | bytes 524320 | tf_op jit(solution)/shard_map/ppermute | solution.py:17
  214.6 17.0 %pick_late.1.far_ref = bf16[4,256,256]{2,1,0:T(8,128)(2,1)} custom-call(s32[1]{0:T(128)} %bitcast.24.p_ref, bf16[4,256,256]{2,1,0:T(8,128)(2,1)} %collective-permute-done.38.refs_0_, bf16[4,256,256]{2,1,0:T(8,128)(2,1)} %collective-permute-done.39.refs_1_), custom_call_target="tpu_custom_call" | custom-call | tf_op jit(solution)/shard_map/pick_late/pallas_call | solution.py:292
  (133 shorter events, 41.2 us)
Async XLA Ops:
  3.6 12.2 %collective-permute-start = (bf16[1040,256]{1,0:T(8,128)(2,1)}, bf16[1040,256]{1,0:T(8,128)(2,1)}, u32[]{:S(2)}, u32[]{:S(2)}) collective-permute-start(bf16[1040,256]{1,0:T(8,128)(2,1)} %pad_maximum_fusion), channel_id=1, source_target_pairs={{128,134},{129,135},{130,128},{131,129},{132,130},{133,131},{134,1... | collective-permute-start | bytes 1597448 | tf_op jit(solution)/shard_map/ppermute | solution.py:17
  7.3 9.2 %collective-permute-start.1 = (bf16[1040,256]{1,0:T(8,128)(2,1)}, bf16[1040,256]{1,0:T(8,128)(2,1)S(1)}, u32[]{:S(2)}, u32[]{:S(2)}) collective-permute-start(bf16[1040,256]{1,0:T(8,128)(2,1)} %pad_maximum_fusion), channel_id=1, source_target_pairs={{64,7},{65,0},{66,1},{67,2},{68,3},{69,4},{70,5},{71,6},{72,15},{7... | collective-permute-start | bytes 1597448 | tf_op jit(solution)/shard_map/ppermute | solution.py:17
  10.1 6.5 %collective-permute-start.3 = (bf16[4,256,256]{2,1,0:T(8,128)(2,1)}, bf16[4,256,256]{2,1,0:T(8,128)(2,1)S(1)}, u32[]{:S(2)}, u32[]{:S(2)}) collective-permute-start(bf16[4,256,256]{2,1,0:T(8,128)(2,1)} %inner.8), channel_id=1, source_target_pairs={{0,1},{1,0},{2,3},{3,2},{4,5},{5,4},{6,15},{7,6},{8,9},{9,8},{10,1... | collective-permute-start | bytes 1572872 | tf_op jit(solution)/shard_map/ppermute | solution.py:17
  15.8 9.2 %collective-permute-start.7 = (bf16[1040,256]{1,0:T(8,128)(2,1)}, bf16[1040,256]{1,0:T(8,128)(2,1)S(1)}, u32[]{:S(2)}, u32[]{:S(2)}) collective-permute-start(bf16[1040,256]{1,0:T(8,128)(2,1)} %collective-permute-done), channel_id=1, source_target_pairs={{128,0},{129,1},{130,2},{131,3},{132,4},{133,5},{134,6},{135,7},{1... | collective-permute-start | bytes 1597448 | tf_op jit(solution)/shard_map/ppermute | solution.py:17
  24.4 9.2 %collective-permute-start.6 = (bf16[1040,256]{1,0:T(8,128)(2,1)}, bf16[1040,256]{1,0:T(8,128)(2,1)S(1)}, u32[]{:S(2)}, u32[]{:S(2)}) collective-permute-start(bf16[1040,256]{1,0:T(8,128)(2,1)} %collective-permute-done), channel_id=1, source_target_pairs={{192,0},{193,1},{194,2},{195,3},{196,4},{197,5},{198,6},{199,7},{2... | collective-permute-start | bytes 1597448 | tf_op jit(solution)/shard_map/ppermute | solution.py:17
  28.7 5.0 %collective-permute-start.12 = (bf16[4,256,256]{2,1,0:T(8,128)(2,1)S(1)}, bf16[4,256,256]{2,1,0:T(8,128)(2,1)S(1)}, u32[]{:S(2)}, u32[]{:S(2)}) collective-permute-start(bf16[4,256,256]{2,1,0:T(8,128)(2,1)S(1)} %inner.10), channel_id=1, source_target_pairs={{0,1},{1,0},{2,3},{3,2},{4,13},{5,4},{6,7},{7,6},{8,9},{9,8},{10,1... | collective-permute-start | bytes 1572872 | tf_op jit(solution)/shard_map/ppermute | solution.py:17
  32.9 9.4 %collective-permute-start.5 = (bf16[1040,256]{1,0:T(8,128)(2,1)}, bf16[1040,256]{1,0:T(8,128)(2,1)S(1)}, u32[]{:S(2)}, u32[]{:S(2)}) collective-permute-start(bf16[1040,256]{1,0:T(8,128)(2,1)} %collective-permute-done), channel_id=1, source_target_pairs={{256,0},{257,1},{258,2},{259,3},{260,4},{261,5},{262,6},{263,7},{2... | collective-permute-start | bytes 1597448 | tf_op jit(solution)/shard_map/ppermute | solution.py:17
  37.2 5.2 %collective-permute-start.15 = (bf16[4,256,256]{2,1,0:T(8,128)(2,1)S(1)}, bf16[4,256,256]{2,1,0:T(8,128)(2,1)S(1)}, u32[]{:S(2)}, u32[]{:S(2)}) collective-permute-start(bf16[4,256,256]{2,1,0:T(8,128)(2,1)S(1)} %inner.11), channel_id=1, source_target_pairs={{0,1},{1,0},{2,3},{3,2},{4,13},{5,4},{6,7},{7,6},{8,9},{9,8},{10,1... | collective-permute-start | bytes 1572872 | tf_op jit(solution)/shard_map/ppermute | solution.py:17
  41.6 9.2 %collective-permute-start.19 = (bf16[1040,256]{1,0:T(8,128)(2,1)}, bf16[1040,256]{1,0:T(8,128)(2,1)S(1)}, u32[]{:S(2)}, u32[]{:S(2)}) collective-permute-start(bf16[1040,256]{1,0:T(8,128)(2,1)} %collective-permute-done), channel_id=1, source_target_pairs={{320,0},{321,1},{322,2},{323,3},{324,4},{325,5},{326,6},{327,7},{3... | collective-permute-start | bytes 1597448 | tf_op jit(solution)/shard_map/ppermute | solution.py:17
  45.9 5.0 %collective-permute-start.21 = (bf16[4,256,256]{2,1,0:T(8,128)(2,1)S(1)}, bf16[4,256,256]{2,1,0:T(8,128)(2,1)S(1)}, u32[]{:S(2)}, u32[]{:S(2)}) collective-permute-start(bf16[4,256,256]{2,1,0:T(8,128)(2,1)S(1)} %inner.12), channel_id=1, source_target_pairs={{0,1},{1,0},{2,11},{3,2},{4,5},{5,4},{6,7},{7,6},{8,9},{9,8},{10,1... | collective-permute-start | bytes 1572872 | tf_op jit(solution)/shard_map/ppermute | solution.py:17
  50.1 8.6 %collective-permute-start.18 = (bf16[1040,256]{1,0:T(8,128)(2,1)}, bf16[1040,256]{1,0:T(8,128)(2,1)S(1)}, u32[]{:S(2)}, u32[]{:S(2)}) collective-permute-start(bf16[1040,256]{1,0:T(8,128)(2,1)} %collective-permute-done), channel_id=1, source_target_pairs={{384,0},{385,1},{386,2},{387,3},{388,4},{389,5},{390,6},{391,7},{3... | collective-permute-start | bytes 1597448 | tf_op jit(solution)/shard_map/ppermute | solution.py:17
  54.3 5.2 %collective-permute-start.24 = (bf16[4,256,256]{2,1,0:T(8,128)(2,1)S(1)}, bf16[4,256,256]{2,1,0:T(8,128)(2,1)S(1)}, u32[]{:S(2)}, u32[]{:S(2)}) collective-permute-start(bf16[4,256,256]{2,1,0:T(8,128)(2,1)S(1)} %inner.13), channel_id=1, source_target_pairs={{0,1},{1,0},{2,11},{3,2},{4,5},{5,4},{6,7},{7,6},{8,9},{9,8},{10,1... | collective-permute-start | bytes 1572872 | tf_op jit(solution)/shard_map/ppermute | solution.py:17
  58.0 98.0 %collective-permute-start.32 = (bf16[4,256,256]{2,1,0:T(8,128)(2,1)}, bf16[4,256,256]{2,1,0:T(8,128)(2,1)S(1)}, u32[]{:S(2)}, u32[]{:S(2)}) collective-permute-start(bf16[4,256,256]{2,1,0:T(8,128)(2,1)} %get-tuple-element.33.env_ref), channel_id=1, source_target_pairs={{0,64},{1,65},{2,66},{3,67},{4,68},{5,69},{6,70},{7,71},{8,72},{9,... | collective-permute-start | bytes 1572872 | tf_op jit(solution)/shard_map/ppermute | solution.py:17
  58.7 98.1 %collective-permute-start.33 = (bf16[4,256,256]{2,1,0:T(8,128)(2,1)}, bf16[4,256,256]{2,1,0:T(8,128)(2,1)S(1)}, u32[]{:S(2)}, u32[]{:S(2)}) collective-permute-start(bf16[4,256,256]{2,1,0:T(8,128)(2,1)} %get-tuple-element.39.env_ref), channel_id=1, source_target_pairs={{0,128},{1,129},{2,130},{3,131},{4,132},{5,133},{6,134},{7,135},{8... | collective-permute-start | bytes 1572872 | tf_op jit(solution)/shard_map/ppermute | solution.py:17
  59.4 98.1 %collective-permute-start.34 = (bf16[4,256,256]{2,1,0:T(8,128)(2,1)}, bf16[4,256,256]{2,1,0:T(8,128)(2,1)S(1)}, u32[]{:S(2)}, u32[]{:S(2)}) collective-permute-start(bf16[4,256,256]{2,1,0:T(8,128)(2,1)} %get-tuple-element.42.env_ref), channel_id=1, source_target_pairs={{0,192},{1,193},{2,194},{3,195},{4,196},{5,197},{6,198},{7,199},{8... | collective-permute-start | bytes 1572872 | tf_op jit(solution)/shard_map/ppermute | solution.py:17
  60.1 98.1 %collective-permute-start.35 = (bf16[4,256,256]{2,1,0:T(8,128)(2,1)}, bf16[4,256,256]{2,1,0:T(8,128)(2,1)S(1)}, u32[]{:S(2)}, u32[]{:S(2)}) collective-permute-start(bf16[4,256,256]{2,1,0:T(8,128)(2,1)} %get-tuple-element.45.env_ref), channel_id=1, source_target_pairs={{0,256},{1,257},{2,258},{3,259},{4,260},{5,261},{6,262},{7,263},{8... | collective-permute-start | bytes 1572872 | tf_op jit(solution)/shard_map/ppermute | solution.py:17
  60.9 98.2 %collective-permute-start.17 = (bf16[1040,256]{1,0:T(8,128)(2,1)}, bf16[1040,256]{1,0:T(8,128)(2,1)S(1)}, u32[]{:S(2)}, u32[]{:S(2)}) collective-permute-start(bf16[1040,256]{1,0:T(8,128)(2,1)} %collective-permute-done), channel_id=1, source_target_pairs={{448,0},{449,1},{450,2},{451,3},{452,4},{453,5},{454,6},{455,7},{4... | collective-permute-start | bytes 1597448 | tf_op jit(solution)/shard_map/ppermute | solution.py:17
  156.8 5.3 %collective-permute-start.27 = (bf16[4,256,256]{2,1,0:T(8,128)(2,1)}, bf16[4,256,256]{2,1,0:T(8,128)(2,1)S(1)}, u32[]{:S(2)}, u32[]{:S(2)}) collective-permute-start(bf16[4,256,256]{2,1,0:T(8,128)(2,1)} %inner.14), channel_id=1, source_target_pairs={{0,9},{1,0},{2,3},{3,2},{4,5},{5,4},{6,7},{7,6},{8,17},{9,8},{10,1... | collective-permute-start | bytes 1572872 | tf_op jit(solution)/shard_map/ppermute | solution.py:17
  159.0 11.9 %collective-permute-start.38 = (bf16[4,256,256]{2,1,0:T(8,128)(2,1)}, bf16[4,256,256]{2,1,0:T(8,128)(2,1)}, u32[]{:S(2)}, u32[]{:S(2)}) collective-permute-start(bf16[4,256,256]{2,1,0:T(8,128)(2,1)} %get-tuple-element.53.env_ref), channel_id=1, source_target_pairs={{2,384},{3,385},{4,386},{5,387},{6,388},{7,389},{0,390},{1,391},{1... | collective-permute-start | bytes 1572872 | tf_op jit(solution)/shard_map/ppermute | solution.py:17
  161.4 70.2 %collective-permute-start.37 = (bf16[4,256,256]{2,1,0:T(8,128)(2,1)}, bf16[4,256,256]{2,1,0:T(8,128)(2,1)S(1)}, u32[]{:S(2)}, u32[]{:S(2)}) collective-permute-start(bf16[4,256,256]{2,1,0:T(8,128)(2,1)} %pick.1), channel_id=1, source_target_pairs={{71,64},{64,65},{65,66},{66,67},{67,68},{68,69},{69,70},{70,71},{7... | collective-permute-start | bytes 1572872 | tf_op jit(solution)/shard_map/ppermute | solution.py:17
  164.5 50.1 %collective-permute-start.39 = (bf16[4,256,256]{2,1,0:T(8,128)(2,1)}, bf16[4,256,256]{2,1,0:T(8,128)(2,1)}, u32[]{:S(2)}, u32[]{:S(2)}) collective-permute-start(bf16[4,256,256]{2,1,0:T(8,128)(2,1)} %get-tuple-element.55.env_ref), channel_id=1, source_target_pairs={{1,448},{2,449},{3,450},{4,451},{5,452},{6,453},{7,454},{0,455},{9... | collective-permute-start | bytes 1572872 | tf_op jit(solution)/shard_map/ppermute | solution.py:17
  167.5 64.1 %collective-permute-start.30 = (bf16[4,256,256]{2,1,0:T(8,128)(2,1)S(1)}, bf16[4,256,256]{2,1,0:T(8,128)(2,1)S(1)}, u32[]{:S(2)}, u32[]{:S(2)}) collective-permute-start(bf16[4,256,256]{2,1,0:T(8,128)(2,1)S(1)} %inner.15), channel_id=1, source_target_pairs={{0,9},{1,0},{2,3},{3,2},{4,5},{5,4},{6,7},{7,6},{8,17},{9,8},{10,1... | collective-permute-start | bytes 1572872 | tf_op jit(solution)/shard_map/ppermute | solution.py:17
  170.2 61.4 %collective-permute-start.29 = (bf16[4,256,256]{2,1,0:T(8,128)(2,1)S(1)}, bf16[4,256,256]{2,1,0:T(8,128)(2,1)S(1)}, u32[]{:S(2)}, u32[]{:S(2)}) collective-permute-start(bf16[4,256,256]{2,1,0:T(8,128)(2,1)S(1)} %stay.15.own_ref), channel_id=1, source_target_pairs={{0,8},{8,16},{16,24},{24,32},{32,40},{40,48},{48,56}} | collective-permute-start | bytes 1572872 | tf_op jit(solution)/shard_map/ppermute | solution.py:17
  170.9 60.7 %collective-permute-start.31 = (bf16[4,256,256]{2,1,0:T(8,128)(2,1)}, bf16[4,256,256]{2,1,0:T(8,128)(2,1)S(1)}, u32[]{:S(2)}, u32[]{:S(2)}) collective-permute-start(bf16[4,256,256]{2,1,0:T(8,128)(2,1)} %get-tuple-element.56), channel_id=1, source_target_pairs={{0,7},{1,2},{2,1},{3,4},{4,3},{5,6},{6,5},{7,8},{8,15},{9,10},{10,... | collective-permute-start | bytes 1572872 | tf_op jit(solution)/shard_map/ppermute | solution.py:17
  (26 other events, 77.8 us)
where the time goes:
time: 236 us; the launch traced here: 234 us
  starting transfers between devices  120 us (51%)
  Pallas kernels  63.9 us (27%)
  waiting for transfers between devices  42.9 us (18%)
  other arithmetic  4.07 us (2%)
    ppermute x40, starting transfers between devices, moved(): return lax.ppermute(x, AXES, flat)  120 us
    ppermute x40, waiting for transfers between devices, moved(): return lax.ppermute(x, AXES, flat)  42.9 us
    pallas_call x1, Pallas kernels, local(): pl.pallas_call(functools.partial(pick_kernel, len(direct)), out_shape=blo...  17 us
    pallas_call x9, Pallas kernels, local(): pl.pallas_call(unit_kernel, out_shape=block_shape, in_specs=[SMEM, SMEM,...  16 us
    pallas_call x8, Pallas kernels, local(): pl.pallas_call(pair_kernel, out_shape=block_shape, in_specs=[SMEM, VMEM,...  15.4 us
    pallas_call x7, Pallas kernels, local(): pl.pallas_call(lead_kernel, out_shape=(block_shape, block_shape), in_spec...  14.1 us
  transfers between devices with their start and end apart: 40, of which 1 were waited for; matrix products, arithmetic and copies ran while one was open for 0% of the time, Pallas kernels for 27%

commit v1 on v0

v1 whole, which is shorter than its diff:
```python
import functools

import jax
import jax.numpy as jnp
from jax import lax
from jax.experimental import pallas as pl
from jax.experimental.pallas import tpu as pltpu
from jax.sharding import PartitionSpec as P

AXES = ("site", "sector")
RING = 8
ROUND = (8, 7)


def moved(x, pairs, sectors):
    flat = [(a * sectors + b, c * sectors + d) for (a, b), (c, d) in pairs]
    return lax.ppermute(x, AXES, flat)


def mix_and_multiply(env_ref, a_ref, w_ref, p, mixed_ref, half_ref):
    size = env_ref.shape[-1]
    step = 32
    for i in range(0, size, step):
        rows = [env_ref[w, i : i + step, :].astype(jnp.float32) for w in range(4)]
        for v in range(4):
            total = rows[0] * w_ref[p * 16 + v * 4]
            for w in range(1, 4):
                total = total + rows[w] * w_ref[p * 16 + v * 4 + w]
            mixed_ref[v * size + i : v * size + i + step, :] = total.astype(jnp.bfloat16)
    block = a_ref[pl.ds(pl.multiple_of(p * size, size), size), :]
    half_ref[...] = jnp.dot(
        mixed_ref[...], block, preferred_element_type=jnp.float32
    ).astype(jnp.bfloat16)
    return block


def close(block, half):
    return lax.dot_general(
        block, half, (((0,), (0,)), ((), ())), preferred_element_type=jnp.float32
    )


def one_unit(env_ref, a_ref, w_ref, p, mixed_ref, half_ref, out_ref):
    size = env_ref.shape[-1]
    block = mix_and_multiply(env_ref, a_ref, w_ref, p, mixed_ref, half_ref)
    for v in range(4):
        half = half_ref[v * size : (v + 1) * size, :]
        out_ref[v] = close(block, half).astype(jnp.bfloat16)


def stay_part(env_ref, a_ref, w_ref, mixed_ref, half_ref, mixed2_ref, half2_ref, out_ref):
    size = env_ref.shape[-1]
    first = mix_and_multiply(env_ref, a_ref, w_ref, 1, mixed_ref, half_ref)
    second = mix_and_multiply(env_ref, a_ref, w_ref, 2, mixed2_ref, half2_ref)
    for v in range(4):
        at = slice(v * size, (v + 1) * size)
        total = close(first, half_ref[at, :]) + close(second, half2_ref[at, :])
        out_ref[v] = total.astype(jnp.bfloat16)


def stay_kernel(w_ref, env_ref, a_ref, out_ref, *work):
    stay_part(env_ref, a_ref, w_ref, *work, out_ref)


def moving_parts(p_ref, w_ref, env_ref, a_ref, edge_ref, inner_ref, over_ref, *work):
    edge = p_ref[0]
    one_unit(env_ref, a_ref, w_ref, edge, *work[:2], edge_ref)
    one_unit(env_ref, a_ref, w_ref, 3 - edge, *work[2:], inner_ref)

    @pl.when(p_ref[1] == 1)
    def _():
        stay_part(env_ref, a_ref, w_ref, *work, over_ref)


def first_kernel(p_ref, w_ref, env_ref, a_ref, edge_ref, inner_ref, over_ref, *work):
    moving_parts(p_ref, w_ref, env_ref, a_ref, edge_ref, inner_ref, over_ref, *work)


def summed(turn, cross_ref, swap_ref, came_ref, stay_ref, env_ref):
    size = env_ref.shape[-1]
    step = 32

    def add(one_ref):
        for v in range(4):
            for i in range(0, size, step):
                at = (v, slice(i, i + step))
                total = (
                    swap_ref[at].astype(jnp.float32)
                    + one_ref[at].astype(jnp.float32)
                    + cross_ref[at].astype(jnp.float32)
                )
                env_ref[at] = total.astype(jnp.bfloat16)

    @pl.when(turn == 1)
    def _():
        add(came_ref)

    @pl.when(turn == 0)
    def _():
        add(stay_ref)


def lead_kernel(
    p_ref, w_ref, cross_ref, swap_ref, came_ref, stay_ref, a_ref, env_ref, edge_ref, inner_ref, over_ref, *work
):
    summed(p_ref[2], cross_ref, swap_ref, came_ref, stay_ref, env_ref)
    moving_parts(p_ref, w_ref, env_ref, a_ref, edge_ref, inner_ref, over_ref, *work)


def last_kernel(count, p_ref, cross_ref, swap_ref, came_ref, stay_ref, *refs):
    out_ref, sem = refs[count], refs[count + 1]

    @pl.when(p_ref[0] == 0)
    def _():
        summed(p_ref[1], cross_ref, swap_ref, came_ref, stay_ref, out_ref)

    for i in range(count):

        @pl.when(p_ref[0] == i + 1)
        def _():
            copy = pltpu.make_async_copy(refs[i], out_ref, sem)
            copy.start()
            copy.wait()


def pick_kernel(count, p_ref, *refs):
    out_ref, sem = refs[count], refs[count + 1]
    for i in range(count):

        @pl.when(p_ref[0] == i)
        def _():
            copy = pltpu.make_async_copy(refs[i], out_ref, sem)
            copy.start()
            copy.wait()


VMEM = pl.BlockSpec(memory_space=pltpu.VMEM)
SMEM = pl.BlockSpec(memory_space=pltpu.SMEM)
ANY = pl.BlockSpec(memory_space=pl.ANY)
PARAMS = pltpu.CompilerParams(vmem_limit_bytes=24 * 1024 * 1024)


def scratch(count, channels, size):
    return [pltpu.VMEM((channels * size, size), jnp.bfloat16)] * count


def cost(units, arrays):
    return pl.CostEstimate(
        flops=units * 8 * 2 * 256**3, bytes_accessed=arrays * 2**19, transcendentals=0
    )


def local(site_blocks, operators, op_mask, coupling, start_env):
    sites = lax.axis_size("site")
    sectors = lax.axis_size("sector")
    lines = sectors // RING
    row = lax.axis_index("site")
    place = lax.axis_index("sector")
    slot = lax.rem(place, RING)
    odd = lax.rem(place, 2)
    states, size = site_blocks.shape[2], site_blocks.shape[3]
    block_shape = jax.ShapeDtypeStruct(start_env.shape[1:], jnp.bfloat16)
    channels = start_env.shape[1]

    def at(line, slot_at):
        return line * RING + slot_at % RING

    lane = [(line, u) for line in range(lines) for u in range(RING)]
    coupled = coupling[0, 0].astype(jnp.float32)
    weights = operators[0] * op_mask[0].astype(jnp.float32) * coupled[None, None, :]
    weights = weights.transpose(2, 1, 0).reshape(-1)
    blocks = site_blocks[0, 0].reshape(states * size, size)

    def turn_of(s):
        return (lax.rem(slot + s, RING) == RING - 1).astype(jnp.int32)

    def straight_pairs(s):
        return [((s, at(z, u)), (0, at(z, u - s))) for z, u in lane]

    early = min(3, sites)
    parcels = {s: moved(blocks, straight_pairs(s), sectors) for s in range(1, early)}
    scales = {s: moved(weights, straight_pairs(s), sectors) for s in range(1, early)}
    parcels[0], scales[0] = blocks, weights

    def pack(after):
        held, lying, after = lax.optimization_barrier((weights, blocks, after))
        high = lax.reduce_precision(held, *ROUND)
        middle = lax.reduce_precision(held - high, *ROUND)
        low = lax.reduce_precision(held - high - middle, *ROUND)
        pieces = jnp.stack([high, middle, low]).astype(jnp.bfloat16)
        pieces = jnp.pad(pieces, ((0, 13), (0, size - pieces.shape[1])))
        packed = jnp.concatenate([lying, pieces], axis=0)
        pairs = [((s, at(z, u)), (s, at(z, u - s))) for s in range(early, sites) for z, u in lane]
        return moved(packed, pairs, sectors), after

    def weights_of(parcel):
        parts = parcel[states * size : states * size + 3, : weights.shape[0]].astype(jnp.float32)
        return parts[0] + parts[1] + parts[2]

    def fetch(s, after):
        held, after = lax.optimization_barrier((turned, after))
        pairs = [((s, q), (0, q)) for q in range(sectors)]
        return moved(held, pairs, sectors), after

    def part_pairs(s, crossing):
        pairs = []
        for z, v in lane:
            u = (v + s) % RING
            if (v % 2 == 0) == crossing:
                pairs.append(((0, at(z, v)), (0, at(z, v - 1))))
            elif z + (u >= RING - 2) < lines:
                pairs.append(((0, at(z, v)), (0, at(z + (u >= RING - 2), v + 1))))
        return pairs

    def over_pairs(s):
        v = (RING - 1 - s) % RING
        return [((0, at(z, v)), (0, at(z + 1, v))) for z in range(lines - 1)]

    current = start_env[0]
    kept, raised = {}, {}
    near = min(6, sites)
    work = scratch(4, channels, size)
    for s in range(sites):
        control = jnp.stack([3 * odd, turn_of(s), turn_of(s - 1 + RING)])
        if s == 0:
            edge, inner, over = pl.pallas_call(
                first_kernel,
                out_shape=(block_shape,) * 3,
                in_specs=[SMEM, SMEM, VMEM, VMEM],
                out_specs=(VMEM,) * 3,
                scratch_shapes=work,
                compiler_params=PARAMS,
                cost_estimate=cost(2, 4),
                name="first",
            )(control, scales[0], current, blocks)
        else:
            if s not in scales:
                scales[s] = weights_of(parcels[s])
            current, edge, inner, over = pl.pallas_call(
                lead_kernel,
                out_shape=(block_shape,) * 4,
                in_specs=[SMEM, SMEM] + [VMEM] * 5,
                out_specs=(VMEM,) * 4,
                scratch_shapes=work,
                compiler_params=PARAMS,
                cost_estimate=cost(2, 6),
                name="lead",
            )(control, scales[s], cross, swap, came, stay, parcels[s])
            kept[s] = current
        cross = moved(edge, part_pairs(s, True), sectors)
        swap = moved(inner, part_pairs(s, False), sectors)
        if s == 0:
            turned, swap = pack(swap)
        came = moved(over, over_pairs(s), sectors)
        stay = pl.pallas_call(
            stay_kernel,
            out_shape=block_shape,
            in_specs=[SMEM, VMEM, VMEM],
            out_specs=VMEM,
            scratch_shapes=work,
            compiler_params=PARAMS,
            cost_estimate=cost(40, 4),
            name="stay",
        )(scales[s], current, parcels[s])
        if s >= 1:
            if s < near:
                raised[s] = moved(kept[s], [((0, q), (s, q)) for q in range(sectors)], sectors)
            else:
                raised[s] = moved(
                    kept[s], [((0, at(z, u - s)), (s, at(z, u))) for z, u in lane], sectors
                )
        if s >= 2 and s + 1 < sites:
            stay, raised[s - 1] = lax.optimization_barrier((stay, raised[s - 1]))
        ahead = s + 2
        if early <= ahead < sites:
            parcels[ahead], stay = fetch(ahead, stay)

    picked = pl.pallas_call(
        functools.partial(pick_kernel, near - 1),
        out_shape=block_shape,
        in_specs=[SMEM] + [ANY] * (near - 1),
        out_specs=ANY,
        scratch_shapes=[pltpu.SemaphoreType.DMA],
        name="pick",
    )(jnp.stack([row - 1]), *[raised[r] for r in range(1, near)])
    homeward = moved(
        picked,
        [((r, at(z, u - r)), (r, at(z, u))) for r in range(1, near) for z, u in lane],
        sectors,
    )
    kind = jnp.where(row == 0, 0, jnp.where(row < near, 1, row - near + 2))
    straight = [raised[r] for r in range(near, sites)]
    out = pl.pallas_call(
        functools.partial(last_kernel, 1 + len(straight)),
        out_shape=block_shape,
        in_specs=[SMEM] + [VMEM] * 4 + [ANY] * (1 + len(straight)),
        out_specs=VMEM,
        scratch_shapes=[pltpu.SemaphoreType.DMA],
        compiler_params=PARAMS,
        name="last",
    )(jnp.stack([kind, turn_of(sites - 1)]), cross, swap, came, stay, homeward, *straight)
    return out[None, None]


def solution(mesh):
    return jax.shard_map(
        local,
        mesh=mesh,
        in_specs=(
            P("site", "sector", None, None, None),
            P("site", None, None, None),
            P("site", None, None, None),
            P("site", "sector", None),
            P("sector", None, None, None),
        ),
        out_specs=P("site", "sector", None, None, None),
        check_vma=False,
    )
```

time: 236 us -> 198 us (0.84)
  the two profiles are of different devices: /device:TPU:121 before, /device:TPU:7 now
where the time goes in v1:
time: 198 us; the launch traced here: 194 us
  starting transfers between devices  121 us (61%)
  waiting for transfers between devices  34.7 us (18%)
  Pallas kernels  31.2 us (16%)
  local copies, waits for them, and re-layouts  3.22 us (2%)
  other arithmetic  2.97 us (2%)
    ppermute x42, starting transfers between devices, moved(): return lax.ppermute(x, AXES, flat)  121 us
    ppermute x42, waiting for transfers between devices, moved(): return lax.ppermute(x, AXES, flat)  34.7 us
    pallas_call x7, Pallas kernels, local(): pl.pallas_call(lead_kernel, out_shape=(block_shape,) * 4, in_specs=[SMEM,...  13.5 us
    pallas_call x8, Pallas kernels, local(): pl.pallas_call(stay_kernel, out_shape=block_shape, in_specs=[SMEM, VMEM,...  12.3 us
  transfers between devices with their start and end apart: 42, of which 9 were waited for; matrix products, arithmetic and copies ran while one was open for 1% of the time, Pallas kernels for 15%

profile of v1, /device:TPU:7, one launch (start us, length us, event | category | flops | bytes accessed | tf_op | source)
XLA Modules:
  0.0 194.1 jit_solution(8814921252552522109)
XLA Ops:
  6.4 3.7 %first.1 = (bf16[4,256,256]{2,1,0:T(8,128)(2,1)}, bf16[4,256,256]{2,1,0:T(8,128)(2,1)}, bf16[4,256,256]{2,1,0:T(8,128)(2,1)}) custom-call(s32[3]{0:T(128)S(1)} %pad_add_fusion.2.p_ref, f32[64]{0:T(128)S(1)} %reshape.15.w_ref, bf16[4,256,256]{2,1,0:T(8,128)(2,1)S(1)} %bitcast.50, bf16[1024,256]{1,0:T(8,128)(2,1)S(1)} %bitcast.46), custom_call_target="tpu_custom_call" | custom-call | flops 536870912 | bytes 2097152 | tf_op jit(solution)/shard_map/first/pallas_call | solution.py:226
  11.7 3.8 %collective-permute-start.3 = (bf16[4,256,256]{2,1,0:T(8,128)(2,1)}, bf16[4,256,256]{2,1,0:T(8,128)(2,1)S(1)}, u32[]{:S(2)}, u32[]{:S(2)}) collective-permute-start(bf16[4,256,256]{2,1,0:T(8,128)(2,1)} %get-tuple-element.62), channel_id=1, source_target_pairs={{0,7},{1,2},{2,1},{3,4},{4,3},{5,6},{6,5},{7,8},{8,15},{9,10},{10,... | collective-permute-start | bytes 1572872 | tf_op jit(solution)/shard_map/ppermute | solution.py:17
  15.5 4.2 %collective-permute-start.4 = (bf16[4,256,256]{2,1,0:T(8,128)(2,1)}, bf16[4,256,256]{2,1,0:T(8,128)(2,1)S(1)}, u32[]{:S(2)}, u32[]{:S(2)}) collective-permute-start(bf16[4,256,256]{2,1,0:T(8,128)(2,1)} %get-tuple-element.64), channel_id=1, source_target_pairs={{7,15},{15,23},{23,31},{31,39},{39,47},{47,55},{55,63}} | collective-permute-start | bytes 1572872 | tf_op jit(solution)/shard_map/ppermute | solution.py:17
  28.0 4.3 %collective-permute-done.4.came_ref = bf16[4,256,256]{2,1,0:T(8,128)(2,1)S(1)} collective-permute-done((bf16[4,256,256]{2,1,0:T(8,128)(2,1)}, bf16[4,256,256]{2,1,0:T(8,128)(2,1)S(1)}, u32[]{:S(2)}, u32[]{:S(2)}) %collective-permute-start.4) | collective-permute-done | bytes 524320 | tf_op jit(solution)/shard_map/ppermute | solution.py:17
  34.1 1.9 collective-permute-start.8
  42.7 8.2 %collective-permute-done.8.cross_ref = bf16[4,256,256]{2,1,0:T(8,128)(2,1)S(1)} collective-permute-done((bf16[4,256,256]{2,1,0:T(8,128)(2,1)S(1)}, bf16[4,256,256]{2,1,0:T(8,128)(2,1)S(1)}, u32[]{:S(2)}, u32[]{:S(2)}) %collective-permute-start.8) | collective-permute-done | bytes 524320 | tf_op jit(solution)/shard_map/ppermute | solution.py:17
  50.9 1.8 lead.8
  52.7 1.9 collective-permute-start.12
  54.6 3.2 %collective-permute-start.13 = (bf16[4,256,256]{2,1,0:T(8,128)(2,1)S(1)}, bf16[4,256,256]{2,1,0:T(8,128)(2,1)S(1)}, u32[]{:S(2)}, u32[]{:S(2)}) collective-permute-start(bf16[4,256,256]{2,1,0:T(8,128)(2,1)S(1)} %get-tuple-element.72), channel_id=1, source_target_pairs={{0,1},{1,0},{2,3},{3,2},{4,13},{5,4},{6,7},{7,6},{8,9},{9,8},{10,1... | collective-permute-start | bytes 1572872 | tf_op jit(solution)/shard_map/ppermute | solution.py:17
  66.2 2.1 %collective-permute-start.19 = (bf16[4,256,256]{2,1,0:T(8,128)(2,1)S(1)}, bf16[4,256,256]{2,1,0:T(8,128)(2,1)S(1)}, u32[]{:S(2)}, u32[]{:S(2)}) collective-permute-start(bf16[4,256,256]{2,1,0:T(8,128)(2,1)S(1)} %get-tuple-element.81), channel_id=1, source_target_pairs={{0,7},{1,2},{2,1},{3,12},{4,3},{5,6},{6,5},{7,0},{8,15},{9,10},{10... | collective-permute-start | bytes 1572872 | tf_op jit(solution)/shard_map/ppermute | solution.py:17
  68.3 14.8 %collective-permute-start.20 = (bf16[4,256,256]{2,1,0:T(8,128)(2,1)S(1)}, bf16[4,256,256]{2,1,0:T(8,128)(2,1)S(1)}, u32[]{:S(2)}, u32[]{:S(2)}) collective-permute-start(bf16[4,256,256]{2,1,0:T(8,128)(2,1)S(1)} %get-tuple-element.82), channel_id=1, source_target_pairs={{0,1},{1,0},{2,3},{3,2},{4,13},{5,4},{6,7},{7,6},{8,9},{9,8},{10,1... | collective-permute-start | bytes 1572872 | tf_op jit(solution)/shard_map/ppermute | solution.py:17
  89.9 1.9 collective-permute-start.22
  91.8 4.8 %collective-permute-start.23 = (bf16[4,256,256]{2,1,0:T(8,128)(2,1)S(1)}, bf16[4,256,256]{2,1,0:T(8,128)(2,1)S(1)}, u32[]{:S(2)}, u32[]{:S(2)}) collective-permute-start(bf16[4,256,256]{2,1,0:T(8,128)(2,1)S(1)} %get-tuple-element.86), channel_id=1, source_target_pairs={{0,1},{1,0},{2,11},{3,2},{4,5},{5,4},{6,7},{7,6},{8,9},{9,8},{10,1... | collective-permute-start | bytes 1572872 | tf_op jit(solution)/shard_map/ppermute | solution.py:17
  100.2 5.3 %collective-permute-done.17.a_ref = bf16[1040,256]{1,0:T(8,128)(2,1)S(1)} collective-permute-done((bf16[1040,256]{1,0:T(8,128)(2,1)}, bf16[1040,256]{1,0:T(8,128)(2,1)S(1)}, u32[]{:S(2)}, u32[]{:S(2)}) %collective-permute-start.17) | collective-permute-done | bytes 532512 | tf_op jit(solution)/shard_map/ppermute | solution.py:17
  108.7 1.9 collective-permute-start.29
  110.6 3.9 %collective-permute-start.30 = (bf16[4,256,256]{2,1,0:T(8,128)(2,1)S(1)}, bf16[4,256,256]{2,1,0:T(8,128)(2,1)S(1)}, u32[]{:S(2)}, u32[]{:S(2)}) collective-permute-start(bf16[4,256,256]{2,1,0:T(8,128)(2,1)S(1)} %get-tuple-element.96), channel_id=1, source_target_pairs={{0,1},{1,0},{2,11},{3,2},{4,5},{5,4},{6,7},{7,6},{8,9},{9,8},{10,1... | collective-permute-start | bytes 1572872 | tf_op jit(solution)/shard_map/ppermute | solution.py:17
  118.1 4.4 %collective-permute-done.28.a_ref = bf16[1040,256]{1,0:T(8,128)(2,1)S(1)} collective-permute-done((bf16[1040,256]{1,0:T(8,128)(2,1)}, bf16[1040,256]{1,0:T(8,128)(2,1)S(1)}, u32[]{:S(2)}, u32[]{:S(2)}) %collective-permute-start.28) | collective-permute-done | bytes 532512 | tf_op jit(solution)/shard_map/ppermute | solution.py:17
  123.9 2.9 %lead.12 = (bf16[4,256,256]{2,1,0:T(8,128)(2,1)S(1)}, bf16[4,256,256]{2,1,0:T(8,128)(2,1)}, bf16[4,256,256]{2,1,0:T(8,128)(2,1)}, bf16[4,256,256]{2,1,0:T(8,128)(2,1)}) custom-call(s32[3]{0:T(128)S(1)} %pad_add_fusion.8.p_ref, f32[64]{0:T(128)S(1)} %add_bitcast_fusion.w_ref, bf16[4,256,256]{2,1,0:T(8,128)(2,1)S(1)} %collective-permute-done.29.cross_ref, ...), custom_call_target="tpu_custom_call" | custom-call | flops 536870912 | bytes 3145728 | tf_op jit(solution)/shard_map/lead/pallas_call | solution.py:239
  126.9 16.7 %collective-permute-start.32 = (bf16[4,256,256]{2,1,0:T(8,128)(2,1)}, bf16[4,256,256]{2,1,0:T(8,128)(2,1)S(1)}, u32[]{:S(2)}, u32[]{:S(2)}) collective-permute-start(bf16[4,256,256]{2,1,0:T(8,128)(2,1)} %get-tuple-element.99), channel_id=1, source_target_pairs={{0,7},{1,10},{2,1},{3,4},{4,3},{5,6},{6,5},{7,0},{8,15},{9,18},{10... | collective-permute-start | bytes 1572872 | tf_op jit(solution)/shard_map/ppermute | solution.py:17
  143.6 1.9 collective-permute-start.33
  151.0 1.8 lead.13
  152.8 24.5 %collective-permute-start.36 = (bf16[4,256,256]{2,1,0:T(8,128)(2,1)S(1)}, bf16[4,256,256]{2,1,0:T(8,128)(2,1)S(1)}, u32[]{:S(2)}, u32[]{:S(2)}) collective-permute-start(bf16[4,256,256]{2,1,0:T(8,128)(2,1)S(1)} %get-tuple-element.104), channel_id=1, source_target_pairs={{0,7},{1,2},{2,1},{3,4},{4,3},{5,6},{6,5},{7,8},{8,15},{9,10},{10,... | collective-permute-start | bytes 1572872 | tf_op jit(solution)/shard_map/ppermute | solution.py:17
  177.3 1.9 collective-permute-start.37
  183.4 8.9 %collective-permute-done.41.refs_2_ = bf16[4,256,256]{2,1,0:T(8,128)(2,1)S(1)} collective-permute-done((bf16[4,256,256]{2,1,0:T(8,128)(2,1)S(1)}, bf16[4,256,256]{2,1,0:T(8,128)(2,1)S(1)}, u32[]{:S(2)}, u32[]{:S(2)}) %collective-permute-start.41) | collective-permute-done | bytes 524320 | tf_op jit(solution)/shard_map/ppermute | solution.py:17
  (124 shorter events, 62.1 us)
Async XLA Ops:
  1.6 22.6 %collective-permute-start.2 = (f32[64]{0:T(128)S(1)}, f32[64]{0:T(128)S(1)}, u32[]{:S(2)}, u32[]{:S(2)}) collective-permute-start(f32[64]{0:T(128)S(1)} %reshape.15.w_ref), channel_id=1, source_target_pairs={{64,7},{65,0},{66,1},{67,2},{68,3},{69,4},{70,5},{71,6},{72,15},{7... | collective-permute-start | bytes 776 | tf_op jit(solution)/shard_map/ppermute | solution.py:17
  2.9 29.4 %collective-permute-start.5 = (bf16[1024,256]{1,0:T(8,128)(2,1)}, bf16[1024,256]{1,0:T(8,128)(2,1)S(1)}, u32[]{:S(2)}, u32[]{:S(2)}) collective-permute-start(bf16[1024,256]{1,0:T(8,128)(2,1)} %bitcast.45), channel_id=1, source_target_pairs={{64,7},{65,0},{66,1},{67,2},{68,3},{69,4},{70,5},{71,6},{72,15},{7... | collective-permute-start | bytes 1572872 | tf_op jit(solution)/shard_map/ppermute | solution.py:17
  15.5 16.8 %collective-permute-start.4 = (bf16[4,256,256]{2,1,0:T(8,128)(2,1)}, bf16[4,256,256]{2,1,0:T(8,128)(2,1)S(1)}, u32[]{:S(2)}, u32[]{:S(2)}) collective-permute-start(bf16[4,256,256]{2,1,0:T(8,128)(2,1)} %get-tuple-element.64), channel_id=1, source_target_pairs={{7,15},{15,23},{23,31},{31,39},{39,47},{47,55},{55,63}} | collective-permute-start | bytes 1572872 | tf_op jit(solution)/shard_map/ppermute | solution.py:17
  22.3 15.4 %collective-permute-start.1 = (bf16[1040,256]{1,0:T(8,128)(2,1)}, bf16[1040,256]{1,0:T(8,128)(2,1)}, u32[]{:S(2)}, u32[]{:S(2)}) collective-permute-start(bf16[1040,256]{1,0:T(8,128)(2,1)} %pad_maximum_fusion), channel_id=1, source_target_pairs={{192,197},{193,198},{194,199},{195,192},{196,193},{197,194},{198,1... | collective-permute-start | bytes 1597448 | tf_op jit(solution)/shard_map/ppermute | solution.py:17
  24.1 15.8 %collective-permute-start.7 = (f32[64]{0:T(128)S(1)}, f32[64]{0:T(128)S(1)}, u32[]{:S(2)}, u32[]{:S(2)}) collective-permute-start(f32[64]{0:T(128)S(1)} %reshape.15.w_ref), channel_id=1, source_target_pairs={{128,6},{129,7},{130,0},{131,1},{132,2},{133,3},{134,4},{135,5},{1... | collective-permute-start | bytes 776 | tf_op jit(solution)/shard_map/ppermute | solution.py:17
  34.1 16.8 %collective-permute-start.8 = (bf16[4,256,256]{2,1,0:T(8,128)(2,1)S(1)}, bf16[4,256,256]{2,1,0:T(8,128)(2,1)S(1)}, u32[]{:S(2)}, u32[]{:S(2)}) collective-permute-start(bf16[4,256,256]{2,1,0:T(8,128)(2,1)S(1)} %get-tuple-element.67), channel_id=1, source_target_pairs={{0,7},{1,2},{2,1},{3,4},{4,3},{5,14},{6,5},{7,0},{8,15},{9,10},{10... | collective-permute-start | bytes 1572872 | tf_op jit(solution)/shard_map/ppermute | solution.py:17
  40.0 20.0 %collective-permute-start.15 = (bf16[4,256,256]{2,1,0:T(8,128)(2,1)S(1)}, bf16[4,256,256]{2,1,0:T(8,128)(2,1)S(1)}, u32[]{:S(2)}, u32[]{:S(2)}) collective-permute-start(bf16[4,256,256]{2,1,0:T(8,128)(2,1)S(1)} %get-tuple-element.65.env_ref), channel_id=1, source_target_pairs={{0,64},{1,65},{2,66},{3,67},{4,68},{5,69},{6,70},{7,71},{8,72},{9,... | collective-permute-start | bytes 1572872 | tf_op jit(solution)/shard_map/ppermute | solution.py:17
  41.4 20.2 %collective-permute-start.6 = (bf16[1040,256]{1,0:T(8,128)(2,1)}, bf16[1040,256]{1,0:T(8,128)(2,1)S(1)}, u32[]{:S(2)}, u32[]{:S(2)}) collective-permute-start(bf16[1040,256]{1,0:T(8,128)(2,1)} %collective-permute-done.1), channel_id=1, source_target_pairs={{192,0},{193,1},{194,2},{195,3},{196,4},{197,5},{198,6},{199,7},{2... | collective-permute-start | bytes 1597448 | tf_op jit(solution)/shard_map/ppermute | solution.py:17
  60.0 25.3 %collective-permute-start.16 = (bf16[4,256,256]{2,1,0:T(8,128)(2,1)S(1)}, bf16[4,256,256]{2,1,0:T(8,128)(2,1)S(1)}, u32[]{:S(2)}, u32[]{:S(2)}) collective-permute-start(bf16[4,256,256]{2,1,0:T(8,128)(2,1)S(1)} %get-tuple-element.74.env_ref), channel_id=1, source_target_pairs={{0,128},{1,129},{2,130},{3,131},{4,132},{5,133},{6,134},{7,135},{8... | collective-permute-start | bytes 1572872 | tf_op jit(solution)/shard_map/ppermute | solution.py:17
  61.5 25.2 %collective-permute-start.18 = (bf16[1040,256]{1,0:T(8,128)(2,1)}, bf16[1040,256]{1,0:T(8,128)(2,1)S(1)}, u32[]{:S(2)}, u32[]{:S(2)}) collective-permute-start(bf16[1040,256]{1,0:T(8,128)(2,1)} %collective-permute-done.1), channel_id=1, source_target_pairs={{256,0},{257,1},{258,2},{259,3},{260,4},{261,5},{262,6},{263,7},{2... | collective-permute-start | bytes 1597448 | tf_op jit(solution)/shard_map/ppermute | solution.py:17
  66.2 21.9 %collective-permute-start.19 = (bf16[4,256,256]{2,1,0:T(8,128)(2,1)S(1)}, bf16[4,256,256]{2,1,0:T(8,128)(2,1)S(1)}, u32[]{:S(2)}, u32[]{:S(2)}) collective-permute-start(bf16[4,256,256]{2,1,0:T(8,128)(2,1)S(1)} %get-tuple-element.81), channel_id=1, source_target_pairs={{0,7},{1,2},{2,1},{3,12},{4,3},{5,6},{6,5},{7,0},{8,15},{9,10},{10... | collective-permute-start | bytes 1572872 | tf_op jit(solution)/shard_map/ppermute | solution.py:17
  68.3 19.7 %collective-permute-start.20 = (bf16[4,256,256]{2,1,0:T(8,128)(2,1)S(1)}, bf16[4,256,256]{2,1,0:T(8,128)(2,1)S(1)}, u32[]{:S(2)}, u32[]{:S(2)}) collective-permute-start(bf16[4,256,256]{2,1,0:T(8,128)(2,1)S(1)} %get-tuple-element.82), channel_id=1, source_target_pairs={{0,1},{1,0},{2,3},{3,2},{4,13},{5,4},{6,7},{7,6},{8,9},{9,8},{10,1... | collective-permute-start | bytes 1572872 | tf_op jit(solution)/shard_map/ppermute | solution.py:17
  86.7 18.8 %collective-permute-start.17 = (bf16[1040,256]{1,0:T(8,128)(2,1)}, bf16[1040,256]{1,0:T(8,128)(2,1)S(1)}, u32[]{:S(2)}, u32[]{:S(2)}) collective-permute-start(bf16[1040,256]{1,0:T(8,128)(2,1)} %collective-permute-done.1), channel_id=1, source_target_pairs={{320,0},{321,1},{322,2},{323,3},{324,4},{325,5},{326,6},{327,7},{3... | collective-permute-start | bytes 1597448 | tf_op jit(solution)/shard_map/ppermute | solution.py:17
  89.9 17.0 %collective-permute-start.22 = (bf16[4,256,256]{2,1,0:T(8,128)(2,1)S(1)}, bf16[4,256,256]{2,1,0:T(8,128)(2,1)S(1)}, u32[]{:S(2)}, u32[]{:S(2)}) collective-permute-start(bf16[4,256,256]{2,1,0:T(8,128)(2,1)S(1)} %get-tuple-element.85), channel_id=1, source_target_pairs={{0,7},{1,2},{2,1},{3,12},{4,3},{5,6},{6,5},{7,0},{8,15},{9,10},{10... | collective-permute-start | bytes 1572872 | tf_op jit(solution)/shard_map/ppermute | solution.py:17
  91.8 15.1 %collective-permute-start.23 = (bf16[4,256,256]{2,1,0:T(8,128)(2,1)S(1)}, bf16[4,256,256]{2,1,0:T(8,128)(2,1)S(1)}, u32[]{:S(2)}, u32[]{:S(2)}) collective-permute-start(bf16[4,256,256]{2,1,0:T(8,128)(2,1)S(1)} %get-tuple-element.86), channel_id=1, source_target_pairs={{0,1},{1,0},{2,11},{3,2},{4,5},{5,4},{6,7},{7,6},{8,9},{9,8},{10,1... | collective-permute-start | bytes 1572872 | tf_op jit(solution)/shard_map/ppermute | solution.py:17
  98.9 17.9 %collective-permute-start.26 = (bf16[4,256,256]{2,1,0:T(8,128)(2,1)S(1)}, bf16[4,256,256]{2,1,0:T(8,128)(2,1)S(1)}, u32[]{:S(2)}, u32[]{:S(2)}) collective-permute-start(bf16[4,256,256]{2,1,0:T(8,128)(2,1)S(1)} %get-tuple-element.88.env_ref), channel_id=1, source_target_pairs={{0,256},{1,257},{2,258},{3,259},{4,260},{5,261},{6,262},{7,263},{8... | collective-permute-start | bytes 1572872 | tf_op jit(solution)/shard_map/ppermute | solution.py:17
  105.6 17.0 %collective-permute-start.28 = (bf16[1040,256]{1,0:T(8,128)(2,1)}, bf16[1040,256]{1,0:T(8,128)(2,1)S(1)}, u32[]{:S(2)}, u32[]{:S(2)}) collective-permute-start(bf16[1040,256]{1,0:T(8,128)(2,1)} %collective-permute-done.1), channel_id=1, source_target_pairs={{384,0},{385,1},{386,2},{387,3},{388,4},{389,5},{390,6},{391,7},{3... | collective-permute-start | bytes 1597448 | tf_op jit(solution)/shard_map/ppermute | solution.py:17
  108.7 15.2 %collective-permute-start.29 = (bf16[4,256,256]{2,1,0:T(8,128)(2,1)S(1)}, bf16[4,256,256]{2,1,0:T(8,128)(2,1)S(1)}, u32[]{:S(2)}, u32[]{:S(2)}) collective-permute-start(bf16[4,256,256]{2,1,0:T(8,128)(2,1)S(1)} %get-tuple-element.95), channel_id=1, source_target_pairs={{0,7},{1,10},{2,1},{3,4},{4,3},{5,6},{6,5},{7,0},{8,15},{9,18},{10... | collective-permute-start | bytes 1572872 | tf_op jit(solution)/shard_map/ppermute | solution.py:17
  116.8 31.0 %collective-permute-start.35 = (bf16[4,256,256]{2,1,0:T(8,128)(2,1)S(1)}, bf16[4,256,256]{2,1,0:T(8,128)(2,1)S(1)}, u32[]{:S(2)}, u32[]{:S(2)}) collective-permute-start(bf16[4,256,256]{2,1,0:T(8,128)(2,1)S(1)} %get-tuple-element.91.env_ref), channel_id=1, source_target_pairs={{0,320},{1,321},{2,322},{3,323},{4,324},{5,325},{6,326},{7,327},{8... | collective-permute-start | bytes 1572872 | tf_op jit(solution)/shard_map/ppermute | solution.py:17
  122.6 26.9 %collective-permute-start.27 = (bf16[1040,256]{1,0:T(8,128)(2,1)}, bf16[1040,256]{1,0:T(8,128)(2,1)S(1)}, u32[]{:S(2)}, u32[]{:S(2)}) collective-permute-start(bf16[1040,256]{1,0:T(8,128)(2,1)} %collective-permute-done.1), channel_id=1, source_target_pairs={{448,0},{449,1},{450,2},{451,3},{452,4},{453,5},{454,6},{455,7},{4... | collective-permute-start | bytes 1597448 | tf_op jit(solution)/shard_map/ppermute | solution.py:17
  126.9 24.1 %collective-permute-start.32 = (bf16[4,256,256]{2,1,0:T(8,128)(2,1)}, bf16[4,256,256]{2,1,0:T(8,128)(2,1)S(1)}, u32[]{:S(2)}, u32[]{:S(2)}) collective-permute-start(bf16[4,256,256]{2,1,0:T(8,128)(2,1)} %get-tuple-element.99), channel_id=1, source_target_pairs={{0,7},{1,10},{2,1},{3,4},{4,3},{5,6},{6,5},{7,0},{8,15},{9,18},{10... | collective-permute-start | bytes 1572872 | tf_op jit(solution)/shard_map/ppermute | solution.py:17
  148.6 31.3 %collective-permute-start.39 = (bf16[4,256,256]{2,1,0:T(8,128)(2,1)}, bf16[4,256,256]{2,1,0:T(8,128)(2,1)S(1)}, u32[]{:S(2)}, u32[]{:S(2)}) collective-permute-start(bf16[4,256,256]{2,1,0:T(8,128)(2,1)} %pick.1), channel_id=1, source_target_pairs={{71,64},{64,65},{65,66},{66,67},{67,68},{68,69},{69,70},{70,71},{7... | collective-permute-start | bytes 1572872 | tf_op jit(solution)/shard_map/ppermute | solution.py:17
  149.6 33.2 %collective-permute-start.40 = (bf16[4,256,256]{2,1,0:T(8,128)(2,1)S(1)}, bf16[4,256,256]{2,1,0:T(8,128)(2,1)S(1)}, u32[]{:S(2)}, u32[]{:S(2)}) collective-permute-start(bf16[4,256,256]{2,1,0:T(8,128)(2,1)S(1)} %copy-done.4), channel_id=1, source_target_pairs={{2,384},{3,385},{4,386},{5,387},{6,388},{7,389},{0,390},{1,391},{1... | collective-permute-start | bytes 1572872 | tf_op jit(solution)/shard_map/ppermute | solution.py:17
  152.8 30.6 %collective-permute-start.36 = (bf16[4,256,256]{2,1,0:T(8,128)(2,1)S(1)}, bf16[4,256,256]{2,1,0:T(8,128)(2,1)S(1)}, u32[]{:S(2)}, u32[]{:S(2)}) collective-permute-start(bf16[4,256,256]{2,1,0:T(8,128)(2,1)S(1)} %get-tuple-element.104), channel_id=1, source_target_pairs={{0,7},{1,2},{2,1},{3,4},{4,3},{5,6},{6,5},{7,8},{8,15},{9,10},{10,... | collective-permute-start | bytes 1572872 | tf_op jit(solution)/shard_map/ppermute | solution.py:17
  (28 other events, 240.6 us)

commit v2 on v1

v2 whole, which is shorter than its diff:
```python
import functools

import jax
import jax.numpy as jnp
from jax import lax
from jax.experimental import pallas as pl
from jax.experimental.pallas import tpu as pltpu
from jax.sharding import PartitionSpec as P

AXES = ("site", "sector")
RING = 8
ROUND = (8, 7)


def moved(x, pairs, sectors):
    flat = [(a * sectors + b, c * sectors + d) for (a, b), (c, d) in pairs]
    return lax.ppermute(x, AXES, flat)


def mix_and_multiply(env_ref, a_ref, w_ref, p, mixed_ref, half_ref):
    size = env_ref.shape[-1]
    step = 32
    for i in range(0, size, step):
        rows = [env_ref[w, i : i + step, :].astype(jnp.float32) for w in range(4)]
        for v in range(4):
            total = rows[0] * w_ref[p * 16 + v * 4]
            for w in range(1, 4):
                total = total + rows[w] * w_ref[p * 16 + v * 4 + w]
            mixed_ref[v * size + i : v * size + i + step, :] = total.astype(jnp.bfloat16)
    block = a_ref[pl.ds(pl.multiple_of(p * size, size), size), :]
    half_ref[...] = jnp.dot(
        mixed_ref[...], block, preferred_element_type=jnp.float32
    ).astype(jnp.bfloat16)
    return block


def close(block, half):
    return lax.dot_general(
        block, half, (((0,), (0,)), ((), ())), preferred_element_type=jnp.float32
    )


def one_unit(env_ref, a_ref, w_ref, p, mixed_ref, half_ref, out_ref):
    size = env_ref.shape[-1]
    block = mix_and_multiply(env_ref, a_ref, w_ref, p, mixed_ref, half_ref)
    for v in range(4):
        half = half_ref[v * size : (v + 1) * size, :]
        out_ref[v] = close(block, half).astype(jnp.bfloat16)


def stay_part(env_ref, a_ref, w_ref, mixed_ref, half_ref, mixed2_ref, half2_ref, out_ref):
    size = env_ref.shape[-1]
    first = mix_and_multiply(env_ref, a_ref, w_ref, 1, mixed_ref, half_ref)
    second = mix_and_multiply(env_ref, a_ref, w_ref, 2, mixed2_ref, half2_ref)
    for v in range(4):
        at = slice(v * size, (v + 1) * size)
        total = close(first, half_ref[at, :]) + close(second, half2_ref[at, :])
        out_ref[v] = total.astype(jnp.bfloat16)


def stay_kernel(w_ref, env_ref, a_ref, out_ref, *work):
    stay_part(env_ref, a_ref, w_ref, *work, out_ref)


def moving_parts(p_ref, w_ref, env_ref, a_ref, edge_ref, inner_ref, *work):
    edge = p_ref[0]
    one_unit(env_ref, a_ref, w_ref, edge, *work[:2], edge_ref)
    one_unit(env_ref, a_ref, w_ref, 3 - edge, *work[2:], inner_ref)


def summed(fresh, cross_ref, swap_ref, stay_ref, env_ref):
    size = env_ref.shape[-1]
    step = 32

    def add(refs):
        for v in range(4):
            for i in range(0, size, step):
                at = (v, slice(i, i + step))
                total = refs[0][at].astype(jnp.float32)
                for ref in refs[1:]:
                    total = total + ref[at].astype(jnp.float32)
                env_ref[at] = total.astype(jnp.bfloat16)

    @pl.when(fresh == 1)
    def _():
        add((swap_ref, cross_ref))

    @pl.when(fresh == 0)
    def _():
        add((swap_ref, stay_ref, cross_ref))


def lead_kernel(
    p_ref, w_ref, cross_ref, swap_ref, stay_ref, a_ref, env_ref, edge_ref, inner_ref, *work
):
    summed(p_ref[1], cross_ref, swap_ref, stay_ref, env_ref)
    moving_parts(p_ref, w_ref, env_ref, a_ref, edge_ref, inner_ref, *work)


def last_kernel(count, p_ref, cross_ref, swap_ref, stay_ref, *refs):
    out_ref, sem = refs[count], refs[count + 1]

    @pl.when(p_ref[0] == 0)
    def _():
        summed(p_ref[1], cross_ref, swap_ref, stay_ref, out_ref)

    for i in range(count):

        @pl.when(p_ref[0] == i + 1)
        def _():
            copy = pltpu.make_async_copy(refs[i], out_ref, sem)
            copy.start()
            copy.wait()


def pick_kernel(count, p_ref, *refs):
    out_ref, sem = refs[count], refs[count + 1]
    for i in range(count):

        @pl.when(p_ref[0] == i)
        def _():
            copy = pltpu.make_async_copy(refs[i], out_ref, sem)
            copy.start()
            copy.wait()


VMEM = pl.BlockSpec(memory_space=pltpu.VMEM)
SMEM = pl.BlockSpec(memory_space=pltpu.SMEM)
ANY = pl.BlockSpec(memory_space=pl.ANY)
PARAMS = pltpu.CompilerParams(vmem_limit_bytes=24 * 1024 * 1024)


def scratch(count, channels, size):
    return [pltpu.VMEM((channels * size, size), jnp.bfloat16)] * count


def cost(units, arrays):
    return pl.CostEstimate(
        flops=units * 8 * 2 * 256**3, bytes_accessed=arrays * 2**19, transcendentals=0
    )


def local(site_blocks, operators, op_mask, coupling, start_env):
    sites = lax.axis_size("site")
    sectors = lax.axis_size("sector")
    row = lax.axis_index("site")
    place = lax.axis_index("sector")
    odd = lax.rem(place, 2)
    states, size = site_blocks.shape[2], site_blocks.shape[3]
    block_shape = jax.ShapeDtypeStruct(start_env.shape[1:], jnp.bfloat16)
    channels = start_env.shape[1]

    def device(position):
        return (0, position) if position >= 0 else (1, position + sites)

    def fresh_of(s):
        position = jnp.where(row == 1, place - sites, place)
        return (position + s < 0).astype(jnp.int32)

    coupled = coupling[0, 0].astype(jnp.float32)
    weights = operators[0] * op_mask[0].astype(jnp.float32) * coupled[None, None, :]
    weights = weights.transpose(2, 1, 0).reshape(-1)
    blocks = site_blocks[0, 0].reshape(states * size, size)

    def straight_pairs(s):
        return [((s, t), device(t - s)) for t in range(sectors)]

    early = min(3, sites)
    parcels = {s: moved(blocks, straight_pairs(s), sectors) for s in range(1, early)}
    scales = {s: moved(weights, straight_pairs(s), sectors) for s in range(1, early)}
    parcels[0], scales[0] = blocks, weights

    def pack(after):
        held, lying, after = lax.optimization_barrier((weights, blocks, after))
        high = lax.reduce_precision(held, *ROUND)
        middle = lax.reduce_precision(held - high, *ROUND)
        low = lax.reduce_precision(held - high - middle, *ROUND)
        pieces = jnp.stack([high, middle, low]).astype(jnp.bfloat16)
        pieces = jnp.pad(pieces, ((0, 13), (0, size - pieces.shape[1])))
        packed = jnp.concatenate([lying, pieces], axis=0)
        pairs = [
            ((s, t), (s, (t - s) % sectors)) for s in range(early, sites) for t in range(sectors)
        ]
        return moved(packed, pairs, sectors), after

    def weights_of(parcel):
        parts = parcel[states * size : states * size + 3, : weights.shape[0]].astype(jnp.float32)
        return parts[0] + parts[1] + parts[2]

    def fetch(s, after):
        held, after = lax.optimization_barrier((turned, after))
        pairs = [((s, (t - s) % sectors), device(t - s)) for t in range(sectors)]
        return moved(held, pairs, sectors), after

    def part_pairs(s, crossing):
        pairs = []
        for t in range(sectors):
            at = t - s
            if (at % 2 == 0) == crossing:
                pairs.append((device(at), device(at - 1)))
            elif t + 2 < sectors:
                pairs.append((device(at), device(at + 1)))
        return pairs

    current = start_env[0]
    kept, raised, direct = {}, {}, {}
    work = scratch(4, channels, size)
    late = sites - 1
    for s in range(sites):
        control = jnp.stack([3 * odd, fresh_of(s - 1)])
        if s == 0:
            edge, inner = pl.pallas_call(
                moving_parts,
                out_shape=(block_shape,) * 2,
                in_specs=[SMEM, SMEM, VMEM, VMEM],
                out_specs=(VMEM,) * 2,
                scratch_shapes=work,
                compiler_params=PARAMS,
                cost_estimate=cost(2, 4),
                name="first",
            )(control, scales[0], current, blocks)
        else:
            if s not in scales:
                scales[s] = weights_of(parcels[s])
            current, edge, inner = pl.pallas_call(
                lead_kernel,
                out_shape=(block_shape,) * 3,
                in_specs=[SMEM, SMEM] + [VMEM] * 4,
                out_specs=(VMEM,) * 3,
                scratch_shapes=work,
                compiler_params=PARAMS,
                cost_estimate=cost(2, 6),
                name="lead",
            )(control, scales[s], cross, swap, stay, parcels[s])
            kept[s] = current
        cross = moved(edge, part_pairs(s, True), sectors)
        swap = moved(inner, part_pairs(s, False), sectors)
        if s == 0:
            turned, scales[1] = pack(scales[1])
        stay = pl.pallas_call(
            stay_kernel,
            out_shape=block_shape,
            in_specs=[SMEM, VMEM, VMEM],
            out_specs=VMEM,
            scratch_shapes=work,
            compiler_params=PARAMS,
            cost_estimate=cost(40, 4),
            name="stay",
        )(scales[s], current, parcels[s])
        if s in (1, late):
            direct[s] = moved(kept[s], [(device(t - s), (s, t)) for t in range(sectors)], sectors)
        elif s:
            raised[s] = moved(
                kept[s],
                [(device(t - s), (s, (t - s) % sectors)) for t in range(sectors)],
                sectors,
            )
        if s - 1 in raised and s < late:
            stay, raised[s - 1] = lax.optimization_barrier((stay, raised[s - 1]))
        ahead = s + 2
        if early <= ahead < sites:
            parcels[ahead], stay = fetch(ahead, stay)

    resting = [raised[r] for r in range(2, late)]
    ended = pl.pallas_call(
        functools.partial(last_kernel, len(resting)),
        out_shape=block_shape,
        in_specs=[SMEM] + [VMEM] * 3 + [ANY] * len(resting),
        out_specs=VMEM,
        scratch_shapes=[pltpu.SemaphoreType.DMA],
        compiler_params=PARAMS,
        name="last",
    )(
        jnp.stack([jnp.maximum(row - 1, 0), fresh_of(sites - 1)]),
        cross,
        swap,
        stay,
        *resting,
    )
    pairs = [(device(t - sites), (0, t)) for t in range(sectors)]
    for r in range(2, late):
        pairs += [((r, (t - r) % sectors), (r, t)) for t in range(sectors)]
    home = moved(ended, pairs, sectors)
    out = pl.pallas_call(
        functools.partial(pick_kernel, 3),
        out_shape=block_shape,
        in_specs=[SMEM, VMEM, ANY, ANY],
        out_specs=ANY,
        scratch_shapes=[pltpu.SemaphoreType.DMA],
        name="pick",
    )(
        jnp.stack([jnp.where(row == 1, 1, jnp.where(row == late, 2, 0))]),
        home,
        direct[1],
        direct[late],
    )
    return out[None, None]


def solution(mesh):
    return jax.shard_map(
        local,
        mesh=mesh,
        in_specs=(
            P("site", "sector", None, None, None),
            P("site", None, None, None),
            P("site", None, None, None),
            P("site", "sector", None),
            P("sector", None, None, None),
        ),
        out_specs=P("site", "sector", None, None, None),
        check_vma=False,
    )
```

time: 198 us -> 207 us (1.045)
  the two profiles are of different devices: /device:TPU:7 before, /device:TPU:10 now
where the time goes in v2:
time: 207 us; the launch traced here: 206 us
  starting transfers between devices  78.6 us (38%)
  waiting for transfers between devices  75.4 us (36%)
  Pallas kernels  45.1 us (22%)
  local copies, waits for them, and re-layouts  3.9 us (2%)
  other arithmetic  2.16 us (1%)
    ppermute x34, starting transfers between devices, moved(): return lax.ppermute(x, AXES, flat)  78.6 us
    ppermute x34, waiting for transfers between devices, moved(): return lax.ppermute(x, AXES, flat)  75.4 us
    pallas_call x1, Pallas kernels, local(): pl.pallas_call(functools.partial(pick_kernel, 3), out_shape=block_shape,...  18 us
    pallas_call x8, Pallas kernels, local(): pl.pallas_call(stay_kernel, out_shape=block_shape, in_specs=[SMEM, VMEM,...  12.3 us
    pallas_call x7, Pallas kernels, local(): pl.pallas_call(lead_kernel, out_shape=(block_shape,) * 3, in_specs=[SMEM,...  11.9 us
  transfers between devices with their start and end apart: 34, of which 4 were waited for; matrix products, arithmetic and copies ran while one was open for 0% of the time, Pallas kernels for 13%

profile of v2, /device:TPU:10, one launch (start us, length us, event | category | flops | bytes accessed | tf_op | source)
XLA Modules:
  0.0 206.1 jit_solution(170935268182814400)
XLA Ops:
  3.6 1.6 collective-permute-start.4
  8.0 2.0 first.1
  11.6 1.5 stay.8.stay_ref
  15.3 12.9 %collective-permute-done.4.a_ref = bf16[1024,256]{1,0:T(8,128)(2,1)S(1)} collective-permute-done((bf16[1024,256]{1,0:T(8,128)(2,1)}, bf16[1024,256]{1,0:T(8,128)(2,1)S(1)}, u32[]{:S(2)}, u32[]{:S(2)}) %collective-permute-start.4) | collective-permute-done | bytes 524320 | tf_op jit(solution)/shard_map/ppermute | solution.py:17
  28.2 1.7 lead.7
  31.2 1.5 stay.9.stay_ref
  34.9 1.7 lead.8
  38.6 1.5 stay.10.stay_ref
  40.9 1.7 lead.9
  44.0 1.5 stay.11.stay_ref
  47.0 1.8 lead.10
  53.9 1.7 lead.11
  57.6 1.5 stay.13.stay_ref
  59.8 11.6 %collective-permute-done.22.a_ref = bf16[1040,256]{1,0:T(8,128)(2,1)S(1)} collective-permute-done((bf16[1040,256]{1,0:T(8,128)(2,1)S(1)}, bf16[1040,256]{1,0:T(8,128)(2,1)S(1)}, u32[]{:S(2)}, u32[]{:S(2)}) %collective-permute-start.22) | collective-permute-done | bytes 532512 | tf_op jit(solution)/shard_map/ppermute | solution.py:17
  72.8 39.8 %collective-permute-done.24.swap_ref = bf16[4,256,256]{2,1,0:T(8,128)(2,1)S(1)} collective-permute-done((bf16[4,256,256]{2,1,0:T(8,128)(2,1)S(1)}, bf16[4,256,256]{2,1,0:T(8,128)(2,1)S(1)}, u32[]{:S(2)}, u32[]{:S(2)}) %collective-permute-start.24) | collective-permute-done | bytes 524320 | tf_op jit(solution)/shard_map/ppermute | solution.py:17
  112.6 1.7 lead.12
  115.6 19.7 %collective-permute-start.26 = (bf16[4,256,256]{2,1,0:T(8,128)(2,1)S(1)}, bf16[4,256,256]{2,1,0:T(8,128)(2,1)S(1)}, u32[]{:S(2)}, u32[]{:S(2)}) collective-permute-start(bf16[4,256,256]{2,1,0:T(8,128)(2,1)S(1)} %get-tuple-element.83), channel_id=1, source_target_pairs={{66,67},{67,66},{68,69},{69,68},{70,71},{71,70},{0,1},{1,0},{2,3},... | collective-permute-start | bytes 1572872 | tf_op jit(solution)/shard_map/ppermute | solution.py:17
  135.3 1.5 stay.14.stay_ref
  138.2 1.7 lead.13
  139.9 1.9 collective-permute-start.28
  141.9 12.2 %collective-permute-start.29 = (bf16[4,256,256]{2,1,0:T(8,128)(2,1)S(1)}, bf16[4,256,256]{2,1,0:T(8,128)(2,1)S(1)}, u32[]{:S(2)}, u32[]{:S(2)}) collective-permute-start(bf16[4,256,256]{2,1,0:T(8,128)(2,1)S(1)} %get-tuple-element.87), channel_id=1, source_target_pairs={{65,64},{66,67},{67,66},{68,69},{69,68},{70,71},{71,70},{0,1},{1,0... | collective-permute-start | bytes 1572872 | tf_op jit(solution)/shard_map/ppermute | solution.py:17
  157.8 18.3 %collective-permute-start.31 = (bf16[4,256,256]{2,1,0:T(8,128)(2,1)S(1)}, bf16[4,256,256]{2,1,0:T(8,128)(2,1)S(1)}, u32[]{:S(2)}, u32[]{:S(2)}) collective-permute-start(bf16[4,256,256]{2,1,0:T(8,128)(2,1)S(1)} %last.1), channel_id=1, source_target_pairs={{64,0},{65,1},{66,2},{67,3},{68,4},{69,5},{70,6},{71,7},{0,8},{1,9... | collective-permute-start | bytes 1572872 | tf_op jit(solution)/shard_map/ppermute | solution.py:17
  176.1 11.0 %collective-permute-done.31.refs_0_ = bf16[4,256,256]{2,1,0:T(8,128)(2,1)S(1)} collective-permute-done((bf16[4,256,256]{2,1,0:T(8,128)(2,1)S(1)}, bf16[4,256,256]{2,1,0:T(8,128)(2,1)S(1)}, u32[]{:S(2)}, u32[]{:S(2)}) %collective-permute-start.31) | collective-permute-done | bytes 524320 | tf_op jit(solution)/shard_map/ppermute | solution.py:17
  187.9 18.0 %pick.1 = bf16[4,256,256]{2,1,0:T(8,128)(2,1)} custom-call(s32[1]{0:T(128)} %bitcast.p_ref, bf16[4,256,256]{2,1,0:T(8,128)(2,1)} %copy-done.7, bf16[4,256,256]{2,1,0:T(8,128)(2,1)} %copy-done.5, bf16[4,256,256]{2,1,0:T(8,128)(2,1)} %copy-done.6), custom_call_target="tpu_custom_call" | custom-call | tf_op jit(solution)/shard_map/pick/pallas_call | solution.py:284
  (104 shorter events, 34.9 us)
Async XLA Ops:
  1.6 12.2 %collective-permute-start = (f32[64]{0:T(128)S(1)}, f32[64]{0:T(128)S(1)}, u32[]{:S(2)}, u32[]{:S(2)}) collective-permute-start(f32[64]{0:T(128)S(1)} %reshape.15.w_ref), channel_id=1, source_target_pairs={{64,71},{65,0},{66,1},{67,2},{68,3},{69,4},{70,5},{71,6},{72,7},{7... | collective-permute-start | bytes 776 | tf_op jit(solution)/shard_map/ppermute | solution.py:17
  2.9 31.2 %collective-permute-start.6 = (f32[64]{0:T(128)S(1)}, f32[64]{0:T(128)S(1)}, u32[]{:S(2)}, u32[]{:S(2)}) collective-permute-start(f32[64]{0:T(128)S(1)} %reshape.15.w_ref), channel_id=1, source_target_pairs={{128,70},{129,71},{130,0},{131,1},{132,2},{133,3},{134,4},{135,5},... | collective-permute-start | bytes 776 | tf_op jit(solution)/shard_map/ppermute | solution.py:17
  3.6 24.6 %collective-permute-start.4 = (bf16[1024,256]{1,0:T(8,128)(2,1)}, bf16[1024,256]{1,0:T(8,128)(2,1)S(1)}, u32[]{:S(2)}, u32[]{:S(2)}) collective-permute-start(bf16[1024,256]{1,0:T(8,128)(2,1)} %bitcast.39), channel_id=1, source_target_pairs={{64,71},{65,0},{66,1},{67,2},{68,3},{69,4},{70,5},{71,6},{72,7},{7... | collective-permute-start | bytes 1572872 | tf_op jit(solution)/shard_map/ppermute | solution.py:17
  5.2 29.7 %collective-permute-start.9 = (bf16[1024,256]{1,0:T(8,128)(2,1)}, bf16[1024,256]{1,0:T(8,128)(2,1)S(1)}, u32[]{:S(2)}, u32[]{:S(2)}) collective-permute-start(bf16[1024,256]{1,0:T(8,128)(2,1)} %bitcast.40), channel_id=1, source_target_pairs={{128,70},{129,71},{130,0},{131,1},{132,2},{133,3},{134,4},{135,5},... | collective-permute-start | bytes 1572872 | tf_op jit(solution)/shard_map/ppermute | solution.py:17
  14.6 18.2 %collective-permute-start.1 = (bf16[1040,256]{1,0:T(8,128)(2,1)S(1)}, bf16[1040,256]{1,0:T(8,128)(2,1)S(1)}, u32[]{:S(2)}, u32[]{:S(2)}) collective-permute-start(bf16[1040,256]{1,0:T(8,128)(2,1)S(1)} %pad_maximum_fusion), channel_id=1, source_target_pairs={{192,253},{193,254},{194,255},{195,192},{196,193},{197,194},{198,1... | collective-permute-start | bytes 1597448 | tf_op jit(solution)/shard_map/ppermute | solution.py:17
  32.8 143.3 %collective-permute-start.32 = (bf16[4,256,256]{2,1,0:T(8,128)(2,1)S(1)}, bf16[4,256,256]{2,1,0:T(8,128)(2,1)S(1)}, u32[]{:S(2)}, u32[]{:S(2)}) collective-permute-start(bf16[4,256,256]{2,1,0:T(8,128)(2,1)S(1)} %get-tuple-element.54.env_ref), channel_id=1, source_target_pairs={{71,64},{0,65},{1,66},{2,67},{3,68},{4,69},{5,70},{6,71},{7,72},{8... | collective-permute-start | bytes 1572872 | tf_op jit(solution)/shard_map/ppermute | solution.py:17
  34.1 6.1 %collective-permute-start.5 = (bf16[1040,256]{1,0:T(8,128)(2,1)S(1)}, bf16[1040,256]{1,0:T(8,128)(2,1)S(1)}, u32[]{:S(2)}, u32[]{:S(2)}) collective-permute-start(bf16[1040,256]{1,0:T(8,128)(2,1)S(1)} %collective-permute-done.1), channel_id=1, source_target_pairs={{253,69},{254,70},{255,71},{192,0},{193,1},{194,2},{195,3},{196,4}... | collective-permute-start | bytes 1597448 | tf_op jit(solution)/shard_map/ppermute | solution.py:17
  37.9 7.6 %collective-permute-start.12 = (bf16[4,256,256]{2,1,0:T(8,128)(2,1)S(1)}, bf16[4,256,256]{2,1,0:T(8,128)(2,1)S(1)}, u32[]{:S(2)}, u32[]{:S(2)}) collective-permute-start(bf16[4,256,256]{2,1,0:T(8,128)(2,1)S(1)} %get-tuple-element.61.env_ref), channel_id=1, source_target_pairs={{70,190},{71,191},{0,128},{1,129},{2,130},{3,131},{4,132},{5,133},... | collective-permute-start | bytes 1572872 | tf_op jit(solution)/shard_map/ppermute | solution.py:17
  40.2 6.1 %collective-permute-start.14 = (bf16[1040,256]{1,0:T(8,128)(2,1)S(1)}, bf16[1040,256]{1,0:T(8,128)(2,1)S(1)}, u32[]{:S(2)}, u32[]{:S(2)}) collective-permute-start(bf16[1040,256]{1,0:T(8,128)(2,1)S(1)} %collective-permute-done.1), channel_id=1, source_target_pairs={{316,68},{317,69},{318,70},{319,71},{256,0},{257,1},{258,2},{259,3... | collective-permute-start | bytes 1597448 | tf_op jit(solution)/shard_map/ppermute | solution.py:17
  45.6 6.3 %collective-permute-start.19 = (bf16[4,256,256]{2,1,0:T(8,128)(2,1)S(1)}, bf16[4,256,256]{2,1,0:T(8,128)(2,1)S(1)}, u32[]{:S(2)}, u32[]{:S(2)}) collective-permute-start(bf16[4,256,256]{2,1,0:T(8,128)(2,1)S(1)} %get-tuple-element.63.env_ref), channel_id=1, source_target_pairs={{69,253},{70,254},{71,255},{0,192},{1,193},{2,194},{3,195},{4,196}... | collective-permute-start | bytes 1572872 | tf_op jit(solution)/shard_map/ppermute | solution.py:17
  46.3 6.3 %collective-permute-start.13 = (bf16[1040,256]{1,0:T(8,128)(2,1)S(1)}, bf16[1040,256]{1,0:T(8,128)(2,1)S(1)}, u32[]{:S(2)}, u32[]{:S(2)}) collective-permute-start(bf16[1040,256]{1,0:T(8,128)(2,1)S(1)} %collective-permute-done.1), channel_id=1, source_target_pairs={{379,67},{380,68},{381,69},{382,70},{383,71},{320,0},{321,1},{322,... | collective-permute-start | bytes 1597448 | tf_op jit(solution)/shard_map/ppermute | solution.py:17
  51.8 7.3 %collective-permute-start.20 = (bf16[4,256,256]{2,1,0:T(8,128)(2,1)S(1)}, bf16[4,256,256]{2,1,0:T(8,128)(2,1)S(1)}, u32[]{:S(2)}, u32[]{:S(2)}) collective-permute-start(bf16[4,256,256]{2,1,0:T(8,128)(2,1)S(1)} %get-tuple-element.72.env_ref), channel_id=1, source_target_pairs={{68,316},{69,317},{70,318},{71,319},{0,256},{1,257},{2,258},{3,259... | collective-permute-start | bytes 1572872 | tf_op jit(solution)/shard_map/ppermute | solution.py:17
  52.6 18.9 %collective-permute-start.22 = (bf16[1040,256]{1,0:T(8,128)(2,1)S(1)}, bf16[1040,256]{1,0:T(8,128)(2,1)S(1)}, u32[]{:S(2)}, u32[]{:S(2)}) collective-permute-start(bf16[1040,256]{1,0:T(8,128)(2,1)S(1)} %collective-permute-done.1), channel_id=1, source_target_pairs={{442,66},{443,67},{444,68},{445,69},{446,70},{447,71},{384,0},{385... | collective-permute-start | bytes 1597448 | tf_op jit(solution)/shard_map/ppermute | solution.py:17
  55.6 17.2 %collective-permute-start.23 = (bf16[4,256,256]{2,1,0:T(8,128)(2,1)S(1)}, bf16[4,256,256]{2,1,0:T(8,128)(2,1)S(1)}, u32[]{:S(2)}, u32[]{:S(2)}) collective-permute-start(bf16[4,256,256]{2,1,0:T(8,128)(2,1)S(1)} %get-tuple-element.79), channel_id=1, source_target_pairs={{67,68},{68,67},{69,70},{70,69},{71,0},{0,71},{1,2},{2,1},{3,4},{4... | collective-permute-start | bytes 1572872 | tf_op jit(solution)/shard_map/ppermute | solution.py:17
  56.3 56.3 %collective-permute-start.24 = (bf16[4,256,256]{2,1,0:T(8,128)(2,1)S(1)}, bf16[4,256,256]{2,1,0:T(8,128)(2,1)S(1)}, u32[]{:S(2)}, u32[]{:S(2)}) collective-permute-start(bf16[4,256,256]{2,1,0:T(8,128)(2,1)S(1)} %get-tuple-element.80), channel_id=1, source_target_pairs={{67,66},{68,69},{69,68},{70,71},{71,70},{0,1},{1,0},{2,3},{3,2},{4... | collective-permute-start | bytes 1572872 | tf_op jit(solution)/shard_map/ppermute | solution.py:17
  59.1 77.7 %collective-permute-start.27 = (bf16[4,256,256]{2,1,0:T(8,128)(2,1)S(1)}, bf16[4,256,256]{2,1,0:T(8,128)(2,1)S(1)}, u32[]{:S(2)}, u32[]{:S(2)}) collective-permute-start(bf16[4,256,256]{2,1,0:T(8,128)(2,1)S(1)} %get-tuple-element.75.env_ref), channel_id=1, source_target_pairs={{67,379},{68,380},{69,381},{70,382},{71,383},{0,320},{1,321},{2,32... | collective-permute-start | bytes 1572872 | tf_op jit(solution)/shard_map/ppermute | solution.py:17
  71.4 66.7 %collective-permute-start.21 = (bf16[1040,256]{1,0:T(8,128)(2,1)S(1)}, bf16[1040,256]{1,0:T(8,128)(2,1)S(1)}, u32[]{:S(2)}, u32[]{:S(2)}) collective-permute-start(bf16[1040,256]{1,0:T(8,128)(2,1)S(1)} %collective-permute-done.1), channel_id=1, source_target_pairs={{505,65},{506,66},{507,67},{508,68},{509,69},{510,70},{511,71},{44... | collective-permute-start | bytes 1597448 | tf_op jit(solution)/shard_map/ppermute | solution.py:17
  114.3 23.9 %collective-permute-start.25 = (bf16[4,256,256]{2,1,0:T(8,128)(2,1)S(1)}, bf16[4,256,256]{2,1,0:T(8,128)(2,1)S(1)}, u32[]{:S(2)}, u32[]{:S(2)}) collective-permute-start(bf16[4,256,256]{2,1,0:T(8,128)(2,1)S(1)} %get-tuple-element.82), channel_id=1, source_target_pairs={{66,65},{67,68},{68,67},{69,70},{70,69},{71,0},{0,71},{1,2},{2,1},... | collective-permute-start | bytes 1572872 | tf_op jit(solution)/shard_map/ppermute | solution.py:17
  115.6 22.6 %collective-permute-start.26 = (bf16[4,256,256]{2,1,0:T(8,128)(2,1)S(1)}, bf16[4,256,256]{2,1,0:T(8,128)(2,1)S(1)}, u32[]{:S(2)}, u32[]{:S(2)}) collective-permute-start(bf16[4,256,256]{2,1,0:T(8,128)(2,1)S(1)} %get-tuple-element.83), channel_id=1, source_target_pairs={{66,67},{67,66},{68,69},{69,68},{70,71},{71,70},{0,1},{1,0},{2,3},... | collective-permute-start | bytes 1572872 | tf_op jit(solution)/shard_map/ppermute | solution.py:17
  136.8 20.1 %collective-permute-start.30 = (bf16[4,256,256]{2,1,0:T(8,128)(2,1)S(1)}, bf16[4,256,256]{2,1,0:T(8,128)(2,1)S(1)}, u32[]{:S(2)}, u32[]{:S(2)}) collective-permute-start(bf16[4,256,256]{2,1,0:T(8,128)(2,1)S(1)} %get-tuple-element.84.env_ref), channel_id=1, source_target_pairs={{66,442},{67,443},{68,444},{69,445},{70,446},{71,447},{0,384},{1,3... | collective-permute-start | bytes 1572872 | tf_op jit(solution)/shard_map/ppermute | solution.py:17
  139.9 17.0 %collective-permute-start.28 = (bf16[4,256,256]{2,1,0:T(8,128)(2,1)S(1)}, bf16[4,256,256]{2,1,0:T(8,128)(2,1)S(1)}, u32[]{:S(2)}, u32[]{:S(2)}) collective-permute-start(bf16[4,256,256]{2,1,0:T(8,128)(2,1)S(1)} %get-tuple-element.86), channel_id=1, source_target_pairs={{65,66},{66,65},{67,68},{68,67},{69,70},{70,69},{71,0},{0,71},{1,2... | collective-permute-start | bytes 1572872 | tf_op jit(solution)/shard_map/ppermute | solution.py:17
  141.9 15.1 %collective-permute-start.29 = (bf16[4,256,256]{2,1,0:T(8,128)(2,1)S(1)}, bf16[4,256,256]{2,1,0:T(8,128)(2,1)S(1)}, u32[]{:S(2)}, u32[]{:S(2)}) collective-permute-start(bf16[4,256,256]{2,1,0:T(8,128)(2,1)S(1)} %get-tuple-element.87), channel_id=1, source_target_pairs={{65,64},{66,67},{67,66},{68,69},{69,68},{70,71},{71,70},{0,1},{1,0... | collective-permute-start | bytes 1572872 | tf_op jit(solution)/shard_map/ppermute | solution.py:17
  154.1 22.1 %collective-permute-start.33 = (bf16[4,256,256]{2,1,0:T(8,128)(2,1)S(1)}, bf16[4,256,256]{2,1,0:T(8,128)(2,1)S(1)}, u32[]{:S(2)}, u32[]{:S(2)}) collective-permute-start(bf16[4,256,256]{2,1,0:T(8,128)(2,1)S(1)} %get-tuple-element.88.env_ref), channel_id=1, source_target_pairs={{65,448},{66,449},{67,450},{68,451},{69,452},{70,453},{71,454},{0,... | collective-permute-start | bytes 1572872 | tf_op jit(solution)/shard_map/ppermute | solution.py:17
  157.8 29.3 %collective-permute-start.31 = (bf16[4,256,256]{2,1,0:T(8,128)(2,1)S(1)}, bf16[4,256,256]{2,1,0:T(8,128)(2,1)S(1)}, u32[]{:S(2)}, u32[]{:S(2)}) collective-permute-start(bf16[4,256,256]{2,1,0:T(8,128)(2,1)S(1)} %last.1), channel_id=1, source_target_pairs={{64,0},{65,1},{66,2},{67,3},{68,4},{69,5},{70,6},{71,7},{0,8},{1,9... | collective-permute-start | bytes 1572872 | tf_op jit(solution)/shard_map/ppermute | solution.py:17
  (18 other events, 72.7 us)

commit v3 on v2

--- a/solution.py
+++ b/solution.py
@@ -8,8 +8,6 @@
 from jax.sharding import PartitionSpec as P
 
 AXES = ("site", "sector")
-RING = 8
-ROUND = (8, 7)
 
 
 def moved(x, pairs, sectors):
@@ -17,15 +15,15 @@
     return lax.ppermute(x, AXES, flat)
 
 
-def mix_and_multiply(env_ref, a_ref, w_ref, p, mixed_ref, half_ref):
+def mix_and_multiply(env_ref, a_ref, weight, p, mixed_ref, half_ref):
     size = env_ref.shape[-1]
     step = 32
     for i in range(0, size, step):
         rows = [env_ref[w, i : i + step, :].astype(jnp.float32) for w in range(4)]
         for v in range(4):
-            total = rows[0] * w_ref[p * 16 + v * 4]
+            total = rows[0] * weight(p, v, 0)
             for w in range(1, 4):
-                total = total + rows[w] * w_ref[p * 16 + v * 4 + w]
+                total = total + rows[w] * weight(p, v, w)
             mixed_ref[v * size + i : v * size + i + step, :] = total.astype(jnp.bfloat16)
     block = a_ref[pl.ds(pl.multiple_of(p * size, size), size), :]
     half_ref[...] = jnp.dot(
@@ -40,32 +38,51 @@
     )
 
 
-def one_unit(env_ref, a_ref, w_ref, p, mixed_ref, half_ref, out_ref):
-    size = env_ref.shape[-1]
-    block = mix_and_multiply(env_ref, a_ref, w_ref, p, mixed_ref, half_ref)
+def one_unit(env_ref, a_ref, weight, p, mixed_ref, half_ref, out_ref):
+    size = env_ref.shape[-1]
+    block = mix_and_multiply(env_ref, a_ref, weight, p, mixed_ref, half_ref)
     for v in range(4):
         half = half_ref[v * size : (v + 1) * size, :]
         out_ref[v] = close(block, half).astype(jnp.bfloat16)
 
 
-def stay_part(env_ref, a_ref, w_ref, mixed_ref, half_ref, mixed2_ref, half2_ref, out_ref):
-    size = env_ref.shape[-1]
-    first = mix_and_multiply(env_ref, a_ref, w_ref, 1, mixed_ref, half_ref)
-    second = mix_and_multiply(env_ref, a_ref, w_ref, 2, mixed2_ref, half2_ref)
+def listed(w_ref):
+    return lambda p, v, w: w_ref[p * 16 + v * 4 + w]
+
+
+def stay_kernel(w_ref, env_ref, a_ref, out_ref, mixed_ref, half_ref, mixed2_ref, half2_ref):
+    size = env_ref.shape[-1]
+    weight = listed(w_ref)
+    first = mix_and_multiply(env_ref, a_ref, weight, 1, mixed_ref, half_ref)
+    second = mix_and_multiply(env_ref, a_ref, weight, 2, mixed2_ref, half2_ref)
     for v in range(4):
         at = slice(v * size, (v + 1) * size)
         total = close(first, half_ref[at, :]) + close(second, half2_ref[at, :])
         out_ref[v] = total.astype(jnp.bfloat16)
 
 
-def stay_kernel(w_ref, env_ref, a_ref, out_ref, *work):
-    stay_part(env_ref, a_ref, w_ref, *work, out_ref)
-
-
-def moving_parts(p_ref, w_ref, env_ref, a_ref, edge_ref, inner_ref, *work):
+def inner_kernel(p_ref, w_ref, env_ref, a_ref, out_ref, *work):
+    one_unit(env_ref, a_ref, listed(w_ref), 3 - p_ref[0], *work, out_ref)
+
+
+def first_kernel(
+    p_ref, operator_ref, mask_ref, couple_ref, env_any, a_any, edge_ref, env_ref, a_ref, mixed_ref, half_ref, sems
+):
+    size = env_ref.shape[-1]
     edge = p_ref[0]
-    one_unit(env_ref, a_ref, w_ref, edge, *work[:2], edge_ref)
-    one_unit(env_ref, a_ref, w_ref, 3 - edge, *work[2:], inner_ref)
+    rows = pl.ds(pl.multiple_of(edge * size, size), size)
+    copies = [pltpu.make_async_copy(env_any.at[w], env_ref.at[w], sems.at[w]) for w in range(4)]
+    copies.append(pltpu.make_async_copy(a_any.at[rows], a_ref.at[rows], sems.at[4]))
+    for copy in copies:
+        copy.start()
+    for copy in copies:
+        copy.wait()
+
+    def weight(p, v, w):
+        scale = operator_ref[w, v, p] * mask_ref[w, v, p].astype(jnp.float32)
+        return scale * couple_ref[p].astype(jnp.float32)
+
+    one_unit(env_ref, a_ref, weight, edge, mixed_ref, half_ref, edge_ref)
 
 
 def summed(fresh, cross_ref, swap_ref, stay_ref, env_ref):
@@ -90,11 +107,9 @@
         add((swap_ref, stay_ref, cross_ref))
 
 
-def lead_kernel(
-    p_ref, w_ref, cross_ref, swap_ref, stay_ref, a_ref, env_ref, edge_ref, inner_ref, *work
-):
+def lead_kernel(p_ref, w_ref, cross_ref, swap_ref, stay_ref, a_ref, env_ref, edge_ref, *work):
     summed(p_ref[1], cross_ref, swap_ref, stay_ref, env_ref)
-    moving_parts(p_ref, w_ref, env_ref, a_ref, edge_ref, inner_ref, *work)
+    one_unit(env_ref, a_ref, listed(w_ref), p_ref[0], *work, edge_ref)
 
 
 def last_kernel(count, p_ref, cross_ref, swap_ref, stay_ref, *refs):
@@ -127,6 +142,8 @@
 VMEM = pl.BlockSpec(memory_space=pltpu.VMEM)
 SMEM = pl.BlockSpec(memory_space=pltpu.SMEM)
 ANY = pl.BlockSpec(memory_space=pl.ANY)
+HBM = pl.BlockSpec(memory_space=pltpu.HBM)
+WHOLE = pltpu.CompilerParams(vmem_limit_bytes=64400 * 1024)
 PARAMS = pltpu.CompilerParams(vmem_limit_bytes=24 * 1024 * 1024)
 
 
@@ -165,32 +182,23 @@
     def straight_pairs(s):
         return [((s, t), device(t - s)) for t in range(sectors)]
 
-    early = min(3, sites)
+    early = min(2, sites)
     parcels = {s: moved(blocks, straight_pairs(s), sectors) for s in range(1, early)}
-    scales = {s: moved(weights, straight_pairs(s), sectors) for s in range(1, early)}
-    parcels[0], scales[0] = blocks, weights
-
-    def pack(after):
-        held, lying, after = lax.optimization_barrier((weights, blocks, after))
-        high = lax.reduce_precision(held, *ROUND)
-        middle = lax.reduce_precision(held - high, *ROUND)
-        low = lax.reduce_precision(held - high - middle, *ROUND)
-        pieces = jnp.stack([high, middle, low]).astype(jnp.bfloat16)
-        pieces = jnp.pad(pieces, ((0, 13), (0, size - pieces.shape[1])))
-        packed = jnp.concatenate([lying, pieces], axis=0)
-        pairs = [
-            ((s, t), (s, (t - s) % sectors)) for s in range(early, sites) for t in range(sectors)
-        ]
-        return moved(packed, pairs, sectors), after
-
-    def weights_of(parcel):
-        parts = parcel[states * size : states * size + 3, : weights.shape[0]].astype(jnp.float32)
-        return parts[0] + parts[1] + parts[2]
+    parcels[0], scales = blocks, {0: weights}
+    turned = moved(
+        blocks,
+        [((s, t), (s, (t - s) % sectors)) for s in range(early, sites) for t in range(sectors)],
+        sectors,
+    )
 
     def fetch(s, after):
         held, after = lax.optimization_barrier((turned, after))
         pairs = [((s, (t - s) % sectors), device(t - s)) for t in range(sectors)]
         return moved(held, pairs, sectors), after
+
+    def fetch_weights(s, after):
+        held, after = lax.optimization_barrier((weights, after))
+        return moved(held, straight_pairs(s), sectors), after
 
     def part_pairs(s, crossing):
         pairs = []
@@ -209,34 +217,48 @@
     for s in range(sites):
         control = jnp.stack([3 * odd, fresh_of(s - 1)])
         if s == 0:
-            edge, inner = pl.pallas_call(
-                moving_parts,
+            edge = pl.pallas_call(
+                first_kernel,
+                out_shape=block_shape,
+                in_specs=[SMEM] * 4 + [HBM] * 2,
+                out_specs=VMEM,
+                scratch_shapes=[
+                    pltpu.VMEM((channels, size, size), jnp.bfloat16),
+                    pltpu.VMEM((states * size, size), jnp.bfloat16),
+                ]
+                + work[:2]
+                + [pltpu.SemaphoreType.DMA((5,))],
+                compiler_params=WHOLE,
+                cost_estimate=cost(1, 4),
+                name="first",
+            )(control, operators[0], op_mask[0], coupling[0, 0], current, blocks)
+        else:
+            current, edge = pl.pallas_call(
+                lead_kernel,
                 out_shape=(block_shape,) * 2,
-                in_specs=[SMEM, SMEM, VMEM, VMEM],
+                in_specs=[SMEM, SMEM] + [VMEM] * 4,
                 out_specs=(VMEM,) * 2,
-                scratch_shapes=work,
+                scratch_shapes=work[:2],
                 compiler_params=PARAMS,
-                cost_estimate=cost(2, 4),
-                name="first",
-            )(control, scales[0], current, blocks)
-        else:
-            if s not in scales:
-                scales[s] = weights_of(parcels[s])
-            current, edge, inner = pl.pallas_call(
-                lead_kernel,
-                out_shape=(block_shape,) * 3,
-                in_specs=[SMEM, SMEM] + [VMEM] * 4,
-                out_specs=(VMEM,) * 3,
-                scratch_shapes=work,
-                compiler_params=PARAMS,
-                cost_estimate=cost(2, 6),
+                cost_estimate=cost(1, 6),
                 name="lead",
             )(control, scales[s], cross, swap, stay, parcels[s])
             kept[s] = current
         cross = moved(edge, part_pairs(s, True), sectors)
+        source = current
+        if s == 0:
+            source, _ = lax.optimization_barrier((current, edge))
+        inner = pl.pallas_call(
+            inner_kernel,
+            out_shape=block_shape,
+            in_specs=[SMEM, SMEM, VMEM, VMEM],
+            out_specs=VMEM,
+            scratch_shapes=work[:2],
+            compiler_params=PARAMS,
+            cost_estimate=cost(1, 4),
+            name="inner",
+        )(control, scales[s], source, parcels[s])
         swap = moved(inner, part_pairs(s, False), sectors)
-        if s == 0:
-            turned, scales[1] = pack(scales[1])
         stay = pl.pallas_call(
             stay_kernel,
             out_shape=block_shape,
@@ -246,7 +268,7 @@
             compiler_params=PARAMS,
             cost_estimate=cost(40, 4),
             name="stay",
-        )(scales[s], current, parcels[s])
+        )(scales[s], source, parcels[s])
         if s in (1, late):
             direct[s] = moved(kept[s], [(device(t - s), (s, t)) for t in range(sectors)], sectors)
         elif s:
@@ -257,9 +279,11 @@
             )
         if s - 1 in raised and s < late:
             stay, raised[s - 1] = lax.optimization_barrier((stay, raised[s - 1]))
-        ahead = s + 2
-        if early <= ahead < sites:
-            parcels[ahead], stay = fetch(ahead, stay)
+        if s == 0:
+            scales[1], swap = fetch_weights(1, swap)
+        if s + 2 < sites:
+            parcels[s + 2], stay = fetch(s + 2, stay)
+            scales[s + 2], stay = fetch_weights(s + 2, stay)
 
     resting = [raised[r] for r in range(2, late)]
     ended = pl.pallas_call(
@@ -285,8 +309,9 @@
         functools.partial(pick_kernel, 3),
         out_shape=block_shape,
         in_specs=[SMEM, VMEM, ANY, ANY],
-        out_specs=ANY,
+        out_specs=VMEM,
         scratch_shapes=[pltpu.SemaphoreType.DMA],
+        compiler_params=PARAMS,
         name="pick",
     )(
         jnp.stack([jnp.where(row == 1, 1, jnp.where(row == late, 2, 0))]),

time: 207 us -> 230 us (1.11)
  the two profiles are of different devices: /device:TPU:10 before, /device:TPU:25 now
where the time goes in v3:
time: 230 us; the launch traced here: 229 us
  starting transfers between devices  144 us (63%)
  waiting for transfers between devices  44.3 us (19%)
  Pallas kernels  38 us (17%)
    ppermute x39, starting transfers between devices, moved(): return lax.ppermute(x, AXES, flat)  144 us
    ppermute x39, waiting for transfers between devices, moved(): return lax.ppermute(x, AXES, flat)  44.3 us
    pallas_call x8, Pallas kernels, local(): pl.pallas_call(stay_kernel, out_shape=block_shape, in_specs=[SMEM, VMEM,...  12.8 us
    pallas_call x7, Pallas kernels, local(): pl.pallas_call(lead_kernel, out_shape=(block_shape,) * 2, in_specs=[SMEM,...  10.1 us
    pallas_call x8, Pallas kernels, local(): pl.pallas_call(inner_kernel, out_shape=block_shape, in_specs=[SMEM, SMEM,...  9.89 us
  transfers between devices with their start and end apart: 39, of which 3 were waited for; matrix products, arithmetic and copies ran while one was open for 1% of the time, Pallas kernels for 16%

profile of v3, /device:TPU:25, one launch (start us, length us, event | category | flops | bytes accessed | tf_op | source)
XLA Modules:
  0.0 229.3 jit_solution(15033617244392498176)
XLA Ops:
  0.0 18.6 %collective-permute-start = (bf16[1024,256]{1,0:T(8,128)(2,1)}, bf16[1024,256]{1,0:T(8,128)(2,1)}, u32[]{:S(2)}, u32[]{:S(2)}) collective-permute-start(bf16[1024,256]{1,0:T(8,128)(2,1)} %bitcast.27), channel_id=1, source_target_pairs={{128,190},{129,191},{130,128},{131,129},{132,130},{133,131},{134,1... | collective-permute-start | bytes 1572872 | tf_op jit(solution)/shard_map/ppermute | solution.py:15
  18.6 1.5 collective-permute-start.4
  20.7 3.7 %first.1 = bf16[4,256,256]{2,1,0:T(8,128)(2,1)} custom-call(s32[2]{0:T(128)} %pad_add_fusion.2.p_ref, f32[4,4,4]{2,1,0:T(4,128)} %bitcast.33, s32[4,4,4]{2,1,0:T(4,128)} %bitcast.32, s32[4]{0:T(128)} %bitcast.34, bf16[4,256,256]{2,1,0:T(8,128)(2,1)} %bitcast.24, bf16[1024,256]{1,0:T(8,128)(2,1)} %bitcast.29), custom_call_target="tpu_custom_call" | custom-call | flops 268435456 | bytes 2097152 | tf_op jit(solution)/shard_map/first/pallas_call | solution.py:220
  27.7 1.5 stay.8.stay_ref
  32.0 1.9 lead.7
  34.6 1.7 inner.9
  37.0 2.1 stay.9.stay_ref
  39.0 11.6 %collective-permute-start.5 = (f32[64]{0:T(128)S(1)}, f32[64]{0:T(128)S(1)}, u32[]{:S(2)}, u32[]{:S(2)}) collective-permute-start(f32[64]{0:T(128)S(1)} %reshape.3.w_ref), channel_id=1, source_target_pairs={{192,69},{193,70},{194,71},{195,0},{196,1},{197,2},{198,3},{199,4}... | collective-permute-start | bytes 776 | tf_op jit(solution)/shard_map/ppermute | solution.py:15
  50.7 5.2 %collective-permute-start.12 = (bf16[1024,256]{1,0:T(8,128)(2,1)}, bf16[1024,256]{1,0:T(8,128)(2,1)S(1)}, u32[]{:S(2)}, u32[]{:S(2)}) collective-permute-start(bf16[1024,256]{1,0:T(8,128)(2,1)} %collective-permute-done), channel_id=1, source_target_pairs={{253,69},{254,70},{255,71},{192,0},{193,1},{194,2},{195,3},{196,4}... | collective-permute-start | bytes 1572872 | tf_op jit(solution)/shard_map/ppermute | solution.py:15
  56.0 1.4 lead.8
  60.6 1.5 stay.10.stay_ref
  62.8 4.2 %collective-permute-done.12.a_ref = bf16[1024,256]{1,0:T(8,128)(2,1)S(1)} collective-permute-done((bf16[1024,256]{1,0:T(8,128)(2,1)}, bf16[1024,256]{1,0:T(8,128)(2,1)S(1)}, u32[]{:S(2)}, u32[]{:S(2)}) %collective-permute-start.12) | collective-permute-done | bytes 524320 | tf_op jit(solution)/shard_map/ppermute | solution.py:15
  67.7 1.4 lead.9
  71.9 1.5 stay.11.stay_ref
  80.1 1.5 stay.12.stay_ref
  81.6 19.2 %collective-permute-done.21.refs_1_ = bf16[4,256,256]{2,1,0:T(8,128)(2,1)S(1)} collective-permute-done((bf16[4,256,256]{2,1,0:T(8,128)(2,1)S(1)}, bf16[4,256,256]{2,1,0:T(8,128)(2,1)S(1)}, u32[]{:S(2)}, u32[]{:S(2)}) %collective-permute-start.21) | collective-permute-done | bytes 524320 | tf_op jit(solution)/shard_map/ppermute | solution.py:15
  106.9 1.5 stay.13.stay_ref
  109.1 36.2 %collective-permute-start.24 = (f32[64]{0:T(128)S(1)}, f32[64]{0:T(128)S(1)}, u32[]{:S(2)}, u32[]{:S(2)}) collective-permute-start(f32[64]{0:T(128)S(1)} %reshape.3.w_ref), channel_id=1, source_target_pairs={{448,65},{449,66},{450,67},{451,68},{452,69},{453,70},{454,71},{45... | collective-permute-start | bytes 776 | tf_op jit(solution)/shard_map/ppermute | solution.py:15
  146.0 1.4 lead.12
  150.0 1.5 stay.14.stay_ref
  153.0 1.4 lead.13
  157.9 1.5 stay.15.stay_ref
  160.1 47.3 %collective-permute-start.36 = (bf16[4,256,256]{2,1,0:T(8,128)(2,1)S(1)}, bf16[4,256,256]{2,1,0:T(8,128)(2,1)S(1)}, u32[]{:S(2)}, u32[]{:S(2)}) collective-permute-start(bf16[4,256,256]{2,1,0:T(8,128)(2,1)S(1)} %last.1), channel_id=1, source_target_pairs={{64,0},{65,1},{66,2},{67,3},{68,4},{69,5},{70,6},{71,7},{0,8},{1,9... | collective-permute-start | bytes 1572872 | tf_op jit(solution)/shard_map/ppermute | solution.py:15
  207.4 20.8 %collective-permute-done.36.refs_0_ = bf16[4,256,256]{2,1,0:T(8,128)(2,1)S(1)} collective-permute-done((bf16[4,256,256]{2,1,0:T(8,128)(2,1)S(1)}, bf16[4,256,256]{2,1,0:T(8,128)(2,1)S(1)}, u32[]{:S(2)}, u32[]{:S(2)}) %collective-permute-start.36) | collective-permute-done | bytes 524320 | tf_op jit(solution)/shard_map/ppermute | solution.py:15
  (105 shorter events, 38.1 us)
Async XLA Ops:
  0.0 30.6 %collective-permute-start = (bf16[1024,256]{1,0:T(8,128)(2,1)}, bf16[1024,256]{1,0:T(8,128)(2,1)}, u32[]{:S(2)}, u32[]{:S(2)}) collective-permute-start(bf16[1024,256]{1,0:T(8,128)(2,1)} %bitcast.27), channel_id=1, source_target_pairs={{128,190},{129,191},{130,128},{131,129},{132,130},{133,131},{134,1... | collective-permute-start | bytes 1572872 | tf_op jit(solution)/shard_map/ppermute | solution.py:15
  18.6 13.3 %collective-permute-start.4 = (bf16[1024,256]{1,0:T(8,128)(2,1)}, bf16[1024,256]{1,0:T(8,128)(2,1)}, u32[]{:S(2)}, u32[]{:S(2)}) collective-permute-start(bf16[1024,256]{1,0:T(8,128)(2,1)} %bitcast.28), channel_id=1, source_target_pairs={{64,71},{65,0},{66,1},{67,2},{68,3},{69,4},{70,5},{71,6},{72,7},{7... | collective-permute-start | bytes 1572872 | tf_op jit(solution)/shard_map/ppermute | solution.py:15
  30.6 20.1 %collective-permute-start.6 = (f32[64]{0:T(128)S(1)}, f32[64]{0:T(128)S(1)}, u32[]{:S(2)}, u32[]{:S(2)}) collective-permute-start(f32[64]{0:T(128)S(1)} %reshape.3.w_ref), channel_id=1, source_target_pairs={{128,70},{129,71},{130,0},{131,1},{132,2},{133,3},{134,4},{135,5},... | collective-permute-start | bytes 776 | tf_op jit(solution)/shard_map/ppermute | solution.py:15
  31.2 24.7 %collective-permute-start.9 = (bf16[1024,256]{1,0:T(8,128)(2,1)}, bf16[1024,256]{1,0:T(8,128)(2,1)S(1)}, u32[]{:S(2)}, u32[]{:S(2)}) collective-permute-start(bf16[1024,256]{1,0:T(8,128)(2,1)} %collective-permute-done), channel_id=1, source_target_pairs={{190,70},{191,71},{128,0},{129,1},{130,2},{131,3},{132,4},{133,5},... | collective-permute-start | bytes 1572872 | tf_op jit(solution)/shard_map/ppermute | solution.py:15
  33.9 22.1 %collective-permute-start.7 = (bf16[4,256,256]{2,1,0:T(8,128)(2,1)S(1)}, bf16[4,256,256]{2,1,0:T(8,128)(2,1)S(1)}, u32[]{:S(2)}, u32[]{:S(2)}) collective-permute-start(bf16[4,256,256]{2,1,0:T(8,128)(2,1)S(1)} %get-tuple-element.63), channel_id=1, source_target_pairs={{71,0},{0,71},{1,2},{2,1},{3,4},{4,3},{5,6},{6,5},{7,8},{8,7},{9,1... | collective-permute-start | bytes 1572872 | tf_op jit(solution)/shard_map/ppermute | solution.py:15
  36.3 19.7 %collective-permute-start.8 = (bf16[4,256,256]{2,1,0:T(8,128)(2,1)S(1)}, bf16[4,256,256]{2,1,0:T(8,128)(2,1)S(1)}, u32[]{:S(2)}, u32[]{:S(2)}) collective-permute-start(bf16[4,256,256]{2,1,0:T(8,128)(2,1)S(1)} %inner.9), channel_id=1, source_target_pairs={{71,70},{0,1},{1,0},{2,3},{3,2},{4,5},{5,4},{6,7},{7,6},{8,9},{9,8... | collective-permute-start | bytes 1572872 | tf_op jit(solution)/shard_map/ppermute | solution.py:15
  39.0 23.1 %collective-permute-start.5 = (f32[64]{0:T(128)S(1)}, f32[64]{0:T(128)S(1)}, u32[]{:S(2)}, u32[]{:S(2)}) collective-permute-start(f32[64]{0:T(128)S(1)} %reshape.3.w_ref), channel_id=1, source_target_pairs={{192,69},{193,70},{194,71},{195,0},{196,1},{197,2},{198,3},{199,4}... | collective-permute-start | bytes 776 | tf_op jit(solution)/shard_map/ppermute | solution.py:15
  50.7 16.3 %collective-permute-start.12 = (bf16[1024,256]{1,0:T(8,128)(2,1)}, bf16[1024,256]{1,0:T(8,128)(2,1)S(1)}, u32[]{:S(2)}, u32[]{:S(2)}) collective-permute-start(bf16[1024,256]{1,0:T(8,128)(2,1)} %collective-permute-done), channel_id=1, source_target_pairs={{253,69},{254,70},{255,71},{192,0},{193,1},{194,2},{195,3},{196,4}... | collective-permute-start | bytes 1572872 | tf_op jit(solution)/shard_map/ppermute | solution.py:15
  57.3 10.4 %collective-permute-start.10 = (bf16[4,256,256]{2,1,0:T(8,128)(2,1)S(1)}, bf16[4,256,256]{2,1,0:T(8,128)(2,1)S(1)}, u32[]{:S(2)}, u32[]{:S(2)}) collective-permute-start(bf16[4,256,256]{2,1,0:T(8,128)(2,1)S(1)} %get-tuple-element.66), channel_id=1, source_target_pairs={{70,69},{71,0},{0,71},{1,2},{2,1},{3,4},{4,3},{5,6},{6,5},{7,8},{8... | collective-permute-start | bytes 1572872 | tf_op jit(solution)/shard_map/ppermute | solution.py:15
  58.0 15.4 %collective-permute-start.13 = (bf16[4,256,256]{2,1,0:T(8,128)(2,1)S(1)}, bf16[4,256,256]{2,1,0:T(8,128)(2,1)S(1)}, u32[]{:S(2)}, u32[]{:S(2)}) collective-permute-start(bf16[4,256,256]{2,1,0:T(8,128)(2,1)S(1)} %get-tuple-element.67.env_ref), channel_id=1, source_target_pairs={{70,190},{71,191},{0,128},{1,129},{2,130},{3,131},{4,132},{5,133},... | collective-permute-start | bytes 1572872 | tf_op jit(solution)/shard_map/ppermute | solution.py:15
  62.2 12.6 %collective-permute-start.15 = (f32[64]{0:T(128)S(1)}, f32[64]{0:T(128)S(1)}, u32[]{:S(2)}, u32[]{:S(2)}) collective-permute-start(f32[64]{0:T(128)S(1)} %reshape.3.w_ref), channel_id=1, source_target_pairs={{256,68},{257,69},{258,70},{259,71},{260,0},{261,1},{262,2},{263,3... | collective-permute-start | bytes 776 | tf_op jit(solution)/shard_map/ppermute | solution.py:15
  73.4 27.4 %collective-permute-start.21 = (bf16[4,256,256]{2,1,0:T(8,128)(2,1)S(1)}, bf16[4,256,256]{2,1,0:T(8,128)(2,1)S(1)}, u32[]{:S(2)}, u32[]{:S(2)}) collective-permute-start(bf16[4,256,256]{2,1,0:T(8,128)(2,1)S(1)} %get-tuple-element.71.env_ref), channel_id=1, source_target_pairs={{69,253},{70,254},{71,255},{0,192},{1,193},{2,194},{3,195},{4,196}... | collective-permute-start | bytes 1572872 | tf_op jit(solution)/shard_map/ppermute | solution.py:15
  74.7 26.8 %collective-permute-start.14 = (f32[64]{0:T(128)S(1)}, f32[64]{0:T(128)S(1)}, u32[]{:S(2)}, u32[]{:S(2)}) collective-permute-start(f32[64]{0:T(128)S(1)} %reshape.3.w_ref), channel_id=1, source_target_pairs={{320,67},{321,68},{322,69},{323,70},{324,71},{325,0},{326,1},{327,... | collective-permute-start | bytes 776 | tf_op jit(solution)/shard_map/ppermute | solution.py:15
  75.4 26.8 %collective-permute-start.22 = (bf16[1024,256]{1,0:T(8,128)(2,1)}, bf16[1024,256]{1,0:T(8,128)(2,1)S(1)}, u32[]{:S(2)}, u32[]{:S(2)}) collective-permute-start(bf16[1024,256]{1,0:T(8,128)(2,1)} %collective-permute-done), channel_id=1, source_target_pairs={{379,67},{380,68},{381,69},{382,70},{383,71},{320,0},{321,1},{322,... | collective-permute-start | bytes 1572872 | tf_op jit(solution)/shard_map/ppermute | solution.py:15
  77.5 25.4 %collective-permute-start.19 = (bf16[4,256,256]{2,1,0:T(8,128)(2,1)S(1)}, bf16[4,256,256]{2,1,0:T(8,128)(2,1)S(1)}, u32[]{:S(2)}, u32[]{:S(2)}) collective-permute-start(bf16[4,256,256]{2,1,0:T(8,128)(2,1)S(1)} %get-tuple-element.79), channel_id=1, source_target_pairs={{68,67},{69,70},{70,69},{71,0},{0,71},{1,2},{2,1},{3,4},{4,3},{5,6... | collective-permute-start | bytes 1572872 | tf_op jit(solution)/shard_map/ppermute | solution.py:15
  79.4 23.5 %collective-permute-start.20 = (bf16[4,256,256]{2,1,0:T(8,128)(2,1)S(1)}, bf16[4,256,256]{2,1,0:T(8,128)(2,1)S(1)}, u32[]{:S(2)}, u32[]{:S(2)}) collective-permute-start(bf16[4,256,256]{2,1,0:T(8,128)(2,1)S(1)} %inner.12), channel_id=1, source_target_pairs={{68,69},{69,68},{70,71},{71,70},{0,1},{1,0},{2,3},{3,2},{4,5},{5,4... | collective-permute-start | bytes 1572872 | tf_op jit(solution)/shard_map/ppermute | solution.py:15
  102.2 43.1 %collective-permute-start.28 = (bf16[1024,256]{1,0:T(8,128)(2,1)}, bf16[1024,256]{1,0:T(8,128)(2,1)S(1)}, u32[]{:S(2)}, u32[]{:S(2)}) collective-permute-start(bf16[1024,256]{1,0:T(8,128)(2,1)} %collective-permute-done), channel_id=1, source_target_pairs={{442,66},{443,67},{444,68},{445,69},{446,70},{447,71},{384,0},{385... | collective-permute-start | bytes 1572872 | tf_op jit(solution)/shard_map/ppermute | solution.py:15
  104.3 41.7 %collective-permute-start.26 = (bf16[4,256,256]{2,1,0:T(8,128)(2,1)S(1)}, bf16[4,256,256]{2,1,0:T(8,128)(2,1)S(1)}, u32[]{:S(2)}, u32[]{:S(2)}) collective-permute-start(bf16[4,256,256]{2,1,0:T(8,128)(2,1)S(1)} %get-tuple-element.90), channel_id=1, source_target_pairs={{67,68},{68,67},{69,70},{70,69},{71,0},{0,71},{1,2},{2,1},{3,4},{4... | collective-permute-start | bytes 1572872 | tf_op jit(solution)/shard_map/ppermute | solution.py:15
  106.2 39.8 %collective-permute-start.27 = (bf16[4,256,256]{2,1,0:T(8,128)(2,1)S(1)}, bf16[4,256,256]{2,1,0:T(8,128)(2,1)S(1)}, u32[]{:S(2)}, u32[]{:S(2)}) collective-permute-start(bf16[4,256,256]{2,1,0:T(8,128)(2,1)S(1)} %inner.13), channel_id=1, source_target_pairs={{67,66},{68,69},{69,68},{70,71},{71,70},{0,1},{1,0},{2,3},{3,2},{4... | collective-permute-start | bytes 1572872 | tf_op jit(solution)/shard_map/ppermute | solution.py:15
  108.4 43.1 %collective-permute-start.31 = (bf16[4,256,256]{2,1,0:T(8,128)(2,1)S(1)}, bf16[4,256,256]{2,1,0:T(8,128)(2,1)S(1)}, u32[]{:S(2)}, u32[]{:S(2)}) collective-permute-start(bf16[4,256,256]{2,1,0:T(8,128)(2,1)S(1)} %get-tuple-element.85.env_ref), channel_id=1, source_target_pairs={{67,379},{68,380},{69,381},{70,382},{71,383},{0,320},{1,321},{2,32... | collective-permute-start | bytes 1572872 | tf_op jit(solution)/shard_map/ppermute | solution.py:15
  109.1 43.1 %collective-permute-start.24 = (f32[64]{0:T(128)S(1)}, f32[64]{0:T(128)S(1)}, u32[]{:S(2)}, u32[]{:S(2)}) collective-permute-start(f32[64]{0:T(128)S(1)} %reshape.3.w_ref), channel_id=1, source_target_pairs={{448,65},{449,66},{450,67},{451,68},{452,69},{453,70},{454,71},{45... | collective-permute-start | bytes 776 | tf_op jit(solution)/shard_map/ppermute | solution.py:15
  151.5 55.9 %collective-permute-start.37 = (bf16[4,256,256]{2,1,0:T(8,128)(2,1)S(1)}, bf16[4,256,256]{2,1,0:T(8,128)(2,1)S(1)}, u32[]{:S(2)}, u32[]{:S(2)}) collective-permute-start(bf16[4,256,256]{2,1,0:T(8,128)(2,1)S(1)} %get-tuple-element.59.env_ref), channel_id=1, source_target_pairs={{71,64},{0,65},{1,66},{2,67},{3,68},{4,69},{5,70},{6,71},{7,72},{8... | collective-permute-start | bytes 1572872 | tf_op jit(solution)/shard_map/ppermute | solution.py:15
  155.1 52.4 %collective-permute-start.38 = (bf16[4,256,256]{2,1,0:T(8,128)(2,1)S(1)}, bf16[4,256,256]{2,1,0:T(8,128)(2,1)S(1)}, u32[]{:S(2)}, u32[]{:S(2)}) collective-permute-start(bf16[4,256,256]{2,1,0:T(8,128)(2,1)S(1)} %get-tuple-element.98.env_ref), channel_id=1, source_target_pairs={{65,448},{66,449},{67,450},{68,451},{69,452},{70,453},{71,454},{0,... | collective-permute-start | bytes 1572872 | tf_op jit(solution)/shard_map/ppermute | solution.py:15
  160.1 68.2 %collective-permute-start.36 = (bf16[4,256,256]{2,1,0:T(8,128)(2,1)S(1)}, bf16[4,256,256]{2,1,0:T(8,128)(2,1)S(1)}, u32[]{:S(2)}, u32[]{:S(2)}) collective-permute-start(bf16[4,256,256]{2,1,0:T(8,128)(2,1)S(1)} %last.1), channel_id=1, source_target_pairs={{64,0},{65,1},{66,2},{67,3},{68,4},{69,5},{70,6},{71,7},{0,8},{1,9... | collective-permute-start | bytes 1572872 | tf_op jit(solution)/shard_map/ppermute | solution.py:15
  (21 other events, 110.9 us)

commit v4 on v3

--- a/solution.py
+++ b/solution.py
@@ -8,6 +8,7 @@
 from jax.sharding import PartitionSpec as P
 
 AXES = ("site", "sector")
+ROUND = (8, 7)
 
 
 def moved(x, pairs, sectors):
@@ -61,18 +62,19 @@
         out_ref[v] = total.astype(jnp.bfloat16)
 
 
-def inner_kernel(p_ref, w_ref, env_ref, a_ref, out_ref, *work):
-    one_unit(env_ref, a_ref, listed(w_ref), 3 - p_ref[0], *work, out_ref)
+def moving_parts(edge, weight, env_ref, a_ref, edge_ref, inner_ref, *work):
+    one_unit(env_ref, a_ref, weight, edge, *work[:2], edge_ref)
+    one_unit(env_ref, a_ref, weight, 3 - edge, *work[2:], inner_ref)
 
 
 def first_kernel(
-    p_ref, operator_ref, mask_ref, couple_ref, env_any, a_any, edge_ref, env_ref, a_ref, mixed_ref, half_ref, sems
+    p_ref, operator_ref, mask_ref, couple_ref, env_any, a_any, edge_ref, inner_ref, env_ref, a_ref, sems, *work
 ):
     size = env_ref.shape[-1]
-    edge = p_ref[0]
-    rows = pl.ds(pl.multiple_of(edge * size, size), size)
     copies = [pltpu.make_async_copy(env_any.at[w], env_ref.at[w], sems.at[w]) for w in range(4)]
-    copies.append(pltpu.make_async_copy(a_any.at[rows], a_ref.at[rows], sems.at[4]))
+    for i, p in enumerate((0, 3)):
+        rows = pl.ds(p * size, size)
+        copies.append(pltpu.make_async_copy(a_any.at[rows], a_ref.at[rows], sems.at[4 + i]))
     for copy in copies:
         copy.start()
     for copy in copies:
@@ -82,7 +84,7 @@
         scale = operator_ref[w, v, p] * mask_ref[w, v, p].astype(jnp.float32)
         return scale * couple_ref[p].astype(jnp.float32)
 
-    one_unit(env_ref, a_ref, weight, edge, mixed_ref, half_ref, edge_ref)
+    moving_parts(p_ref[0], weight, env_ref, a_ref, edge_ref, inner_ref, *work)
 
 
 def summed(fresh, cross_ref, swap_ref, stay_ref, env_ref):
@@ -107,25 +109,15 @@
         add((swap_ref, stay_ref, cross_ref))
 
 
-def lead_kernel(p_ref, w_ref, cross_ref, swap_ref, stay_ref, a_ref, env_ref, edge_ref, *work):
+def lead_kernel(
+    p_ref, w_ref, cross_ref, swap_ref, stay_ref, a_ref, env_ref, edge_ref, inner_ref, *work
+):
     summed(p_ref[1], cross_ref, swap_ref, stay_ref, env_ref)
-    one_unit(env_ref, a_ref, listed(w_ref), p_ref[0], *work, edge_ref)
-
-
-def last_kernel(count, p_ref, cross_ref, swap_ref, stay_ref, *refs):
-    out_ref, sem = refs[count], refs[count + 1]
-
-    @pl.when(p_ref[0] == 0)
-    def _():
-        summed(p_ref[1], cross_ref, swap_ref, stay_ref, out_ref)
-
-    for i in range(count):
-
-        @pl.when(p_ref[0] == i + 1)
-        def _():
-            copy = pltpu.make_async_copy(refs[i], out_ref, sem)
-            copy.start()
-            copy.wait()
+    moving_parts(p_ref[0], listed(w_ref), env_ref, a_ref, edge_ref, inner_ref, *work)
+
+
+def last_kernel(p_ref, cross_ref, swap_ref, stay_ref, out_ref):
+    summed(p_ref[0], cross_ref, swap_ref, stay_ref, out_ref)
 
 
 def pick_kernel(count, p_ref, *refs):
@@ -182,22 +174,24 @@
     def straight_pairs(s):
         return [((s, t), device(t - s)) for t in range(sectors)]
 
-    early = min(2, sites)
-    parcels = {s: moved(blocks, straight_pairs(s), sectors) for s in range(1, early)}
-    parcels[0], scales = blocks, {0: weights}
-    turned = moved(
-        blocks,
-        [((s, t), (s, (t - s) % sectors)) for s in range(early, sites) for t in range(sectors)],
-        sectors,
-    )
+    parcels = {0: blocks, 1: moved(blocks, straight_pairs(1), sectors)}
+    scales = {0: weights, 1: moved(weights, straight_pairs(1), sectors)}
+
+    def pack(after):
+        held, lying, after = lax.optimization_barrier((weights, blocks, after))
+        high = lax.reduce_precision(held, *ROUND)
+        middle = lax.reduce_precision(held - high, *ROUND)
+        low = lax.reduce_precision(held - high - middle, *ROUND)
+        pieces = jnp.stack([high, middle, low]).astype(jnp.bfloat16)
+        pieces = jnp.pad(pieces, ((0, 13), (0, size - pieces.shape[1])))
+        return jnp.concatenate([lying, pieces], axis=0), after
+
+    def weights_of(parcel):
+        parts = parcel[states * size : states * size + 3, : weights.shape[0]].astype(jnp.float32)
+        return parts[0] + parts[1] + parts[2]
 
     def fetch(s, after):
-        held, after = lax.optimization_barrier((turned, after))
-        pairs = [((s, (t - s) % sectors), device(t - s)) for t in range(sectors)]
-        return moved(held, pairs, sectors), after
-
-    def fetch_weights(s, after):
-        held, after = lax.optimization_barrier((weights, after))
+        held, after = lax.optimization_barrier((packed, after))
         return moved(held, straight_pairs(s), sectors), after
 
     def part_pairs(s, crossing):
@@ -211,53 +205,43 @@
         return pairs
 
     current = start_env[0]
-    kept, raised, direct = {}, {}, {}
+    homed = {}
     work = scratch(4, channels, size)
-    late = sites - 1
     for s in range(sites):
         control = jnp.stack([3 * odd, fresh_of(s - 1)])
         if s == 0:
-            edge = pl.pallas_call(
+            edge, inner = pl.pallas_call(
                 first_kernel,
-                out_shape=block_shape,
+                out_shape=(block_shape,) * 2,
                 in_specs=[SMEM] * 4 + [HBM] * 2,
-                out_specs=VMEM,
+                out_specs=(VMEM,) * 2,
                 scratch_shapes=[
                     pltpu.VMEM((channels, size, size), jnp.bfloat16),
                     pltpu.VMEM((states * size, size), jnp.bfloat16),
+                    pltpu.SemaphoreType.DMA((6,)),
                 ]
-                + work[:2]
-                + [pltpu.SemaphoreType.DMA((5,))],
+                + work,
                 compiler_params=WHOLE,
-                cost_estimate=cost(1, 4),
+                cost_estimate=cost(2, 4),
                 name="first",
             )(control, operators[0], op_mask[0], coupling[0, 0], current, blocks)
         else:
-            current, edge = pl.pallas_call(
+            if s > 1:
+                scales[s] = weights_of(parcels[s])
+            current, edge, inner = pl.pallas_call(
                 lead_kernel,
-                out_shape=(block_shape,) * 2,
+                out_shape=(block_shape,) * 3,
                 in_specs=[SMEM, SMEM] + [VMEM] * 4,
-                out_specs=(VMEM,) * 2,
-                scratch_shapes=work[:2],
+                out_specs=(VMEM,) * 3,
+                scratch_shapes=work,
                 compiler_params=PARAMS,
-                cost_estimate=cost(1, 6),
+                cost_estimate=cost(2, 6),
                 name="lead",
             )(control, scales[s], cross, swap, stay, parcels[s])
-            kept[s] = current
         cross = moved(edge, part_pairs(s, True), sectors)
         source = current
         if s == 0:
             source, _ = lax.optimization_barrier((current, edge))
-        inner = pl.pallas_call(
-            inner_kernel,
-            out_shape=block_shape,
-            in_specs=[SMEM, SMEM, VMEM, VMEM],
-            out_specs=VMEM,
-            scratch_shapes=work[:2],
-            compiler_params=PARAMS,
-            cost_estimate=cost(1, 4),
-            name="inner",
-        )(control, scales[s], source, parcels[s])
         swap = moved(inner, part_pairs(s, False), sectors)
         stay = pl.pallas_call(
             stay_kernel,
@@ -269,56 +253,33 @@
             cost_estimate=cost(40, 4),
             name="stay",
         )(scales[s], source, parcels[s])
-        if s in (1, late):
-            direct[s] = moved(kept[s], [(device(t - s), (s, t)) for t in range(sectors)], sectors)
-        elif s:
-            raised[s] = moved(
-                kept[s],
-                [(device(t - s), (s, (t - s) % sectors)) for t in range(sectors)],
-                sectors,
-            )
-        if s - 1 in raised and s < late:
-            stay, raised[s - 1] = lax.optimization_barrier((stay, raised[s - 1]))
         if s == 0:
-            scales[1], swap = fetch_weights(1, swap)
+            packed, scales[1] = pack(scales[1])
+        else:
+            homed[s] = moved(current, [(device(t - s), (s, t)) for t in range(sectors)], sectors)
+        if 2 <= s < sites - 1:
+            stay, homed[s - 1] = lax.optimization_barrier((stay, homed[s - 1]))
         if s + 2 < sites:
             parcels[s + 2], stay = fetch(s + 2, stay)
-            scales[s + 2], stay = fetch_weights(s + 2, stay)
-
-    resting = [raised[r] for r in range(2, late)]
+
     ended = pl.pallas_call(
-        functools.partial(last_kernel, len(resting)),
+        last_kernel,
         out_shape=block_shape,
-        in_specs=[SMEM] + [VMEM] * 3 + [ANY] * len(resting),
+        in_specs=[SMEM] + [VMEM] * 3,
         out_specs=VMEM,
-        scratch_shapes=[pltpu.SemaphoreType.DMA],
         compiler_params=PARAMS,
         name="last",
-    )(
-        jnp.stack([jnp.maximum(row - 1, 0), fresh_of(sites - 1)]),
-        cross,
-        swap,
-        stay,
-        *resting,
-    )
-    pairs = [(device(t - sites), (0, t)) for t in range(sectors)]
-    for r in range(2, late):
-        pairs += [((r, (t - r) % sectors), (r, t)) for t in range(sectors)]
-    home = moved(ended, pairs, sectors)
+    )(fresh_of(sites - 1)[None], cross, swap, stay)
+    homed[0] = moved(ended, [(device(t - sites), (0, t)) for t in range(sectors)], sectors)
     out = pl.pallas_call(
-        functools.partial(pick_kernel, 3),
+        functools.partial(pick_kernel, sites),
         out_shape=block_shape,
-        in_specs=[SMEM, VMEM, ANY, ANY],
+        in_specs=[SMEM, VMEM] + [ANY] * (sites - 1),
         out_specs=VMEM,
         scratch_shapes=[pltpu.SemaphoreType.DMA],
         compiler_params=PARAMS,
         name="pick",
-    )(
-        jnp.stack([jnp.where(row == 1, 1, jnp.where(row == late, 2, 0))]),
-        home,
-        direct[1],
-        direct[late],
-    )
+    )(row[None], *[homed[r] for r in range(sites)])
     return out[None, None]
 
 

time: 230 us -> 209 us (0.909)
  the two profiles are of different devices: /device:TPU:25 before, /device:TPU:7 now
where the time goes in v4:
time: 209 us; the launch traced here: 208 us
  waiting for transfers between devices  118 us (56%)
  starting transfers between devices  55 us (26%)
  Pallas kernels  29.8 us (14%)
  other arithmetic  2.68 us (1%)
    ppermute x32, waiting for transfers between devices, moved(): return lax.ppermute(x, AXES, flat)  118 us
    ppermute x32, starting transfers between devices, moved(): return lax.ppermute(x, AXES, flat)  55 us
    pallas_call x8, Pallas kernels, local(): pl.pallas_call(stay_kernel, out_shape=block_shape, in_specs=[SMEM, VMEM,...  12.3 us
    pallas_call x7, Pallas kernels, local(): pl.pallas_call(lead_kernel, out_shape=(block_shape,) * 3, in_specs=[SMEM,...  12.3 us
  transfers between devices with their start and end apart: 32, of which 14 were waited for; matrix products, arithmetic and copies ran while one was open for 1% of the time, Pallas kernels for 14%

profile of v4, /device:TPU:7, one launch (start us, length us, event | category | flops | bytes accessed | tf_op | source)
XLA Modules:
  0.0 207.7 jit_solution(9362248171752569213)
XLA Ops:
  4.9 4.1 %first.1 = (bf16[4,256,256]{2,1,0:T(8,128)(2,1)}, bf16[4,256,256]{2,1,0:T(8,128)(2,1)}) custom-call(s32[2]{0:T(128)} %pad_add_fusion.2.p_ref, f32[4,4,4]{2,1,0:T(4,128)} %bitcast.48, s32[4,4,4]{2,1,0:T(4,128)} %bitcast.47, s32[4]{0:T(128)} %bitcast.49, bf16[4,256,256]{2,1,0:T(8,128)(2,1)} %bitcast.45, bf16[1024,256]{1,0:T(8,128)(2,1)} %bitcast.42), custom_call_target="tpu_custom_call" | custom-call | flops 536870912 | bytes 2097152 | tf_op jit(solution)/shard_map/first/pallas_call | solution.py:213
  9.0 4.5 %collective-permute-start.1 = (bf16[4,256,256]{2,1,0:T(8,128)(2,1)}, bf16[4,256,256]{2,1,0:T(8,128)(2,1)S(1)}, u32[]{:S(2)}, u32[]{:S(2)}) collective-permute-start(bf16[4,256,256]{2,1,0:T(8,128)(2,1)} %get-tuple-element.57), channel_id=1, source_target_pairs={{0,71},{1,2},{2,1},{3,4},{4,3},{5,6},{6,5},{7,8},{8,7},{9,10},{10,... | collective-permute-start | bytes 1572872 | tf_op jit(solution)/shard_map/ppermute | solution.py:16
  19.9 4.9 %collective-permute-done.1.cross_ref = bf16[4,256,256]{2,1,0:T(8,128)(2,1)S(1)} collective-permute-done((bf16[4,256,256]{2,1,0:T(8,128)(2,1)}, bf16[4,256,256]{2,1,0:T(8,128)(2,1)S(1)}, u32[]{:S(2)}, u32[]{:S(2)}) %collective-permute-start.1) | collective-permute-done | bytes 524320 | tf_op jit(solution)/shard_map/ppermute | solution.py:16
  26.6 1.9 collective-permute-start.6
  28.5 1.9 collective-permute-start.7
  34.6 3.0 %collective-permute-done.5.a_ref = bf16[1040,256]{1,0:T(8,128)(2,1)S(1)} collective-permute-done((bf16[1040,256]{1,0:T(8,128)(2,1)S(1)}, bf16[1040,256]{1,0:T(8,128)(2,1)S(1)}, u32[]{:S(2)}, u32[]{:S(2)}) %collective-permute-start.5) | collective-permute-done | bytes 532512 | tf_op jit(solution)/shard_map/ppermute | solution.py:16
  37.6 19.7 %collective-permute-done.6.cross_ref = bf16[4,256,256]{2,1,0:T(8,128)(2,1)S(1)} collective-permute-done((bf16[4,256,256]{2,1,0:T(8,128)(2,1)S(1)}, bf16[4,256,256]{2,1,0:T(8,128)(2,1)S(1)}, u32[]{:S(2)}, u32[]{:S(2)}) %collective-permute-start.6) | collective-permute-done | bytes 524320 | tf_op jit(solution)/shard_map/ppermute | solution.py:16
  59.0 1.9 collective-permute-start.8
  60.9 1.9 collective-permute-start.9
  67.1 4.5 %collective-permute-done.8.cross_ref = bf16[4,256,256]{2,1,0:T(8,128)(2,1)S(1)} collective-permute-done((bf16[4,256,256]{2,1,0:T(8,128)(2,1)S(1)}, bf16[4,256,256]{2,1,0:T(8,128)(2,1)S(1)}, u32[]{:S(2)}, u32[]{:S(2)}) %collective-permute-start.8) | collective-permute-done | bytes 524320 | tf_op jit(solution)/shard_map/ppermute | solution.py:16
  73.4 1.9 collective-permute-start.14
  75.3 1.9 collective-permute-start.15
  81.4 8.6 %collective-permute-done.13.a_ref = bf16[1040,256]{1,0:T(8,128)(2,1)S(1)} collective-permute-done((bf16[1040,256]{1,0:T(8,128)(2,1)S(1)}, bf16[1040,256]{1,0:T(8,128)(2,1)S(1)}, u32[]{:S(2)}, u32[]{:S(2)}) %collective-permute-start.13) | collective-permute-done | bytes 532512 | tf_op jit(solution)/shard_map/ppermute | solution.py:16
  90.1 14.9 %collective-permute-done.14.cross_ref = bf16[4,256,256]{2,1,0:T(8,128)(2,1)S(1)} collective-permute-done((bf16[4,256,256]{2,1,0:T(8,128)(2,1)S(1)}, bf16[4,256,256]{2,1,0:T(8,128)(2,1)S(1)}, u32[]{:S(2)}, u32[]{:S(2)}) %collective-permute-start.14) | collective-permute-done | bytes 524320 | tf_op jit(solution)/shard_map/ppermute | solution.py:16
  115.0 16.2 %collective-permute-done.16.cross_ref = bf16[4,256,256]{2,1,0:T(8,128)(2,1)S(1)} collective-permute-done((bf16[4,256,256]{2,1,0:T(8,128)(2,1)S(1)}, bf16[4,256,256]{2,1,0:T(8,128)(2,1)S(1)}, u32[]{:S(2)}, u32[]{:S(2)}) %collective-permute-start.16) | collective-permute-done | bytes 524320 | tf_op jit(solution)/shard_map/ppermute | solution.py:16
  133.0 1.9 collective-permute-start.22
  141.0 4.5 %collective-permute-done.22.cross_ref = bf16[4,256,256]{2,1,0:T(8,128)(2,1)S(1)} collective-permute-done((bf16[4,256,256]{2,1,0:T(8,128)(2,1)S(1)}, bf16[4,256,256]{2,1,0:T(8,128)(2,1)S(1)}, u32[]{:S(2)}, u32[]{:S(2)}) %collective-permute-start.22) | collective-permute-done | bytes 524320 | tf_op jit(solution)/shard_map/ppermute | solution.py:16
  147.3 1.9 collective-permute-start.24
  154.0 6.3 %collective-permute-done.26.refs_5_ = bf16[4,256,256]{2,1,0:T(8,128)(2,1)S(1)} collective-permute-done((bf16[4,256,256]{2,1,0:T(8,128)(2,1)S(1)}, bf16[4,256,256]{2,1,0:T(8,128)(2,1)S(1)}, u32[]{:S(2)}, u32[]{:S(2)}) %collective-permute-start.26) | collective-permute-done | bytes 524320 | tf_op jit(solution)/shard_map/ppermute | solution.py:16
  160.3 3.8 %collective-permute-done.24.cross_ref = bf16[4,256,256]{2,1,0:T(8,128)(2,1)S(1)} collective-permute-done((bf16[4,256,256]{2,1,0:T(8,128)(2,1)S(1)}, bf16[4,256,256]{2,1,0:T(8,128)(2,1)S(1)}, u32[]{:S(2)}, u32[]{:S(2)}) %collective-permute-start.24) | collective-permute-done | bytes 524320 | tf_op jit(solution)/shard_map/ppermute | solution.py:16
  165.9 2.2 %collective-permute-start.27 = (bf16[4,256,256]{2,1,0:T(8,128)(2,1)S(1)}, bf16[4,256,256]{2,1,0:T(8,128)(2,1)S(1)}, u32[]{:S(2)}, u32[]{:S(2)}) collective-permute-start(bf16[4,256,256]{2,1,0:T(8,128)(2,1)S(1)} %get-tuple-element.95), channel_id=1, source_target_pairs={{65,66},{66,65},{67,68},{68,67},{69,70},{70,69},{71,0},{0,71},{1,2... | collective-permute-start | bytes 1572872 | tf_op jit(solution)/shard_map/ppermute | solution.py:16
  172.9 5.6 %collective-permute-done.27.cross_ref = bf16[4,256,256]{2,1,0:T(8,128)(2,1)S(1)} collective-permute-done((bf16[4,256,256]{2,1,0:T(8,128)(2,1)S(1)}, bf16[4,256,256]{2,1,0:T(8,128)(2,1)S(1)}, u32[]{:S(2)}, u32[]{:S(2)}) %collective-permute-start.27) | collective-permute-done | bytes 524320 | tf_op jit(solution)/shard_map/ppermute | solution.py:16
  180.6 3.8 %collective-permute-done.30.refs_6_ = bf16[4,256,256]{2,1,0:T(8,128)(2,1)S(1)} collective-permute-done((bf16[4,256,256]{2,1,0:T(8,128)(2,1)S(1)}, bf16[4,256,256]{2,1,0:T(8,128)(2,1)S(1)}, u32[]{:S(2)}, u32[]{:S(2)}) %collective-permute-start.30) | collective-permute-done | bytes 524320 | tf_op jit(solution)/shard_map/ppermute | solution.py:16
  184.4 20.9 %collective-permute-done.31.refs_7_ = bf16[4,256,256]{2,1,0:T(8,128)(2,1)S(1)} collective-permute-done((bf16[4,256,256]{2,1,0:T(8,128)(2,1)S(1)}, bf16[4,256,256]{2,1,0:T(8,128)(2,1)S(1)}, u32[]{:S(2)}, u32[]{:S(2)}) %collective-permute-start.31) | collective-permute-done | bytes 524320 | tf_op jit(solution)/shard_map/ppermute | solution.py:16
  (89 shorter events, 64.0 us)
Async XLA Ops:
  1.6 17.0 %collective-permute-start = (f32[64]{0:T(128)S(1)}, f32[64]{0:T(128)S(1)}, u32[]{:S(2)}, u32[]{:S(2)}) collective-permute-start(f32[64]{0:T(128)S(1)} %reshape.15.w_ref), channel_id=1, source_target_pairs={{64,71},{65,0},{66,1},{67,2},{68,3},{69,4},{70,5},{71,6},{72,7},{7... | collective-permute-start | bytes 776 | tf_op jit(solution)/shard_map/ppermute | solution.py:16
  2.9 22.0 %collective-permute-start.3 = (bf16[1024,256]{1,0:T(8,128)(2,1)}, bf16[1024,256]{1,0:T(8,128)(2,1)S(1)}, u32[]{:S(2)}, u32[]{:S(2)}) collective-permute-start(bf16[1024,256]{1,0:T(8,128)(2,1)} %bitcast.41), channel_id=1, source_target_pairs={{64,71},{65,0},{66,1},{67,2},{68,3},{69,4},{70,5},{71,6},{72,7},{7... | collective-permute-start | bytes 1572872 | tf_op jit(solution)/shard_map/ppermute | solution.py:16
  9.0 15.9 %collective-permute-start.1 = (bf16[4,256,256]{2,1,0:T(8,128)(2,1)}, bf16[4,256,256]{2,1,0:T(8,128)(2,1)S(1)}, u32[]{:S(2)}, u32[]{:S(2)}) collective-permute-start(bf16[4,256,256]{2,1,0:T(8,128)(2,1)} %get-tuple-element.57), channel_id=1, source_target_pairs={{0,71},{1,2},{2,1},{3,4},{4,3},{5,6},{6,5},{7,8},{8,7},{9,10},{10,... | collective-permute-start | bytes 1572872 | tf_op jit(solution)/shard_map/ppermute | solution.py:16
  18.6 19.0 %collective-permute-start.5 = (bf16[1040,256]{1,0:T(8,128)(2,1)S(1)}, bf16[1040,256]{1,0:T(8,128)(2,1)S(1)}, u32[]{:S(2)}, u32[]{:S(2)}) collective-permute-start(bf16[1040,256]{1,0:T(8,128)(2,1)S(1)} %pad_maximum_fusion), channel_id=1, source_target_pairs={{128,70},{129,71},{130,0},{131,1},{132,2},{133,3},{134,4},{135,5},... | collective-permute-start | bytes 1597448 | tf_op jit(solution)/shard_map/ppermute | solution.py:16
  26.6 30.7 %collective-permute-start.6 = (bf16[4,256,256]{2,1,0:T(8,128)(2,1)S(1)}, bf16[4,256,256]{2,1,0:T(8,128)(2,1)S(1)}, u32[]{:S(2)}, u32[]{:S(2)}) collective-permute-start(bf16[4,256,256]{2,1,0:T(8,128)(2,1)S(1)} %get-tuple-element.64), channel_id=1, source_target_pairs={{71,0},{0,71},{1,2},{2,1},{3,4},{4,3},{5,6},{6,5},{7,8},{8,7},{9,1... | collective-permute-start | bytes 1572872 | tf_op jit(solution)/shard_map/ppermute | solution.py:16
  28.5 28.8 %collective-permute-start.7 = (bf16[4,256,256]{2,1,0:T(8,128)(2,1)S(1)}, bf16[4,256,256]{2,1,0:T(8,128)(2,1)S(1)}, u32[]{:S(2)}, u32[]{:S(2)}) collective-permute-start(bf16[4,256,256]{2,1,0:T(8,128)(2,1)S(1)} %get-tuple-element.65), channel_id=1, source_target_pairs={{71,70},{0,1},{1,0},{2,3},{3,2},{4,5},{5,4},{6,7},{7,6},{8,9},{9,8... | collective-permute-start | bytes 1572872 | tf_op jit(solution)/shard_map/ppermute | solution.py:16
  30.4 35.3 %collective-permute-start.10 = (bf16[4,256,256]{2,1,0:T(8,128)(2,1)S(1)}, bf16[4,256,256]{2,1,0:T(8,128)(2,1)S(1)}, u32[]{:S(2)}, u32[]{:S(2)}) collective-permute-start(bf16[4,256,256]{2,1,0:T(8,128)(2,1)S(1)} %get-tuple-element.61.env_ref), channel_id=1, source_target_pairs={{71,64},{0,65},{1,66},{2,67},{3,68},{4,69},{5,70},{6,71},{7,72},{8... | collective-permute-start | bytes 1572872 | tf_op jit(solution)/shard_map/ppermute | solution.py:16
  33.3 33.7 %collective-permute-start.4 = (bf16[1040,256]{1,0:T(8,128)(2,1)S(1)}, bf16[1040,256]{1,0:T(8,128)(2,1)S(1)}, u32[]{:S(2)}, u32[]{:S(2)}) collective-permute-start(bf16[1040,256]{1,0:T(8,128)(2,1)S(1)} %pad_maximum_fusion), channel_id=1, source_target_pairs={{192,69},{193,70},{194,71},{195,0},{196,1},{197,2},{198,3},{199,4}... | collective-permute-start | bytes 1597448 | tf_op jit(solution)/shard_map/ppermute | solution.py:16
  62.9 17.2 %collective-permute-start.11 = (bf16[4,256,256]{2,1,0:T(8,128)(2,1)S(1)}, bf16[4,256,256]{2,1,0:T(8,128)(2,1)S(1)}, u32[]{:S(2)}, u32[]{:S(2)}) collective-permute-start(bf16[4,256,256]{2,1,0:T(8,128)(2,1)S(1)} %get-tuple-element.69.env_ref), channel_id=1, source_target_pairs={{70,128},{71,129},{0,130},{1,131},{2,132},{3,133},{4,134},{5,135},... | collective-permute-start | bytes 1572872 | tf_op jit(solution)/shard_map/ppermute | solution.py:16
  65.8 24.3 %collective-permute-start.13 = (bf16[1040,256]{1,0:T(8,128)(2,1)S(1)}, bf16[1040,256]{1,0:T(8,128)(2,1)S(1)}, u32[]{:S(2)}, u32[]{:S(2)}) collective-permute-start(bf16[1040,256]{1,0:T(8,128)(2,1)S(1)} %pad_maximum_fusion), channel_id=1, source_target_pairs={{256,68},{257,69},{258,70},{259,71},{260,0},{261,1},{262,2},{263,3... | collective-permute-start | bytes 1597448 | tf_op jit(solution)/shard_map/ppermute | solution.py:16
  73.4 31.6 %collective-permute-start.14 = (bf16[4,256,256]{2,1,0:T(8,128)(2,1)S(1)}, bf16[4,256,256]{2,1,0:T(8,128)(2,1)S(1)}, u32[]{:S(2)}, u32[]{:S(2)}) collective-permute-start(bf16[4,256,256]{2,1,0:T(8,128)(2,1)S(1)} %get-tuple-element.76), channel_id=1, source_target_pairs={{69,70},{70,69},{71,0},{0,71},{1,2},{2,1},{3,4},{4,3},{5,6},{6,5},... | collective-permute-start | bytes 1572872 | tf_op jit(solution)/shard_map/ppermute | solution.py:16
  75.3 29.7 %collective-permute-start.15 = (bf16[4,256,256]{2,1,0:T(8,128)(2,1)S(1)}, bf16[4,256,256]{2,1,0:T(8,128)(2,1)S(1)}, u32[]{:S(2)}, u32[]{:S(2)}) collective-permute-start(bf16[4,256,256]{2,1,0:T(8,128)(2,1)S(1)} %get-tuple-element.77), channel_id=1, source_target_pairs={{69,68},{70,71},{71,70},{0,1},{1,0},{2,3},{3,2},{4,5},{5,4},{6,7},... | collective-permute-start | bytes 1572872 | tf_op jit(solution)/shard_map/ppermute | solution.py:16
  77.2 36.4 %collective-permute-start.18 = (bf16[4,256,256]{2,1,0:T(8,128)(2,1)S(1)}, bf16[4,256,256]{2,1,0:T(8,128)(2,1)S(1)}, u32[]{:S(2)}, u32[]{:S(2)}) collective-permute-start(bf16[4,256,256]{2,1,0:T(8,128)(2,1)S(1)} %get-tuple-element.72.env_ref), channel_id=1, source_target_pairs={{69,192},{70,193},{71,194},{0,195},{1,196},{2,197},{3,198},{4,199}... | collective-permute-start | bytes 1572872 | tf_op jit(solution)/shard_map/ppermute | solution.py:16
  80.1 34.8 %collective-permute-start.12 = (bf16[1040,256]{1,0:T(8,128)(2,1)S(1)}, bf16[1040,256]{1,0:T(8,128)(2,1)S(1)}, u32[]{:S(2)}, u32[]{:S(2)}) collective-permute-start(bf16[1040,256]{1,0:T(8,128)(2,1)S(1)} %pad_maximum_fusion), channel_id=1, source_target_pairs={{320,67},{321,68},{322,69},{323,70},{324,71},{325,0},{326,1},{327,... | collective-permute-start | bytes 1597448 | tf_op jit(solution)/shard_map/ppermute | solution.py:16
  106.9 24.3 %collective-permute-start.16 = (bf16[4,256,256]{2,1,0:T(8,128)(2,1)S(1)}, bf16[4,256,256]{2,1,0:T(8,128)(2,1)S(1)}, u32[]{:S(2)}, u32[]{:S(2)}) collective-permute-start(bf16[4,256,256]{2,1,0:T(8,128)(2,1)S(1)} %get-tuple-element.79), channel_id=1, source_target_pairs={{68,67},{69,70},{70,69},{71,0},{0,71},{1,2},{2,1},{3,4},{4,3},{5,6... | collective-permute-start | bytes 1572872 | tf_op jit(solution)/shard_map/ppermute | solution.py:16
  108.8 22.4 %collective-permute-start.17 = (bf16[4,256,256]{2,1,0:T(8,128)(2,1)S(1)}, bf16[4,256,256]{2,1,0:T(8,128)(2,1)S(1)}, u32[]{:S(2)}, u32[]{:S(2)}) collective-permute-start(bf16[4,256,256]{2,1,0:T(8,128)(2,1)S(1)} %get-tuple-element.80), channel_id=1, source_target_pairs={{68,69},{69,68},{70,71},{71,70},{0,1},{1,0},{2,3},{3,2},{4,5},{5,4... | collective-permute-start | bytes 1572872 | tf_op jit(solution)/shard_map/ppermute | solution.py:16
  110.8 28.9 %collective-permute-start.19 = (bf16[4,256,256]{2,1,0:T(8,128)(2,1)S(1)}, bf16[4,256,256]{2,1,0:T(8,128)(2,1)S(1)}, u32[]{:S(2)}, u32[]{:S(2)}) collective-permute-start(bf16[4,256,256]{2,1,0:T(8,128)(2,1)S(1)} %get-tuple-element.81.env_ref), channel_id=1, source_target_pairs={{68,256},{69,257},{70,258},{71,259},{0,260},{1,261},{2,262},{3,263... | collective-permute-start | bytes 1572872 | tf_op jit(solution)/shard_map/ppermute | solution.py:16
  113.6 27.4 %collective-permute-start.21 = (bf16[1040,256]{1,0:T(8,128)(2,1)S(1)}, bf16[1040,256]{1,0:T(8,128)(2,1)S(1)}, u32[]{:S(2)}, u32[]{:S(2)}) collective-permute-start(bf16[1040,256]{1,0:T(8,128)(2,1)S(1)} %pad_maximum_fusion), channel_id=1, source_target_pairs={{384,66},{385,67},{386,68},{387,69},{388,70},{389,71},{390,0},{391... | collective-permute-start | bytes 1597448 | tf_op jit(solution)/shard_map/ppermute | solution.py:16
  136.8 23.5 %collective-permute-start.26 = (bf16[4,256,256]{2,1,0:T(8,128)(2,1)S(1)}, bf16[4,256,256]{2,1,0:T(8,128)(2,1)S(1)}, u32[]{:S(2)}, u32[]{:S(2)}) collective-permute-start(bf16[4,256,256]{2,1,0:T(8,128)(2,1)S(1)} %get-tuple-element.84.env_ref), channel_id=1, source_target_pairs={{67,320},{68,321},{69,322},{70,323},{71,324},{0,325},{1,326},{2,32... | collective-permute-start | bytes 1572872 | tf_op jit(solution)/shard_map/ppermute | solution.py:16
  139.7 20.6 %collective-permute-start.20 = (bf16[1040,256]{1,0:T(8,128)(2,1)S(1)}, bf16[1040,256]{1,0:T(8,128)(2,1)S(1)}, u32[]{:S(2)}, u32[]{:S(2)}) collective-permute-start(bf16[1040,256]{1,0:T(8,128)(2,1)S(1)} %pad_maximum_fusion), channel_id=1, source_target_pairs={{448,65},{449,66},{450,67},{451,68},{452,69},{453,70},{454,71},{45... | collective-permute-start | bytes 1597448 | tf_op jit(solution)/shard_map/ppermute | solution.py:16
  147.3 16.8 %collective-permute-start.24 = (bf16[4,256,256]{2,1,0:T(8,128)(2,1)S(1)}, bf16[4,256,256]{2,1,0:T(8,128)(2,1)S(1)}, u32[]{:S(2)}, u32[]{:S(2)}) collective-permute-start(bf16[4,256,256]{2,1,0:T(8,128)(2,1)S(1)} %get-tuple-element.91), channel_id=1, source_target_pairs={{66,65},{67,68},{68,67},{69,70},{70,69},{71,0},{0,71},{1,2},{2,1},... | collective-permute-start | bytes 1572872 | tf_op jit(solution)/shard_map/ppermute | solution.py:16
  151.2 33.3 %collective-permute-start.30 = (bf16[4,256,256]{2,1,0:T(8,128)(2,1)S(1)}, bf16[4,256,256]{2,1,0:T(8,128)(2,1)S(1)}, u32[]{:S(2)}, u32[]{:S(2)}) collective-permute-start(bf16[4,256,256]{2,1,0:T(8,128)(2,1)S(1)} %get-tuple-element.93.env_ref), channel_id=1, source_target_pairs={{66,384},{67,385},{68,386},{69,387},{70,388},{71,389},{0,390},{1,3... | collective-permute-start | bytes 1572872 | tf_op jit(solution)/shard_map/ppermute | solution.py:16
  170.0 35.4 %collective-permute-start.31 = (bf16[4,256,256]{2,1,0:T(8,128)(2,1)S(1)}, bf16[4,256,256]{2,1,0:T(8,128)(2,1)S(1)}, u32[]{:S(2)}, u32[]{:S(2)}) collective-permute-start(bf16[4,256,256]{2,1,0:T(8,128)(2,1)S(1)} %get-tuple-element.97.env_ref), channel_id=1, source_target_pairs={{65,448},{66,449},{67,450},{68,451},{69,452},{70,453},{71,454},{0,... | collective-permute-start | bytes 1572872 | tf_op jit(solution)/shard_map/ppermute | solution.py:16
  178.7 28.0 %collective-permute-start.29 = (bf16[4,256,256]{2,1,0:T(8,128)(2,1)S(1)}, bf16[4,256,256]{2,1,0:T(8,128)(2,1)S(1)}, u32[]{:S(2)}, u32[]{:S(2)}) collective-permute-start(bf16[4,256,256]{2,1,0:T(8,128)(2,1)S(1)} %last.1), channel_id=1, source_target_pairs={{64,0},{65,1},{66,2},{67,3},{68,4},{69,5},{70,6},{71,7},{0,8},{1,9... | collective-permute-start | bytes 1572872 | tf_op jit(solution)/shard_map/ppermute | solution.py:16
  (10 other events, 107.5 us)

commit v5 on v4

--- a/solution.py
+++ b/solution.py
@@ -87,37 +87,25 @@
     moving_parts(p_ref[0], weight, env_ref, a_ref, edge_ref, inner_ref, *work)
 
 
-def summed(fresh, cross_ref, swap_ref, stay_ref, env_ref):
+def summed(cross_ref, swap_ref, stay_ref, env_ref):
     size = env_ref.shape[-1]
     step = 32
-
-    def add(refs):
-        for v in range(4):
-            for i in range(0, size, step):
-                at = (v, slice(i, i + step))
-                total = refs[0][at].astype(jnp.float32)
-                for ref in refs[1:]:
-                    total = total + ref[at].astype(jnp.float32)
-                env_ref[at] = total.astype(jnp.bfloat16)
-
-    @pl.when(fresh == 1)
-    def _():
-        add((swap_ref, cross_ref))
-
-    @pl.when(fresh == 0)
-    def _():
-        add((swap_ref, stay_ref, cross_ref))
+    for v in range(4):
+        for i in range(0, size, step):
+            at = (v, slice(i, i + step))
+            total = swap_ref[at].astype(jnp.float32) + stay_ref[at].astype(jnp.float32)
+            env_ref[at] = (total + cross_ref[at].astype(jnp.float32)).astype(jnp.bfloat16)
 
 
 def lead_kernel(
     p_ref, w_ref, cross_ref, swap_ref, stay_ref, a_ref, env_ref, edge_ref, inner_ref, *work
 ):
-    summed(p_ref[1], cross_ref, swap_ref, stay_ref, env_ref)
+    summed(cross_ref, swap_ref, stay_ref, env_ref)
     moving_parts(p_ref[0], listed(w_ref), env_ref, a_ref, edge_ref, inner_ref, *work)
 
 
-def last_kernel(p_ref, cross_ref, swap_ref, stay_ref, out_ref):
-    summed(p_ref[0], cross_ref, swap_ref, stay_ref, out_ref)
+def last_kernel(cross_ref, swap_ref, stay_ref, out_ref):
+    summed(cross_ref, swap_ref, stay_ref, out_ref)
 
 
 def pick_kernel(count, p_ref, *refs):
@@ -162,20 +150,21 @@
     def device(position):
         return (0, position) if position >= 0 else (1, position + sites)
 
-    def fresh_of(s):
-        position = jnp.where(row == 1, place - sites, place)
-        return (position + s < 0).astype(jnp.int32)
-
     coupled = coupling[0, 0].astype(jnp.float32)
     weights = operators[0] * op_mask[0].astype(jnp.float32) * coupled[None, None, :]
     weights = weights.transpose(2, 1, 0).reshape(-1)
+    rooted = jnp.where(row == 0, weights, 0.0)
     blocks = site_blocks[0, 0].reshape(states * size, size)
 
     def straight_pairs(s):
         return [((s, t), device(t - s)) for t in range(sectors)]
 
+    def turn_pairs(s):
+        return [((s, t), (s, (t - s) % sectors)) for t in range(sectors)]
+
     parcels = {0: blocks, 1: moved(blocks, straight_pairs(1), sectors)}
-    scales = {0: weights, 1: moved(weights, straight_pairs(1), sectors)}
+    scales = {0: rooted, 1: moved(weights, straight_pairs(1), sectors)}
+    turned = {2: moved(blocks, turn_pairs(2), sectors)}
 
     def pack(after):
         held, lying, after = lax.optimization_barrier((weights, blocks, after))
@@ -191,24 +180,24 @@
         return parts[0] + parts[1] + parts[2]
 
     def fetch(s, after):
-        held, after = lax.optimization_barrier((packed, after))
-        return moved(held, straight_pairs(s), sectors), after
-
-    def part_pairs(s, crossing):
+        held, after = lax.optimization_barrier((turned[s], after))
+        pairs = [((s, (t - s) % sectors), device(t - s)) for t in range(sectors)]
+        return moved(held, pairs, sectors), after
+
+    def part_pairs(crossing):
         pairs = []
-        for t in range(sectors):
-            at = t - s
-            if (at % 2 == 0) == crossing:
-                pairs.append((device(at), device(at - 1)))
-            elif t + 2 < sectors:
-                pairs.append((device(at), device(at + 1)))
+        for at in range(-sites, sectors):
+            to = at - 1 if (at % 2 == 0) == crossing else at + 1
+            if -sites <= to < sectors:
+                pairs.append((device(at), device(to)))
         return pairs
 
+    control = jnp.stack([3 * odd])
+    began = jnp.where(row == 0, coupling[0, 0], 0)
     current = start_env[0]
-    homed = {}
+    homed, raised = {}, {}
     work = scratch(4, channels, size)
     for s in range(sites):
-        control = jnp.stack([3 * odd, fresh_of(s - 1)])
         if s == 0:
             edge, inner = pl.pallas_call(
                 first_kernel,
@@ -224,9 +213,9 @@
                 compiler_params=WHOLE,
                 cost_estimate=cost(2, 4),
                 name="first",
-            )(control, operators[0], op_mask[0], coupling[0, 0], current, blocks)
+            )(control, operators[0], op_mask[0], began, current, blocks)
         else:
-            if s > 1:
+            if s not in scales:
                 scales[s] = weights_of(parcels[s])
             current, edge, inner = pl.pallas_call(
                 lead_kernel,
@@ -238,11 +227,11 @@
                 cost_estimate=cost(2, 6),
                 name="lead",
             )(control, scales[s], cross, swap, stay, parcels[s])
-        cross = moved(edge, part_pairs(s, True), sectors)
+        cross = moved(edge, part_pairs(True), sectors)
         source = current
         if s == 0:
             source, _ = lax.optimization_barrier((current, edge))
-        swap = moved(inner, part_pairs(s, False), sectors)
+        swap = moved(inner, part_pairs(False), sectors)
         stay = pl.pallas_call(
             stay_kernel,
             out_shape=block_shape,
@@ -255,21 +244,31 @@
         )(scales[s], source, parcels[s])
         if s == 0:
             packed, scales[1] = pack(scales[1])
+            for r in range(3, sites):
+                turned[r] = moved(packed, turn_pairs(r), sectors)
+            scales[2] = moved(weights, straight_pairs(2), sectors)
+        elif s < sites - 2:
+            pairs = [(device(t - s), (s, (t - s) % sectors)) for t in range(sectors)]
+            raised[s] = moved(current, pairs, sectors)
         else:
             homed[s] = moved(current, [(device(t - s), (s, t)) for t in range(sectors)], sectors)
-        if 2 <= s < sites - 1:
-            stay, homed[s - 1] = lax.optimization_barrier((stay, homed[s - 1]))
+        if s - 2 in homed and s < sites - 1:
+            stay, homed[s - 2] = lax.optimization_barrier((stay, homed[s - 2]))
+        if s - 1 in raised:
+            stay, risen = lax.optimization_barrier((stay, raised[s - 1]))
+            pairs = [((s - 1, (t - s + 1) % sectors), (s - 1, t)) for t in range(sectors)]
+            homed[s - 1] = moved(risen, pairs, sectors)
         if s + 2 < sites:
             parcels[s + 2], stay = fetch(s + 2, stay)
 
     ended = pl.pallas_call(
         last_kernel,
         out_shape=block_shape,
-        in_specs=[SMEM] + [VMEM] * 3,
+        in_specs=[VMEM] * 3,
         out_specs=VMEM,
         compiler_params=PARAMS,
         name="last",
-    )(fresh_of(sites - 1)[None], cross, swap, stay)
+    )(cross, swap, stay)
     homed[0] = moved(ended, [(device(t - sites), (0, t)) for t in range(sectors)], sectors)
     out = pl.pallas_call(
         functools.partial(pick_kernel, sites),

time: 209 us -> 210 us (level)
  starting transfers between devices: 55 us -> 103 us
  waiting for transfers between devices: 118 us -> 71.9 us
    ppermute x32 -> x44, starting transfers between devices: 55 us -> 103 us  [moved(): return lax.ppermute(x, AXES, flat)]
    ppermute x32 -> x44, waiting for transfers between devices: 118 us -> 71.9 us  [moved(): return lax.ppermute(x, AXES, flat)]
  transfers between devices with their start and end apart: 32 -> 44, of which waited for: 14 -> 13; matrix products, arithmetic and copies ran while one was open for 1% -> 1% of each run, Pallas kernels for 14% -> 14%
where the time goes in v5:
time: 210 us; the launch traced here: 209 us
  starting transfers between devices  103 us (49%)
  waiting for transfers between devices  71.9 us (34%)
  Pallas kernels  29.7 us (14%)
  other arithmetic  2.15 us (1%)
    ppermute x44, starting transfers between devices, moved(): return lax.ppermute(x, AXES, flat)  103 us
    ppermute x44, waiting for transfers between devices, moved(): return lax.ppermute(x, AXES, flat)  71.9 us
    pallas_call x8, Pallas kernels, local(): pl.pallas_call(stay_kernel, out_shape=block_shape, in_specs=[SMEM, VMEM,...  12.3 us
    pallas_call x7, Pallas kernels, local(): pl.pallas_call(lead_kernel, out_shape=(block_shape,) * 3, in_specs=[SMEM,...  12.2 us
  transfers between devices with their start and end apart: 44, of which 13 were waited for; matrix products, arithmetic and copies ran while one was open for 1% of the time, Pallas kernels for 14%

profile of v5, /device:TPU:7, one launch (start us, length us, event | category | flops | bytes accessed | tf_op | source)
XLA Modules:
  0.0 209.1 jit_solution(2733913085561433690)
XLA Ops:
  7.6 4.1 %first.1 = (bf16[4,256,256]{2,1,0:T(8,128)(2,1)}, bf16[4,256,256]{2,1,0:T(8,128)(2,1)}) custom-call(s32[1]{0:T(128)} %bitcast.1.p_ref, f32[4,4,4]{2,1,0:T(4,128)} %bitcast.39, s32[4,4,4]{2,1,0:T(4,128)} %bitcast.38, s32[4]{0:T(128)} %get-tuple-element.119.couple_ref, bf16[4,256,256]{2,1,0:T(8,128)(2,1)} %bitcast.36, bf16[1024,256]{1,0:T(8,128)(2,1)} %bitcast.33), custom_call_target="tpu_custom_call" | custom-call | flops 536870912 | bytes 2097152 | tf_op jit(solution)/shard_map/first/pallas_call | solution.py:202
  11.7 4.5 %collective-permute-start.4 = (bf16[4,256,256]{2,1,0:T(8,128)(2,1)}, bf16[4,256,256]{2,1,0:T(8,128)(2,1)S(1)}, u32[]{:S(2)}, u32[]{:S(2)}) collective-permute-start(bf16[4,256,256]{2,1,0:T(8,128)(2,1)} %get-tuple-element.65), channel_id=1, source_target_pairs={{65,66},{66,65},{67,68},{68,67},{69,70},{70,69},{71,0},{0,71},{1,2... | collective-permute-start | bytes 1572872 | tf_op jit(solution)/shard_map/ppermute | solution.py:16
  22.3 2.8 %collective-permute-done.4.cross_ref = bf16[4,256,256]{2,1,0:T(8,128)(2,1)S(1)} collective-permute-done((bf16[4,256,256]{2,1,0:T(8,128)(2,1)}, bf16[4,256,256]{2,1,0:T(8,128)(2,1)S(1)}, u32[]{:S(2)}, u32[]{:S(2)}) %collective-permute-start.4) | collective-permute-done | bytes 524320 | tf_op jit(solution)/shard_map/ppermute | solution.py:16
  26.9 3.9 %collective-permute-start.10 = (bf16[4,256,256]{2,1,0:T(8,128)(2,1)S(1)}, bf16[4,256,256]{2,1,0:T(8,128)(2,1)S(1)}, u32[]{:S(2)}, u32[]{:S(2)}) collective-permute-start(bf16[4,256,256]{2,1,0:T(8,128)(2,1)S(1)} %get-tuple-element.71), channel_id=1, source_target_pairs={{65,66},{66,65},{67,68},{68,67},{69,70},{70,69},{71,0},{0,71},{1,2... | collective-permute-start | bytes 1572872 | tf_op jit(solution)/shard_map/ppermute | solution.py:16
  30.8 1.9 collective-permute-start.11
  36.3 6.7 %collective-permute-start.16 = (bf16[4,256,256]{2,1,0:T(8,128)(2,1)S(1)}, bf16[4,256,256]{2,1,0:T(8,128)(2,1)S(1)}, u32[]{:S(2)}, u32[]{:S(2)}) collective-permute-start(bf16[4,256,256]{2,1,0:T(8,128)(2,1)S(1)} %get-tuple-element.69.env_ref), channel_id=1, source_target_pairs={{71,127},{0,64},{1,65},{2,66},{3,67},{4,68},{5,69},{6,70},{7,71},{... | collective-permute-start | bytes 1572872 | tf_op jit(solution)/shard_map/ppermute | solution.py:16
  44.3 4.4 %collective-permute-done.12.a_ref = bf16[1024,256]{1,0:T(8,128)(2,1)S(1)} collective-permute-done((bf16[1024,256]{1,0:T(8,128)(2,1)}, bf16[1024,256]{1,0:T(8,128)(2,1)S(1)}, u32[]{:S(2)}, u32[]{:S(2)}) %collective-permute-start.12) | collective-permute-done | bytes 524320 | tf_op jit(solution)/shard_map/ppermute | solution.py:16
  50.5 16.5 %collective-permute-start.13 = (bf16[4,256,256]{2,1,0:T(8,128)(2,1)S(1)}, bf16[4,256,256]{2,1,0:T(8,128)(2,1)S(1)}, u32[]{:S(2)}, u32[]{:S(2)}) collective-permute-start(bf16[4,256,256]{2,1,0:T(8,128)(2,1)S(1)} %get-tuple-element.75), channel_id=1, source_target_pairs={{65,66},{66,65},{67,68},{68,67},{69,70},{70,69},{71,0},{0,71},{1,2... | collective-permute-start | bytes 1572872 | tf_op jit(solution)/shard_map/ppermute | solution.py:16
  76.9 5.8 %collective-permute-start.21 = (bf16[4,256,256]{2,1,0:T(8,128)(2,1)S(1)}, bf16[4,256,256]{2,1,0:T(8,128)(2,1)S(1)}, u32[]{:S(2)}, u32[]{:S(2)}) collective-permute-start(bf16[4,256,256]{2,1,0:T(8,128)(2,1)S(1)} %get-tuple-element.86), channel_id=1, source_target_pairs={{65,66},{66,65},{67,68},{68,67},{69,70},{70,69},{71,0},{0,71},{1,2... | collective-permute-start | bytes 1572872 | tf_op jit(solution)/shard_map/ppermute | solution.py:16
  87.5 5.8 %collective-permute-done.20.a_ref = bf16[1040,256]{1,0:T(8,128)(2,1)S(1)} collective-permute-done((bf16[1040,256]{1,0:T(8,128)(2,1)S(1)}, bf16[1040,256]{1,0:T(8,128)(2,1)S(1)}, u32[]{:S(2)}, u32[]{:S(2)}) %collective-permute-start.20) | collective-permute-done | bytes 532512 | tf_op jit(solution)/shard_map/ppermute | solution.py:16
  98.0 3.9 %collective-permute-start.23 = (bf16[4,256,256]{2,1,0:T(8,128)(2,1)S(1)}, bf16[4,256,256]{2,1,0:T(8,128)(2,1)S(1)}, u32[]{:S(2)}, u32[]{:S(2)}) collective-permute-start(bf16[4,256,256]{2,1,0:T(8,128)(2,1)S(1)} %get-tuple-element.89), channel_id=1, source_target_pairs={{65,66},{66,65},{67,68},{68,67},{69,70},{70,69},{71,0},{0,71},{1,2... | collective-permute-start | bytes 1572872 | tf_op jit(solution)/shard_map/ppermute | solution.py:16
  101.9 1.9 collective-permute-start.24
  106.9 5.6 %collective-permute-done.19.a_ref = bf16[1040,256]{1,0:T(8,128)(2,1)S(1)} collective-permute-done((bf16[1040,256]{1,0:T(8,128)(2,1)S(1)}, bf16[1040,256]{1,0:T(8,128)(2,1)S(1)}, u32[]{:S(2)}, u32[]{:S(2)}) %collective-permute-start.19) | collective-permute-done | bytes 532512 | tf_op jit(solution)/shard_map/ppermute | solution.py:16
  116.9 2.0 collective-permute-start.32
  118.9 3.5 %collective-permute-start.33 = (bf16[4,256,256]{2,1,0:T(8,128)(2,1)S(1)}, bf16[4,256,256]{2,1,0:T(8,128)(2,1)S(1)}, u32[]{:S(2)}, u32[]{:S(2)}) collective-permute-start(bf16[4,256,256]{2,1,0:T(8,128)(2,1)S(1)} %get-tuple-element.103), channel_id=1, source_target_pairs={{64,65},{65,64},{66,67},{67,66},{68,69},{69,68},{70,71},{71,70},{0... | collective-permute-start | bytes 1572872 | tf_op jit(solution)/shard_map/ppermute | solution.py:16
  126.0 3.8 %collective-permute-done.31.a_ref = bf16[1040,256]{1,0:T(8,128)(2,1)S(1)} collective-permute-done((bf16[1040,256]{1,0:T(8,128)(2,1)S(1)}, bf16[1040,256]{1,0:T(8,128)(2,1)S(1)}, u32[]{:S(2)}, u32[]{:S(2)}) %collective-permute-start.31) | collective-permute-done | bytes 532512 | tf_op jit(solution)/shard_map/ppermute | solution.py:16
  132.9 1.9 collective-permute-start.34
  134.8 4.5 %collective-permute-start.35 = (bf16[4,256,256]{2,1,0:T(8,128)(2,1)S(1)}, bf16[4,256,256]{2,1,0:T(8,128)(2,1)S(1)}, u32[]{:S(2)}, u32[]{:S(2)}) collective-permute-start(bf16[4,256,256]{2,1,0:T(8,128)(2,1)S(1)} %get-tuple-element.106), channel_id=1, source_target_pairs={{64,65},{65,64},{66,67},{67,66},{68,69},{69,68},{70,71},{71,70},{0... | collective-permute-start | bytes 1572872 | tf_op jit(solution)/shard_map/ppermute | solution.py:16
  147.2 2.3 %collective-permute-start.38 = (bf16[4,256,256]{2,1,0:T(8,128)(2,1)S(1)}, bf16[4,256,256]{2,1,0:T(8,128)(2,1)S(1)}, u32[]{:S(2)}, u32[]{:S(2)}) collective-permute-start(bf16[4,256,256]{2,1,0:T(8,128)(2,1)S(1)} %get-tuple-element.111), channel_id=1, source_target_pairs={{65,66},{66,65},{67,68},{68,67},{69,70},{70,69},{71,0},{0,71},{1,2... | collective-permute-start | bytes 1572872 | tf_op jit(solution)/shard_map/ppermute | solution.py:16
  149.5 4.7 %collective-permute-start.39 = (bf16[4,256,256]{2,1,0:T(8,128)(2,1)S(1)}, bf16[4,256,256]{2,1,0:T(8,128)(2,1)S(1)}, u32[]{:S(2)}, u32[]{:S(2)}) collective-permute-start(bf16[4,256,256]{2,1,0:T(8,128)(2,1)S(1)} %get-tuple-element.112), channel_id=1, source_target_pairs={{64,65},{65,64},{66,67},{67,66},{68,69},{69,68},{70,71},{71,70},{0... | collective-permute-start | bytes 1572872 | tf_op jit(solution)/shard_map/ppermute | solution.py:16
  157.1 2.7 %collective-permute-done.38.cross_ref = bf16[4,256,256]{2,1,0:T(8,128)(2,1)S(1)} collective-permute-done((bf16[4,256,256]{2,1,0:T(8,128)(2,1)S(1)}, bf16[4,256,256]{2,1,0:T(8,128)(2,1)S(1)}, u32[]{:S(2)}, u32[]{:S(2)}) %collective-permute-start.38) | collective-permute-done | bytes 524320 | tf_op jit(solution)/shard_map/ppermute | solution.py:16
  160.1 5.3 %collective-permute-start.40 = (bf16[4,256,256]{2,1,0:T(8,128)(2,1)S(1)}, bf16[4,256,256]{2,1,0:T(8,128)(2,1)S(1)}, u32[]{:S(2)}, u32[]{:S(2)}) collective-permute-start(bf16[4,256,256]{2,1,0:T(8,128)(2,1)S(1)} %last.1), channel_id=1, source_target_pairs={{64,0},{65,1},{66,2},{67,3},{68,4},{69,5},{70,6},{71,7},{0,8},{1,9... | collective-permute-start | bytes 1572872 | tf_op jit(solution)/shard_map/ppermute | solution.py:16
  165.4 33.2 %collective-permute-done.43.refs_7_ = bf16[4,256,256]{2,1,0:T(8,128)(2,1)S(1)} collective-permute-done((bf16[4,256,256]{2,1,0:T(8,128)(2,1)S(1)}, bf16[4,256,256]{2,1,0:T(8,128)(2,1)S(1)}, u32[]{:S(2)}, u32[]{:S(2)}) %collective-permute-start.43) | collective-permute-done | bytes 524320 | tf_op jit(solution)/shard_map/ppermute | solution.py:16
  198.6 9.4 %collective-permute-done.40.refs_0_ = bf16[4,256,256]{2,1,0:T(8,128)(2,1)S(1)} collective-permute-done((bf16[4,256,256]{2,1,0:T(8,128)(2,1)S(1)}, bf16[4,256,256]{2,1,0:T(8,128)(2,1)S(1)}, u32[]{:S(2)}, u32[]{:S(2)}) %collective-permute-start.40) | collective-permute-done | bytes 524320 | tf_op jit(solution)/shard_map/ppermute | solution.py:16
  (106 shorter events, 67.0 us)
Async XLA Ops:
  0.0 21.6 %collective-permute-start.6 = (bf16[1024,256]{1,0:T(8,128)(2,1)}, bf16[1024,256]{1,0:T(8,128)(2,1)}, u32[]{:S(2)}, u32[]{:S(2)}) collective-permute-start(bf16[1024,256]{1,0:T(8,128)(2,1)} %bitcast.31), channel_id=1, source_target_pairs={{128,190},{129,191},{130,128},{131,129},{132,130},{133,131},{134,1... | collective-permute-start | bytes 1572872 | tf_op jit(solution)/shard_map/ppermute | solution.py:16
  1.5 23.7 %collective-permute-start.7 = (bf16[1024,256]{1,0:T(8,128)(2,1)}, bf16[1024,256]{1,0:T(8,128)(2,1)S(1)}, u32[]{:S(2)}, u32[]{:S(2)}) collective-permute-start(bf16[1024,256]{1,0:T(8,128)(2,1)} %bitcast.32), channel_id=1, source_target_pairs={{64,71},{65,0},{66,1},{67,2},{68,3},{69,4},{70,5},{71,6},{72,7},{7... | collective-permute-start | bytes 1572872 | tf_op jit(solution)/shard_map/ppermute | solution.py:16
  6.3 30.0 %collective-permute-start.9 = (f32[64]{0:T(128)S(1)}, f32[64]{0:T(128)S(1)}, u32[]{:S(2)}, u32[]{:S(2)}) collective-permute-start(f32[64]{0:T(128)S(1)} %reshape.16), channel_id=1, source_target_pairs={{128,70},{129,71},{130,0},{131,1},{132,2},{133,3},{134,4},{135,5},... | collective-permute-start | bytes 776 | tf_op jit(solution)/shard_map/ppermute | solution.py:16
  26.9 16.1 %collective-permute-start.10 = (bf16[4,256,256]{2,1,0:T(8,128)(2,1)S(1)}, bf16[4,256,256]{2,1,0:T(8,128)(2,1)S(1)}, u32[]{:S(2)}, u32[]{:S(2)}) collective-permute-start(bf16[4,256,256]{2,1,0:T(8,128)(2,1)S(1)} %get-tuple-element.71), channel_id=1, source_target_pairs={{65,66},{66,65},{67,68},{68,67},{69,70},{70,69},{71,0},{0,71},{1,2... | collective-permute-start | bytes 1572872 | tf_op jit(solution)/shard_map/ppermute | solution.py:16
  32.7 16.0 %collective-permute-start.12 = (bf16[1024,256]{1,0:T(8,128)(2,1)}, bf16[1024,256]{1,0:T(8,128)(2,1)S(1)}, u32[]{:S(2)}, u32[]{:S(2)}) collective-permute-start(bf16[1024,256]{1,0:T(8,128)(2,1)} %collective-permute-done.6), channel_id=1, source_target_pairs={{190,70},{191,71},{128,0},{129,1},{130,2},{131,3},{132,4},{133,5},... | collective-permute-start | bytes 1572872 | tf_op jit(solution)/shard_map/ppermute | solution.py:16
  35.6 35.6 %collective-permute-start.15 = (bf16[1040,256]{1,0:T(8,128)(2,1)S(1)}, bf16[1040,256]{1,0:T(8,128)(2,1)S(1)}, u32[]{:S(2)}, u32[]{:S(2)}) collective-permute-start(bf16[1040,256]{1,0:T(8,128)(2,1)S(1)} %pad_maximum_fusion), channel_id=1, source_target_pairs={{256,316},{257,317},{258,318},{259,319},{260,256},{261,257},{262,2... | collective-permute-start | bytes 1597448 | tf_op jit(solution)/shard_map/ppermute | solution.py:16
  36.3 34.2 %collective-permute-start.16 = (bf16[4,256,256]{2,1,0:T(8,128)(2,1)S(1)}, bf16[4,256,256]{2,1,0:T(8,128)(2,1)S(1)}, u32[]{:S(2)}, u32[]{:S(2)}) collective-permute-start(bf16[4,256,256]{2,1,0:T(8,128)(2,1)S(1)} %get-tuple-element.69.env_ref), channel_id=1, source_target_pairs={{71,127},{0,64},{1,65},{2,66},{3,67},{4,68},{5,69},{6,70},{7,71},{... | collective-permute-start | bytes 1572872 | tf_op jit(solution)/shard_map/ppermute | solution.py:16
  43.0 28.9 %collective-permute-start.8 = (bf16[1040,256]{1,0:T(8,128)(2,1)S(1)}, bf16[1040,256]{1,0:T(8,128)(2,1)S(1)}, u32[]{:S(2)}, u32[]{:S(2)}) collective-permute-start(bf16[1040,256]{1,0:T(8,128)(2,1)S(1)} %collective-permute-done.3), channel_id=1, source_target_pairs={{253,69},{254,70},{255,71},{192,0},{193,1},{194,2},{195,3},{196,4}... | collective-permute-start | bytes 1597448 | tf_op jit(solution)/shard_map/ppermute | solution.py:16
  50.5 23.3 %collective-permute-start.13 = (bf16[4,256,256]{2,1,0:T(8,128)(2,1)S(1)}, bf16[4,256,256]{2,1,0:T(8,128)(2,1)S(1)}, u32[]{:S(2)}, u32[]{:S(2)}) collective-permute-start(bf16[4,256,256]{2,1,0:T(8,128)(2,1)S(1)} %get-tuple-element.75), channel_id=1, source_target_pairs={{65,66},{66,65},{67,68},{68,67},{69,70},{70,69},{71,0},{0,71},{1,2... | collective-permute-start | bytes 1572872 | tf_op jit(solution)/shard_map/ppermute | solution.py:16
  71.2 15.7 %collective-permute-start.2 = (bf16[1040,256]{1,0:T(8,128)(2,1)S(1)}, bf16[1040,256]{1,0:T(8,128)(2,1)S(1)}, u32[]{:S(2)}, u32[]{:S(2)}) collective-permute-start(bf16[1040,256]{1,0:T(8,128)(2,1)S(1)} %pad_maximum_fusion), channel_id=1, source_target_pairs={{320,379},{321,380},{322,381},{323,382},{324,383},{325,320},{326,3... | collective-permute-start | bytes 1597448 | tf_op jit(solution)/shard_map/ppermute | solution.py:16
  73.8 19.5 %collective-permute-start.20 = (bf16[1040,256]{1,0:T(8,128)(2,1)S(1)}, bf16[1040,256]{1,0:T(8,128)(2,1)S(1)}, u32[]{:S(2)}, u32[]{:S(2)}) collective-permute-start(bf16[1040,256]{1,0:T(8,128)(2,1)S(1)} %collective-permute-done.15), channel_id=1, source_target_pairs={{316,68},{317,69},{318,70},{319,71},{256,0},{257,1},{258,2},{259,3... | collective-permute-start | bytes 1597448 | tf_op jit(solution)/shard_map/ppermute | solution.py:16
  76.9 17.8 %collective-permute-start.21 = (bf16[4,256,256]{2,1,0:T(8,128)(2,1)S(1)}, bf16[4,256,256]{2,1,0:T(8,128)(2,1)S(1)}, u32[]{:S(2)}, u32[]{:S(2)}) collective-permute-start(bf16[4,256,256]{2,1,0:T(8,128)(2,1)S(1)} %get-tuple-element.86), channel_id=1, source_target_pairs={{65,66},{66,65},{67,68},{68,67},{69,70},{70,69},{71,0},{0,71},{1,2... | collective-permute-start | bytes 1572872 | tf_op jit(solution)/shard_map/ppermute | solution.py:16
  86.1 15.8 %collective-permute-start.26 = (bf16[4,256,256]{2,1,0:T(8,128)(2,1)S(1)}, bf16[4,256,256]{2,1,0:T(8,128)(2,1)S(1)}, u32[]{:S(2)}, u32[]{:S(2)}) collective-permute-start(bf16[4,256,256]{2,1,0:T(8,128)(2,1)S(1)} %collective-permute-done.18), channel_id=1, source_target_pairs={{190,128},{191,129},{128,130},{129,131},{130,132},{131,133},{132,1... | collective-permute-start | bytes 1572872 | tf_op jit(solution)/shard_map/ppermute | solution.py:16
  86.8 19.4 %collective-permute-start.25 = (bf16[1040,256]{1,0:T(8,128)(2,1)S(1)}, bf16[1040,256]{1,0:T(8,128)(2,1)S(1)}, u32[]{:S(2)}, u32[]{:S(2)}) collective-permute-start(bf16[1040,256]{1,0:T(8,128)(2,1)S(1)} %pad_maximum_fusion), channel_id=1, source_target_pairs={{384,442},{385,443},{386,444},{387,445},{388,446},{389,447},{390,3... | collective-permute-start | bytes 1597448 | tf_op jit(solution)/shard_map/ppermute | solution.py:16
  94.7 17.8 %collective-permute-start.19 = (bf16[1040,256]{1,0:T(8,128)(2,1)S(1)}, bf16[1040,256]{1,0:T(8,128)(2,1)S(1)}, u32[]{:S(2)}, u32[]{:S(2)}) collective-permute-start(bf16[1040,256]{1,0:T(8,128)(2,1)S(1)} %collective-permute-done.2), channel_id=1, source_target_pairs={{379,67},{380,68},{381,69},{382,70},{383,71},{320,0},{321,1},{322,... | collective-permute-start | bytes 1597448 | tf_op jit(solution)/shard_map/ppermute | solution.py:16
  98.0 15.9 %collective-permute-start.23 = (bf16[4,256,256]{2,1,0:T(8,128)(2,1)S(1)}, bf16[4,256,256]{2,1,0:T(8,128)(2,1)S(1)}, u32[]{:S(2)}, u32[]{:S(2)}) collective-permute-start(bf16[4,256,256]{2,1,0:T(8,128)(2,1)S(1)} %get-tuple-element.89), channel_id=1, source_target_pairs={{65,66},{66,65},{67,68},{68,67},{69,70},{70,69},{71,0},{0,71},{1,2... | collective-permute-start | bytes 1572872 | tf_op jit(solution)/shard_map/ppermute | solution.py:16
  106.2 19.1 %collective-permute-start.1 = (bf16[1040,256]{1,0:T(8,128)(2,1)S(1)}, bf16[1040,256]{1,0:T(8,128)(2,1)S(1)}, u32[]{:S(2)}, u32[]{:S(2)}) collective-permute-start(bf16[1040,256]{1,0:T(8,128)(2,1)S(1)} %pad_maximum_fusion), channel_id=1, source_target_pairs={{448,505},{449,506},{450,507},{451,508},{452,509},{453,510},{454,5... | collective-permute-start | bytes 1597448 | tf_op jit(solution)/shard_map/ppermute | solution.py:16
  113.8 16.0 %collective-permute-start.31 = (bf16[1040,256]{1,0:T(8,128)(2,1)S(1)}, bf16[1040,256]{1,0:T(8,128)(2,1)S(1)}, u32[]{:S(2)}, u32[]{:S(2)}) collective-permute-start(bf16[1040,256]{1,0:T(8,128)(2,1)S(1)} %collective-permute-done.25), channel_id=1, source_target_pairs={{442,66},{443,67},{444,68},{445,69},{446,70},{447,71},{384,0},{385... | collective-permute-start | bytes 1597448 | tf_op jit(solution)/shard_map/ppermute | solution.py:16
  124.0 18.2 %collective-permute-start.37 = (bf16[4,256,256]{2,1,0:T(8,128)(2,1)S(1)}, bf16[4,256,256]{2,1,0:T(8,128)(2,1)S(1)}, u32[]{:S(2)}, u32[]{:S(2)}) collective-permute-start(bf16[4,256,256]{2,1,0:T(8,128)(2,1)S(1)} %get-tuple-element.96.env_ref), channel_id=1, source_target_pairs={{67,379},{68,380},{69,381},{70,382},{71,383},{0,320},{1,321},{2,32... | collective-permute-start | bytes 1572872 | tf_op jit(solution)/shard_map/ppermute | solution.py:16
  125.3 15.6 %collective-permute-start.36 = (bf16[4,256,256]{2,1,0:T(8,128)(2,1)S(1)}, bf16[4,256,256]{2,1,0:T(8,128)(2,1)S(1)}, u32[]{:S(2)}, u32[]{:S(2)}) collective-permute-start(bf16[4,256,256]{2,1,0:T(8,128)(2,1)S(1)} %collective-permute-done.29), channel_id=1, source_target_pairs={{316,256},{317,257},{318,258},{319,259},{256,260},{257,261},{258,2... | collective-permute-start | bytes 1572872 | tf_op jit(solution)/shard_map/ppermute | solution.py:16
  140.9 24.6 %collective-permute-start.42 = (bf16[4,256,256]{2,1,0:T(8,128)(2,1)S(1)}, bf16[4,256,256]{2,1,0:T(8,128)(2,1)S(1)}, u32[]{:S(2)}, u32[]{:S(2)}) collective-permute-start(bf16[4,256,256]{2,1,0:T(8,128)(2,1)S(1)} %get-tuple-element.107.env_ref), channel_id=1, source_target_pairs={{66,384},{67,385},{68,386},{69,387},{70,388},{71,389},{0,390},{1,3... | collective-permute-start | bytes 1572872 | tf_op jit(solution)/shard_map/ppermute | solution.py:16
  142.2 23.2 %collective-permute-start.41 = (bf16[4,256,256]{2,1,0:T(8,128)(2,1)S(1)}, bf16[4,256,256]{2,1,0:T(8,128)(2,1)S(1)}, u32[]{:S(2)}, u32[]{:S(2)}) collective-permute-start(bf16[4,256,256]{2,1,0:T(8,128)(2,1)S(1)} %collective-permute-done.37), channel_id=1, source_target_pairs={{379,320},{380,321},{381,322},{382,323},{383,324},{320,325},{321,3... | collective-permute-start | bytes 1572872 | tf_op jit(solution)/shard_map/ppermute | solution.py:16
  154.2 44.4 %collective-permute-start.43 = (bf16[4,256,256]{2,1,0:T(8,128)(2,1)S(1)}, bf16[4,256,256]{2,1,0:T(8,128)(2,1)S(1)}, u32[]{:S(2)}, u32[]{:S(2)}) collective-permute-start(bf16[4,256,256]{2,1,0:T(8,128)(2,1)S(1)} %get-tuple-element.113.env_ref), channel_id=1, source_target_pairs={{65,448},{66,449},{67,450},{68,451},{69,452},{70,453},{71,454},{0,... | collective-permute-start | bytes 1572872 | tf_op jit(solution)/shard_map/ppermute | solution.py:16
  160.1 48.0 %collective-permute-start.40 = (bf16[4,256,256]{2,1,0:T(8,128)(2,1)S(1)}, bf16[4,256,256]{2,1,0:T(8,128)(2,1)S(1)}, u32[]{:S(2)}, u32[]{:S(2)}) collective-permute-start(bf16[4,256,256]{2,1,0:T(8,128)(2,1)S(1)} %last.1), channel_id=1, source_target_pairs={{64,0},{65,1},{66,2},{67,3},{68,4},{69,5},{70,6},{71,7},{0,8},{1,9... | collective-permute-start | bytes 1572872 | tf_op jit(solution)/shard_map/ppermute | solution.py:16
  (23 other events, 258.1 us)

commit v6 on v5

--- a/solution.py
+++ b/solution.py
@@ -164,7 +164,7 @@
 
     parcels = {0: blocks, 1: moved(blocks, straight_pairs(1), sectors)}
     scales = {0: rooted, 1: moved(weights, straight_pairs(1), sectors)}
-    turned = {2: moved(blocks, turn_pairs(2), sectors)}
+    turned = {}
 
     def pack(after):
         held, lying, after = lax.optimization_barrier((weights, blocks, after))
@@ -180,6 +180,9 @@
         return parts[0] + parts[1] + parts[2]
 
     def fetch(s, after):
+        if s not in turned:
+            held, after = lax.optimization_barrier((blocks, after))
+            return moved(held, straight_pairs(s), sectors), after
         held, after = lax.optimization_barrier((turned[s], after))
         pairs = [((s, (t - s) % sectors), device(t - s)) for t in range(sectors)]
         return moved(held, pairs, sectors), after
@@ -239,11 +242,11 @@
             out_specs=VMEM,
             scratch_shapes=work,
             compiler_params=PARAMS,
-            cost_estimate=cost(40, 4),
+            cost_estimate=cost(10, 4),
             name="stay",
         )(scales[s], source, parcels[s])
         if s == 0:
-            packed, scales[1] = pack(scales[1])
+            packed, swap = pack(swap)
             for r in range(3, sites):
                 turned[r] = moved(packed, turn_pairs(r), sectors)
             scales[2] = moved(weights, straight_pairs(2), sectors)
@@ -258,8 +261,9 @@
             stay, risen = lax.optimization_barrier((stay, raised[s - 1]))
             pairs = [((s - 1, (t - s + 1) % sectors), (s - 1, t)) for t in range(sectors)]
             homed[s - 1] = moved(risen, pairs, sectors)
-        if s + 2 < sites:
-            parcels[s + 2], stay = fetch(s + 2, stay)
+        for ahead in (2, 3) if s == 0 else (s + 3,):
+            if ahead < sites:
+                parcels[ahead], stay = fetch(ahead, stay)
 
     ended = pl.pallas_call(
         last_kernel,

time: 210 us -> 219 us (1.043)
  waiting for transfers between devices: 71.9 us -> 110 us
  starting transfers between devices: 103 us -> 74.9 us
    ppermute x44 -> x43, waiting for transfers between devices: 71.9 us -> 110 us  [moved(): return lax.ppermute(x, AXES, flat)]
    ppermute x44 -> x43, starting transfers between devices: 103 us -> 74.9 us  [moved(): return lax.ppermute(x, AXES, flat)]
  transfers between devices with their start and end apart: 44 -> 43, of which waited for: 13 -> 16; matrix products, arithmetic and copies ran while one was open for 1% -> 0% of each run, Pallas kernels for 14% -> 11%
where the time goes in v6:
time: 219 us; the launch traced here: 217 us
  waiting for transfers between devices  110 us (50%)
  starting transfers between devices  74.9 us (34%)
  Pallas kernels  29.7 us (14%)
    ppermute x43, waiting for transfers between devices, moved(): return lax.ppermute(x, AXES, flat)  110 us
    ppermute x43, starting transfers between devices, moved(): return lax.ppermute(x, AXES, flat)  74.9 us
    pallas_call x8, Pallas kernels, local(): pl.pallas_call(stay_kernel, out_shape=block_shape, in_specs=[SMEM, VMEM,...  12.3 us
    pallas_call x7, Pallas kernels, local(): pl.pallas_call(lead_kernel, out_shape=(block_shape,) * 3, in_specs=[SMEM,...  12.1 us
  transfers between devices with their start and end apart: 43, of which 16 were waited for; matrix products, arithmetic and copies ran while one was open for 0% of the time, Pallas kernels for 11%

profile of v6, /device:TPU:7, one launch (start us, length us, event | category | flops | bytes accessed | tf_op | source)
XLA Modules:
  0.0 217.4 jit_solution(12552510160002741052)
XLA Ops:
  1.3 4.1 %first.1 = (bf16[4,256,256]{2,1,0:T(8,128)(2,1)}, bf16[4,256,256]{2,1,0:T(8,128)(2,1)}) custom-call(s32[1]{0:T(128)} %bitcast.1.p_ref, f32[4,4,4]{2,1,0:T(4,128)} %bitcast.39, s32[4,4,4]{2,1,0:T(4,128)} %bitcast.38, s32[4]{0:T(128)} %get-tuple-element.122.couple_ref, bf16[4,256,256]{2,1,0:T(8,128)(2,1)} %bitcast.36, bf16[1024,256]{1,0:T(8,128)(2,1)} %bitcast.31), custom_call_target="tpu_custom_call" | custom-call | flops 536870912 | bytes 2097152 | tf_op jit(solution)/shard_map/first/pallas_call | solution.py:205
  5.5 2.6 %collective-permute-start = (bf16[4,256,256]{2,1,0:T(8,128)(2,1)}, bf16[4,256,256]{2,1,0:T(8,128)(2,1)S(1)}, u32[]{:S(2)}, u32[]{:S(2)}) collective-permute-start(bf16[4,256,256]{2,1,0:T(8,128)(2,1)} %get-tuple-element.62), channel_id=1, source_target_pairs={{64,65},{65,64},{66,67},{67,66},{68,69},{69,68},{70,71},{71,70},{0... | collective-permute-start | bytes 1572872 | tf_op jit(solution)/shard_map/ppermute | solution.py:16
  9.4 3.8 %collective-permute-start.4 = (bf16[4,256,256]{2,1,0:T(8,128)(2,1)}, bf16[4,256,256]{2,1,0:T(8,128)(2,1)S(1)}, u32[]{:S(2)}, u32[]{:S(2)}) collective-permute-start(bf16[4,256,256]{2,1,0:T(8,128)(2,1)} %get-tuple-element.65), channel_id=1, source_target_pairs={{65,66},{66,65},{67,68},{68,67},{69,70},{70,69},{71,0},{0,71},{1,2... | collective-permute-start | bytes 1572872 | tf_op jit(solution)/shard_map/ppermute | solution.py:16
  19.2 17.4 %collective-permute-done.3.w_ref = f32[64]{0:T(128)S(1)} collective-permute-done((f32[64]{0:T(128)S(1)}, f32[64]{0:T(128)S(1)}, u32[]{:S(2)}, u32[]{:S(2)}) %collective-permute-start.3) | collective-permute-done | bytes 288 | tf_op jit(solution)/shard_map/ppermute | solution.py:16
  36.6 2.1 collective-permute-done.4.cross_ref
  42.4 4.2 %collective-permute-start.11 = (bf16[4,256,256]{2,1,0:T(8,128)(2,1)S(1)}, bf16[4,256,256]{2,1,0:T(8,128)(2,1)S(1)}, u32[]{:S(2)}, u32[]{:S(2)}) collective-permute-start(bf16[4,256,256]{2,1,0:T(8,128)(2,1)S(1)} %get-tuple-element.74), channel_id=1, source_target_pairs={{64,65},{65,64},{66,67},{67,66},{68,69},{69,68},{70,71},{71,70},{0... | collective-permute-start | bytes 1572872 | tf_op jit(solution)/shard_map/ppermute | solution.py:16
  47.9 6.9 %collective-permute-done.9.w_ref = f32[64]{0:T(128)S(1)} collective-permute-done((f32[64]{0:T(128)S(1)}, f32[64]{0:T(128)S(1)}, u32[]{:S(2)}, u32[]{:S(2)}) %collective-permute-start.9) | collective-permute-done | bytes 288 | tf_op jit(solution)/shard_map/ppermute | solution.py:16
  55.5 3.6 %collective-permute-start.16 = (bf16[4,256,256]{2,1,0:T(8,128)(2,1)S(1)}, bf16[4,256,256]{2,1,0:T(8,128)(2,1)S(1)}, u32[]{:S(2)}, u32[]{:S(2)}) collective-permute-start(bf16[4,256,256]{2,1,0:T(8,128)(2,1)S(1)} %get-tuple-element.70.env_ref), channel_id=1, source_target_pairs={{71,127},{0,64},{1,65},{2,66},{3,67},{4,68},{5,69},{6,70},{7,71},{... | collective-permute-start | bytes 1572872 | tf_op jit(solution)/shard_map/ppermute | solution.py:16
  65.7 3.8 %collective-permute-start.14 = (bf16[4,256,256]{2,1,0:T(8,128)(2,1)S(1)}, bf16[4,256,256]{2,1,0:T(8,128)(2,1)S(1)}, u32[]{:S(2)}, u32[]{:S(2)}) collective-permute-start(bf16[4,256,256]{2,1,0:T(8,128)(2,1)S(1)} %get-tuple-element.78), channel_id=1, source_target_pairs={{64,65},{65,64},{66,67},{67,66},{68,69},{69,68},{70,71},{71,70},{0... | collective-permute-start | bytes 1572872 | tf_op jit(solution)/shard_map/ppermute | solution.py:16
  82.2 2.4 %collective-permute-done.21 = bf16[4,256,256]{2,1,0:T(8,128)(2,1)S(1)} collective-permute-done((bf16[4,256,256]{2,1,0:T(8,128)(2,1)S(1)}, bf16[4,256,256]{2,1,0:T(8,128)(2,1)S(1)}, u32[]{:S(2)}, u32[]{:S(2)}) %collective-permute-start.21) | collective-permute-done | bytes 524320 | tf_op jit(solution)/shard_map/ppermute | solution.py:16
  84.6 2.6 %collective-permute-start.18 = (bf16[4,256,256]{2,1,0:T(8,128)(2,1)S(1)}, bf16[4,256,256]{2,1,0:T(8,128)(2,1)S(1)}, u32[]{:S(2)}, u32[]{:S(2)}) collective-permute-start(bf16[4,256,256]{2,1,0:T(8,128)(2,1)S(1)} %get-tuple-element.83), channel_id=1, source_target_pairs={{64,65},{65,64},{66,67},{67,66},{68,69},{69,68},{70,71},{71,70},{0... | collective-permute-start | bytes 1572872 | tf_op jit(solution)/shard_map/ppermute | solution.py:16
  88.7 2.3 %collective-permute-done.7.a_ref = bf16[1040,256]{1,0:T(8,128)(2,1)S(1)} collective-permute-done((bf16[1040,256]{1,0:T(8,128)(2,1)S(1)}, bf16[1040,256]{1,0:T(8,128)(2,1)S(1)}, u32[]{:S(2)}, u32[]{:S(2)}) %collective-permute-start.7) | collective-permute-done | bytes 532512 | tf_op jit(solution)/shard_map/ppermute | solution.py:16
  97.7 8.0 %collective-permute-done.26.a_ref = bf16[1040,256]{1,0:T(8,128)(2,1)S(1)} collective-permute-done((bf16[1040,256]{1,0:T(8,128)(2,1)S(1)}, bf16[1040,256]{1,0:T(8,128)(2,1)S(1)}, u32[]{:S(2)}, u32[]{:S(2)}) %collective-permute-start.26) | collective-permute-done | bytes 532512 | tf_op jit(solution)/shard_map/ppermute | solution.py:16
  105.7 3.0 %collective-permute-start.27 = (bf16[4,256,256]{2,1,0:T(8,128)(2,1)S(1)}, bf16[4,256,256]{2,1,0:T(8,128)(2,1)S(1)}, u32[]{:S(2)}, u32[]{:S(2)}) collective-permute-start(bf16[4,256,256]{2,1,0:T(8,128)(2,1)S(1)} %get-tuple-element.96), channel_id=1, source_target_pairs={{65,66},{66,65},{67,68},{68,67},{69,70},{70,69},{71,0},{0,71},{1,2... | collective-permute-start | bytes 1572872 | tf_op jit(solution)/shard_map/ppermute | solution.py:16
  114.3 4.0 %collective-permute-done.27.cross_ref = bf16[4,256,256]{2,1,0:T(8,128)(2,1)S(1)} collective-permute-done((bf16[4,256,256]{2,1,0:T(8,128)(2,1)S(1)}, bf16[4,256,256]{2,1,0:T(8,128)(2,1)S(1)}, u32[]{:S(2)}, u32[]{:S(2)}) %collective-permute-start.27) | collective-permute-done | bytes 524320 | tf_op jit(solution)/shard_map/ppermute | solution.py:16
  121.4 3.0 %collective-permute-start.29 = (bf16[4,256,256]{2,1,0:T(8,128)(2,1)S(1)}, bf16[4,256,256]{2,1,0:T(8,128)(2,1)S(1)}, u32[]{:S(2)}, u32[]{:S(2)}) collective-permute-start(bf16[4,256,256]{2,1,0:T(8,128)(2,1)S(1)} %get-tuple-element.99), channel_id=1, source_target_pairs={{65,66},{66,65},{67,68},{68,67},{69,70},{70,69},{71,0},{0,71},{1,2... | collective-permute-start | bytes 1572872 | tf_op jit(solution)/shard_map/ppermute | solution.py:16
  130.0 4.0 %collective-permute-done.29.cross_ref = bf16[4,256,256]{2,1,0:T(8,128)(2,1)S(1)} collective-permute-done((bf16[4,256,256]{2,1,0:T(8,128)(2,1)S(1)}, bf16[4,256,256]{2,1,0:T(8,128)(2,1)S(1)}, u32[]{:S(2)}, u32[]{:S(2)}) %collective-permute-start.29) | collective-permute-done | bytes 524320 | tf_op jit(solution)/shard_map/ppermute | solution.py:16
  135.7 3.0 %collective-permute-start.33 = (bf16[4,256,256]{2,1,0:T(8,128)(2,1)S(1)}, bf16[4,256,256]{2,1,0:T(8,128)(2,1)S(1)}, u32[]{:S(2)}, u32[]{:S(2)}) collective-permute-start(bf16[4,256,256]{2,1,0:T(8,128)(2,1)S(1)} %get-tuple-element.105), channel_id=1, source_target_pairs={{65,66},{66,65},{67,68},{68,67},{69,70},{70,69},{71,0},{0,71},{1,2... | collective-permute-start | bytes 1572872 | tf_op jit(solution)/shard_map/ppermute | solution.py:16
  142.3 6.0 %collective-permute-done.33.cross_ref = bf16[4,256,256]{2,1,0:T(8,128)(2,1)S(1)} collective-permute-done((bf16[4,256,256]{2,1,0:T(8,128)(2,1)S(1)}, bf16[4,256,256]{2,1,0:T(8,128)(2,1)S(1)}, u32[]{:S(2)}, u32[]{:S(2)}) %collective-permute-start.33) | collective-permute-done | bytes 524320 | tf_op jit(solution)/shard_map/ppermute | solution.py:16
  150.1 3.0 %collective-permute-start.37 = (bf16[4,256,256]{2,1,0:T(8,128)(2,1)S(1)}, bf16[4,256,256]{2,1,0:T(8,128)(2,1)S(1)}, u32[]{:S(2)}, u32[]{:S(2)}) collective-permute-start(bf16[4,256,256]{2,1,0:T(8,128)(2,1)S(1)} %get-tuple-element.111), channel_id=1, source_target_pairs={{65,66},{66,65},{67,68},{68,67},{69,70},{70,69},{71,0},{0,71},{1,2... | collective-permute-start | bytes 1572872 | tf_op jit(solution)/shard_map/ppermute | solution.py:16
  160.0 2.7 %collective-permute-done.37.cross_ref = bf16[4,256,256]{2,1,0:T(8,128)(2,1)S(1)} collective-permute-done((bf16[4,256,256]{2,1,0:T(8,128)(2,1)S(1)}, bf16[4,256,256]{2,1,0:T(8,128)(2,1)S(1)}, u32[]{:S(2)}, u32[]{:S(2)}) %collective-permute-start.37) | collective-permute-done | bytes 524320 | tf_op jit(solution)/shard_map/ppermute | solution.py:16
  164.8 8.1 %collective-permute-done.41.refs_6_ = bf16[4,256,256]{2,1,0:T(8,128)(2,1)S(1)} collective-permute-done((bf16[4,256,256]{2,1,0:T(8,128)(2,1)S(1)}, bf16[4,256,256]{2,1,0:T(8,128)(2,1)S(1)}, u32[]{:S(2)}, u32[]{:S(2)}) %collective-permute-start.41) | collective-permute-done | bytes 524320 | tf_op jit(solution)/shard_map/ppermute | solution.py:16
  173.0 33.6 %collective-permute-done.42.refs_7_ = bf16[4,256,256]{2,1,0:T(8,128)(2,1)S(1)} collective-permute-done((bf16[4,256,256]{2,1,0:T(8,128)(2,1)S(1)}, bf16[4,256,256]{2,1,0:T(8,128)(2,1)S(1)}, u32[]{:S(2)}, u32[]{:S(2)}) %collective-permute-start.42) | collective-permute-done | bytes 524320 | tf_op jit(solution)/shard_map/ppermute | solution.py:16
  206.5 9.8 %collective-permute-done.39.refs_0_ = bf16[4,256,256]{2,1,0:T(8,128)(2,1)S(1)} collective-permute-done((bf16[4,256,256]{2,1,0:T(8,128)(2,1)S(1)}, bf16[4,256,256]{2,1,0:T(8,128)(2,1)S(1)}, u32[]{:S(2)}, u32[]{:S(2)}) %collective-permute-start.39) | collective-permute-done | bytes 524320 | tf_op jit(solution)/shard_map/ppermute | solution.py:16
  (106 shorter events, 72.2 us)
Async XLA Ops:
  8.1 30.7 %collective-permute-start.6 = (bf16[1024,256]{1,0:T(8,128)(2,1)S(1)}, bf16[1024,256]{1,0:T(8,128)(2,1)S(1)}, u32[]{:S(2)}, u32[]{:S(2)}) collective-permute-start(bf16[1024,256]{1,0:T(8,128)(2,1)S(1)} %bitcast.32), channel_id=1, source_target_pairs={{64,71},{65,0},{66,1},{67,2},{68,3},{69,4},{70,5},{71,6},{72,7},{7... | collective-permute-start | bytes 1572872 | tf_op jit(solution)/shard_map/ppermute | solution.py:16
  9.4 29.4 %collective-permute-start.4 = (bf16[4,256,256]{2,1,0:T(8,128)(2,1)}, bf16[4,256,256]{2,1,0:T(8,128)(2,1)S(1)}, u32[]{:S(2)}, u32[]{:S(2)}) collective-permute-start(bf16[4,256,256]{2,1,0:T(8,128)(2,1)} %get-tuple-element.65), channel_id=1, source_target_pairs={{65,66},{66,65},{67,68},{68,67},{69,70},{70,69},{71,0},{0,71},{1,2... | collective-permute-start | bytes 1572872 | tf_op jit(solution)/shard_map/ppermute | solution.py:16
  14.4 44.8 %collective-permute-start.2 = (bf16[1040,256]{1,0:T(8,128)(2,1)S(1)}, bf16[1040,256]{1,0:T(8,128)(2,1)S(1)}, u32[]{:S(2)}, u32[]{:S(2)}) collective-permute-start(bf16[1040,256]{1,0:T(8,128)(2,1)S(1)} %pad_maximum_fusion), channel_id=1, source_target_pairs={{256,316},{257,317},{258,318},{259,319},{260,256},{261,257},{262,2... | collective-permute-start | bytes 1597448 | tf_op jit(solution)/shard_map/ppermute | solution.py:16
  16.6 38.9 %collective-permute-start.12 = (bf16[1024,256]{1,0:T(8,128)(2,1)S(1)}, bf16[1024,256]{1,0:T(8,128)(2,1)S(1)}, u32[]{:S(2)}, u32[]{:S(2)}) collective-permute-start(bf16[1024,256]{1,0:T(8,128)(2,1)S(1)} %bitcast.35), channel_id=1, source_target_pairs={{128,70},{129,71},{130,0},{131,1},{132,2},{133,3},{134,4},{135,5},... | collective-permute-start | bytes 1572872 | tf_op jit(solution)/shard_map/ppermute | solution.py:16
  17.9 18.7 %collective-permute-start.3 = (f32[64]{0:T(128)S(1)}, f32[64]{0:T(128)S(1)}, u32[]{:S(2)}, u32[]{:S(2)}) collective-permute-start(f32[64]{0:T(128)S(1)} %reshape.16), channel_id=1, source_target_pairs={{64,71},{65,0},{66,1},{67,2},{68,3},{69,4},{70,5},{71,6},{72,7},{7... | collective-permute-start | bytes 776 | tf_op jit(solution)/shard_map/ppermute | solution.py:16
  40.5 21.5 %collective-permute-start.10 = (bf16[4,256,256]{2,1,0:T(8,128)(2,1)S(1)}, bf16[4,256,256]{2,1,0:T(8,128)(2,1)S(1)}, u32[]{:S(2)}, u32[]{:S(2)}) collective-permute-start(bf16[4,256,256]{2,1,0:T(8,128)(2,1)S(1)} %get-tuple-element.73), channel_id=1, source_target_pairs={{65,66},{66,65},{67,68},{68,67},{69,70},{70,69},{71,0},{0,71},{1,2... | collective-permute-start | bytes 1572872 | tf_op jit(solution)/shard_map/ppermute | solution.py:16
  42.4 19.6 %collective-permute-start.11 = (bf16[4,256,256]{2,1,0:T(8,128)(2,1)S(1)}, bf16[4,256,256]{2,1,0:T(8,128)(2,1)S(1)}, u32[]{:S(2)}, u32[]{:S(2)}) collective-permute-start(bf16[4,256,256]{2,1,0:T(8,128)(2,1)S(1)} %get-tuple-element.74), channel_id=1, source_target_pairs={{64,65},{65,64},{66,67},{67,66},{68,69},{69,68},{70,71},{71,70},{0... | collective-permute-start | bytes 1572872 | tf_op jit(solution)/shard_map/ppermute | solution.py:16
  54.8 17.0 %collective-permute-start.15 = (bf16[1040,256]{1,0:T(8,128)(2,1)S(1)}, bf16[1040,256]{1,0:T(8,128)(2,1)S(1)}, u32[]{:S(2)}, u32[]{:S(2)}) collective-permute-start(bf16[1040,256]{1,0:T(8,128)(2,1)S(1)} %pad_maximum_fusion), channel_id=1, source_target_pairs={{320,379},{321,380},{322,381},{323,382},{324,383},{325,320},{326,3... | collective-permute-start | bytes 1597448 | tf_op jit(solution)/shard_map/ppermute | solution.py:16
  55.5 15.6 %collective-permute-start.16 = (bf16[4,256,256]{2,1,0:T(8,128)(2,1)S(1)}, bf16[4,256,256]{2,1,0:T(8,128)(2,1)S(1)}, u32[]{:S(2)}, u32[]{:S(2)}) collective-permute-start(bf16[4,256,256]{2,1,0:T(8,128)(2,1)S(1)} %get-tuple-element.70.env_ref), channel_id=1, source_target_pairs={{71,127},{0,64},{1,65},{2,66},{3,67},{4,68},{5,69},{6,70},{7,71},{... | collective-permute-start | bytes 1572872 | tf_op jit(solution)/shard_map/ppermute | solution.py:16
  59.1 15.4 %collective-permute-start.8 = (bf16[1040,256]{1,0:T(8,128)(2,1)S(1)}, bf16[1040,256]{1,0:T(8,128)(2,1)S(1)}, u32[]{:S(2)}, u32[]{:S(2)}) collective-permute-start(bf16[1040,256]{1,0:T(8,128)(2,1)S(1)} %collective-permute-done.5), channel_id=1, source_target_pairs={{253,69},{254,70},{255,71},{192,0},{193,1},{194,2},{195,3},{196,4}... | collective-permute-start | bytes 1597448 | tf_op jit(solution)/shard_map/ppermute | solution.py:16
  74.5 16.5 %collective-permute-start.7 = (bf16[1040,256]{1,0:T(8,128)(2,1)S(1)}, bf16[1040,256]{1,0:T(8,128)(2,1)S(1)}, u32[]{:S(2)}, u32[]{:S(2)}) collective-permute-start(bf16[1040,256]{1,0:T(8,128)(2,1)S(1)} %collective-permute-done.2), channel_id=1, source_target_pairs={{316,68},{317,69},{318,70},{319,71},{256,0},{257,1},{258,2},{259,3... | collective-permute-start | bytes 1597448 | tf_op jit(solution)/shard_map/ppermute | solution.py:16
  76.5 15.2 %collective-permute-start.19 = (bf16[1040,256]{1,0:T(8,128)(2,1)S(1)}, bf16[1040,256]{1,0:T(8,128)(2,1)S(1)}, u32[]{:S(2)}, u32[]{:S(2)}) collective-permute-start(bf16[1040,256]{1,0:T(8,128)(2,1)S(1)} %pad_maximum_fusion), channel_id=1, source_target_pairs={{384,442},{385,443},{386,444},{387,445},{388,446},{389,447},{390,3... | collective-permute-start | bytes 1597448 | tf_op jit(solution)/shard_map/ppermute | solution.py:16
  77.2 28.5 %collective-permute-start.26 = (bf16[1040,256]{1,0:T(8,128)(2,1)S(1)}, bf16[1040,256]{1,0:T(8,128)(2,1)S(1)}, u32[]{:S(2)}, u32[]{:S(2)}) collective-permute-start(bf16[1040,256]{1,0:T(8,128)(2,1)S(1)} %collective-permute-done.15), channel_id=1, source_target_pairs={{379,67},{380,68},{381,69},{382,70},{383,71},{320,0},{321,1},{322,... | collective-permute-start | bytes 1597448 | tf_op jit(solution)/shard_map/ppermute | solution.py:16
  91.0 17.8 %collective-permute-start.22 = (bf16[4,256,256]{2,1,0:T(8,128)(2,1)S(1)}, bf16[4,256,256]{2,1,0:T(8,128)(2,1)S(1)}, u32[]{:S(2)}, u32[]{:S(2)}) collective-permute-start(bf16[4,256,256]{2,1,0:T(8,128)(2,1)S(1)} %collective-permute-done.21), channel_id=1, source_target_pairs={{190,128},{191,129},{128,130},{129,131},{130,132},{131,133},{132,1... | collective-permute-start | bytes 1572872 | tf_op jit(solution)/shard_map/ppermute | solution.py:16
  91.7 21.9 %collective-permute-start.1 = (bf16[1040,256]{1,0:T(8,128)(2,1)S(1)}, bf16[1040,256]{1,0:T(8,128)(2,1)S(1)}, u32[]{:S(2)}, u32[]{:S(2)}) collective-permute-start(bf16[1040,256]{1,0:T(8,128)(2,1)S(1)} %pad_maximum_fusion), channel_id=1, source_target_pairs={{448,505},{449,506},{450,507},{451,508},{452,509},{453,510},{454,5... | collective-permute-start | bytes 1597448 | tf_op jit(solution)/shard_map/ppermute | solution.py:16
  93.2 19.1 %collective-permute-start.23 = (bf16[4,256,256]{2,1,0:T(8,128)(2,1)S(1)}, bf16[4,256,256]{2,1,0:T(8,128)(2,1)S(1)}, u32[]{:S(2)}, u32[]{:S(2)}) collective-permute-start(bf16[4,256,256]{2,1,0:T(8,128)(2,1)S(1)} %get-tuple-element.84.env_ref), channel_id=1, source_target_pairs={{69,253},{70,254},{71,255},{0,192},{1,193},{2,194},{3,195},{4,196}... | collective-permute-start | bytes 1572872 | tf_op jit(solution)/shard_map/ppermute | solution.py:16
  94.5 29.9 %collective-permute-start.25 = (bf16[1040,256]{1,0:T(8,128)(2,1)S(1)}, bf16[1040,256]{1,0:T(8,128)(2,1)S(1)}, u32[]{:S(2)}, u32[]{:S(2)}) collective-permute-start(bf16[1040,256]{1,0:T(8,128)(2,1)S(1)} %collective-permute-done.19), channel_id=1, source_target_pairs={{442,66},{443,67},{444,68},{445,69},{446,70},{447,71},{384,0},{385... | collective-permute-start | bytes 1597448 | tf_op jit(solution)/shard_map/ppermute | solution.py:16
  112.3 17.0 %collective-permute-start.32 = (bf16[4,256,256]{2,1,0:T(8,128)(2,1)S(1)}, bf16[4,256,256]{2,1,0:T(8,128)(2,1)S(1)}, u32[]{:S(2)}, u32[]{:S(2)}) collective-permute-start(bf16[4,256,256]{2,1,0:T(8,128)(2,1)S(1)} %get-tuple-element.89.env_ref), channel_id=1, source_target_pairs={{68,316},{69,317},{70,318},{71,319},{0,256},{1,257},{2,258},{3,259... | collective-permute-start | bytes 1572872 | tf_op jit(solution)/shard_map/ppermute | solution.py:16
  113.6 14.3 %collective-permute-start.31 = (bf16[4,256,256]{2,1,0:T(8,128)(2,1)S(1)}, bf16[4,256,256]{2,1,0:T(8,128)(2,1)S(1)}, u32[]{:S(2)}, u32[]{:S(2)}) collective-permute-start(bf16[4,256,256]{2,1,0:T(8,128)(2,1)S(1)} %collective-permute-done.23), channel_id=1, source_target_pairs={{253,192},{254,193},{255,194},{192,195},{193,196},{194,197},{195,1... | collective-permute-start | bytes 1572872 | tf_op jit(solution)/shard_map/ppermute | solution.py:16
  118.3 22.4 %collective-permute-start.24 = (bf16[1040,256]{1,0:T(8,128)(2,1)S(1)}, bf16[1040,256]{1,0:T(8,128)(2,1)S(1)}, u32[]{:S(2)}, u32[]{:S(2)}) collective-permute-start(bf16[1040,256]{1,0:T(8,128)(2,1)S(1)} %collective-permute-done.1), channel_id=1, source_target_pairs={{505,65},{506,66},{507,67},{508,68},{509,69},{510,70},{511,71},{44... | collective-permute-start | bytes 1597448 | tf_op jit(solution)/shard_map/ppermute | solution.py:16
  127.9 14.3 %collective-permute-start.36 = (bf16[4,256,256]{2,1,0:T(8,128)(2,1)S(1)}, bf16[4,256,256]{2,1,0:T(8,128)(2,1)S(1)}, u32[]{:S(2)}, u32[]{:S(2)}) collective-permute-start(bf16[4,256,256]{2,1,0:T(8,128)(2,1)S(1)} %get-tuple-element.101.env_ref), channel_id=1, source_target_pairs={{67,379},{68,380},{69,381},{70,382},{71,383},{0,320},{1,321},{2,32... | collective-permute-start | bytes 1572872 | tf_op jit(solution)/shard_map/ppermute | solution.py:16
  155.1 17.9 %collective-permute-start.41 = (bf16[4,256,256]{2,1,0:T(8,128)(2,1)S(1)}, bf16[4,256,256]{2,1,0:T(8,128)(2,1)S(1)}, u32[]{:S(2)}, u32[]{:S(2)}) collective-permute-start(bf16[4,256,256]{2,1,0:T(8,128)(2,1)S(1)} %get-tuple-element.107.env_ref), channel_id=1, source_target_pairs={{66,384},{67,385},{68,386},{69,387},{70,388},{71,389},{0,390},{1,3... | collective-permute-start | bytes 1572872 | tf_op jit(solution)/shard_map/ppermute | solution.py:16
  157.1 49.4 %collective-permute-start.42 = (bf16[4,256,256]{2,1,0:T(8,128)(2,1)S(1)}, bf16[4,256,256]{2,1,0:T(8,128)(2,1)S(1)}, u32[]{:S(2)}, u32[]{:S(2)}) collective-permute-start(bf16[4,256,256]{2,1,0:T(8,128)(2,1)S(1)} %get-tuple-element.113.env_ref), channel_id=1, source_target_pairs={{65,448},{66,449},{67,450},{68,451},{69,452},{70,453},{71,454},{0,... | collective-permute-start | bytes 1572872 | tf_op jit(solution)/shard_map/ppermute | solution.py:16
  162.9 53.4 %collective-permute-start.39 = (bf16[4,256,256]{2,1,0:T(8,128)(2,1)S(1)}, bf16[4,256,256]{2,1,0:T(8,128)(2,1)S(1)}, u32[]{:S(2)}, u32[]{:S(2)}) collective-permute-start(bf16[4,256,256]{2,1,0:T(8,128)(2,1)S(1)} %last.1), channel_id=1, source_target_pairs={{64,0},{65,1},{66,2},{67,3},{68,4},{69,5},{70,6},{71,7},{0,8},{1,9... | collective-permute-start | bytes 1572872 | tf_op jit(solution)/shard_map/ppermute | solution.py:16
  (23 other events, 233.1 us)

commit v7 on v6

--- a/solution.py
+++ b/solution.py
@@ -163,11 +163,15 @@
         return [((s, t), (s, (t - s) % sectors)) for t in range(sectors)]
 
     parcels = {0: blocks, 1: moved(blocks, straight_pairs(1), sectors)}
-    scales = {0: rooted, 1: moved(weights, straight_pairs(1), sectors)}
+    scales = {0: rooted}
+    for early in (1, 2):
+        scales[early] = moved(weights, straight_pairs(early), sectors)
     turned = {}
 
     def pack(after):
-        held, lying, after = lax.optimization_barrier((weights, blocks, after))
+        held, lying, after, scales[1], scales[2] = lax.optimization_barrier(
+            (weights, blocks, after, scales[1], scales[2])
+        )
         high = lax.reduce_precision(held, *ROUND)
         middle = lax.reduce_precision(held - high, *ROUND)
         low = lax.reduce_precision(held - high - middle, *ROUND)
@@ -186,6 +190,10 @@
         held, after = lax.optimization_barrier((turned[s], after))
         pairs = [((s, (t - s) % sectors), device(t - s)) for t in range(sectors)]
         return moved(held, pairs, sectors), after
+
+    def go_home(r, env):
+        pairs = [((r, (t - r) % sectors), (r, t)) for t in range(sectors)]
+        return moved(env, pairs, sectors)
 
     def part_pairs(crossing):
         pairs = []
@@ -249,18 +257,14 @@
             packed, swap = pack(swap)
             for r in range(3, sites):
                 turned[r] = moved(packed, turn_pairs(r), sectors)
-            scales[2] = moved(weights, straight_pairs(2), sectors)
-        elif s < sites - 2:
+        else:
             pairs = [(device(t - s), (s, (t - s) % sectors)) for t in range(sectors)]
             raised[s] = moved(current, pairs, sectors)
-        else:
-            homed[s] = moved(current, [(device(t - s), (s, t)) for t in range(sectors)], sectors)
         if s - 2 in homed and s < sites - 1:
             stay, homed[s - 2] = lax.optimization_barrier((stay, homed[s - 2]))
         if s - 1 in raised:
             stay, risen = lax.optimization_barrier((stay, raised[s - 1]))
-            pairs = [((s - 1, (t - s + 1) % sectors), (s - 1, t)) for t in range(sectors)]
-            homed[s - 1] = moved(risen, pairs, sectors)
+            homed[s - 1] = go_home(s - 1, risen)
         for ahead in (2, 3) if s == 0 else (s + 3,):
             if ahead < sites:
                 parcels[ahead], stay = fetch(ahead, stay)
@@ -273,6 +277,7 @@
         compiler_params=PARAMS,
         name="last",
     )(cross, swap, stay)
+    homed[sites - 1] = go_home(sites - 1, raised[sites - 1])
     homed[0] = moved(ended, [(device(t - sites), (0, t)) for t in range(sectors)], sectors)
     out = pl.pallas_call(
         functools.partial(pick_kernel, sites),

time: 219 us -> 218 us (level)
  the two profiles are of different devices: /device:TPU:7 before, /device:TPU:59 now
where the time goes in v7:
time: 218 us; the launch traced here: 217 us
  starting transfers between devices  100 us (46%)
  waiting for transfers between devices  84 us (39%)
  Pallas kernels  29.6 us (14%)
    ppermute x45, starting transfers between devices, moved(): return lax.ppermute(x, AXES, flat)  100 us
    ppermute x45, waiting for transfers between devices, moved(): return lax.ppermute(x, AXES, flat)  84 us
    pallas_call x8, Pallas kernels, local(): pl.pallas_call(stay_kernel, out_shape=block_shape, in_specs=[SMEM, VMEM,...  12.3 us
    pallas_call x7, Pallas kernels, local(): pl.pallas_call(lead_kernel, out_shape=(block_shape,) * 3, in_specs=[SMEM,...  12.1 us
  transfers between devices with their start and end apart: 45, of which 4 were waited for; matrix products, arithmetic and copies ran while one was open for 0% of the time, Pallas kernels for 11%

profile of v7, /device:TPU:59, one launch (start us, length us, event | category | flops | bytes accessed | tf_op | source)
XLA Modules:
  0.0 216.8 jit_solution(816293586055938074)
XLA Ops:
  1.3 4.1 %first.1 = (bf16[4,256,256]{2,1,0:T(8,128)(2,1)}, bf16[4,256,256]{2,1,0:T(8,128)(2,1)}) custom-call(s32[1]{0:T(128)} %bitcast.1.p_ref, f32[4,4,4]{2,1,0:T(4,128)} %bitcast.39, s32[4,4,4]{2,1,0:T(4,128)} %bitcast.38, s32[4]{0:T(128)} %get-tuple-element.130.couple_ref, bf16[4,256,256]{2,1,0:T(8,128)(2,1)} %bitcast.36, bf16[1024,256]{1,0:T(8,128)(2,1)} %bitcast.31), custom_call_target="tpu_custom_call" | custom-call | flops 536870912 | bytes 2097152 | tf_op jit(solution)/shard_map/first/pallas_call | solution.py:213
  10.8 1.5 stay.8.stay_ref
  13.1 1.7 lead.7
  18.3 1.5 stay.9.stay_ref
  19.9 1.7 lead.8
  23.1 1.5 stay.10.stay_ref
  28.2 1.7 lead.9
  31.4 1.5 stay.11.stay_ref
  33.7 12.2 %collective-permute-start.3 = (bf16[1040,256]{1,0:T(8,128)(2,1)S(1)}, bf16[1040,256]{1,0:T(8,128)(2,1)S(1)}, u32[]{:S(2)}, u32[]{:S(2)}) collective-permute-start(bf16[1040,256]{1,0:T(8,128)(2,1)S(1)} %pad_maximum_fusion), channel_id=1, source_target_pairs={{448,505},{449,506},{450,507},{451,508},{452,509},{453,510},{454,5... | collective-permute-start | bytes 1597448 | tf_op jit(solution)/shard_map/ppermute | solution.py:16
  47.4 1.7 lead.10
  50.6 1.5 stay.12.stay_ref
  52.9 3.9 %collective-permute-done.3 = bf16[1040,256]{1,0:T(8,128)(2,1)S(1)} collective-permute-done((bf16[1040,256]{1,0:T(8,128)(2,1)S(1)}, bf16[1040,256]{1,0:T(8,128)(2,1)S(1)}, u32[]{:S(2)}, u32[]{:S(2)}) %collective-permute-start.3) | collective-permute-done | bytes 532512 | tf_op jit(solution)/shard_map/ppermute | solution.py:16
  57.5 56.4 %collective-permute-start.24 = (bf16[1040,256]{1,0:T(8,128)(2,1)S(1)}, bf16[1040,256]{1,0:T(8,128)(2,1)S(1)}, u32[]{:S(2)}, u32[]{:S(2)}) collective-permute-start(bf16[1040,256]{1,0:T(8,128)(2,1)S(1)} %collective-permute-done.3), channel_id=1, source_target_pairs={{505,65},{506,66},{507,67},{508,68},{509,69},{510,70},{511,71},{44... | collective-permute-start | bytes 1597448 | tf_op jit(solution)/shard_map/ppermute | solution.py:16
  114.0 1.7 lead.11
  117.1 1.5 stay.13.stay_ref
  120.1 1.7 lead.12
  123.3 1.9 collective-permute-done.24.a_ref
  125.8 1.5 stay.14.stay_ref
  127.4 1.7 lead.13
  130.6 1.3 collective-permute-start.43
  132.6 1.5 stay.15.stay_ref
  135.8 62.4 %collective-permute-done.43 = bf16[4,256,256]{2,1,0:T(8,128)(2,1)S(1)} collective-permute-done((bf16[4,256,256]{2,1,0:T(8,128)(2,1)S(1)}, bf16[4,256,256]{2,1,0:T(8,128)(2,1)S(1)}, u32[]{:S(2)}, u32[]{:S(2)}) %collective-permute-start.43) | collective-permute-done | bytes 524320 | tf_op jit(solution)/shard_map/ppermute | solution.py:16
  198.2 1.9 collective-permute-start.44
  200.1 15.7 %collective-permute-done.44.refs_7_ = bf16[4,256,256]{2,1,0:T(8,128)(2,1)S(1)} collective-permute-done((bf16[4,256,256]{2,1,0:T(8,128)(2,1)S(1)}, bf16[4,256,256]{2,1,0:T(8,128)(2,1)S(1)}, u32[]{:S(2)}, u32[]{:S(2)}) %collective-permute-start.44) | collective-permute-done | bytes 524320 | tf_op jit(solution)/shard_map/ppermute | solution.py:16
  (110 shorter events, 31.4 us)
Async XLA Ops:
  10.1 7.6 %collective-permute-start.4 = (bf16[1040,256]{1,0:T(8,128)(2,1)S(1)}, bf16[1040,256]{1,0:T(8,128)(2,1)S(1)}, u32[]{:S(2)}, u32[]{:S(2)}) collective-permute-start(bf16[1040,256]{1,0:T(8,128)(2,1)S(1)} %pad_maximum_fusion), channel_id=1, source_target_pairs={{256,316},{257,317},{258,318},{259,319},{260,256},{261,257},{262,2... | collective-permute-start | bytes 1597448 | tf_op jit(solution)/shard_map/ppermute | solution.py:16
  16.2 9.1 %collective-permute-start.15 = (bf16[1040,256]{1,0:T(8,128)(2,1)S(1)}, bf16[1040,256]{1,0:T(8,128)(2,1)S(1)}, u32[]{:S(2)}, u32[]{:S(2)}) collective-permute-start(bf16[1040,256]{1,0:T(8,128)(2,1)S(1)} %pad_maximum_fusion), channel_id=1, source_target_pairs={{320,379},{321,380},{322,381},{323,382},{324,383},{325,320},{326,3... | collective-permute-start | bytes 1597448 | tf_op jit(solution)/shard_map/ppermute | solution.py:16
  16.9 7.7 %collective-permute-start.16 = (bf16[4,256,256]{2,1,0:T(8,128)(2,1)S(1)}, bf16[4,256,256]{2,1,0:T(8,128)(2,1)S(1)}, u32[]{:S(2)}, u32[]{:S(2)}) collective-permute-start(bf16[4,256,256]{2,1,0:T(8,128)(2,1)S(1)} %get-tuple-element.75.env_ref), channel_id=1, source_target_pairs={{71,127},{0,64},{1,65},{2,66},{3,67},{4,68},{5,69},{6,70},{7,71},{... | collective-permute-start | bytes 1572872 | tf_op jit(solution)/shard_map/ppermute | solution.py:16
  17.6 8.4 %collective-permute-start.9 = (bf16[1040,256]{1,0:T(8,128)(2,1)S(1)}, bf16[1040,256]{1,0:T(8,128)(2,1)S(1)}, u32[]{:S(2)}, u32[]{:S(2)}) collective-permute-start(bf16[1040,256]{1,0:T(8,128)(2,1)S(1)} %collective-permute-done.6), channel_id=1, source_target_pairs={{253,69},{254,70},{255,71},{192,0},{193,1},{194,2},{195,3},{196,4}... | collective-permute-start | bytes 1597448 | tf_op jit(solution)/shard_map/ppermute | solution.py:16
  26.1 6.9 %collective-permute-start.8 = (bf16[1040,256]{1,0:T(8,128)(2,1)S(1)}, bf16[1040,256]{1,0:T(8,128)(2,1)S(1)}, u32[]{:S(2)}, u32[]{:S(2)}) collective-permute-start(bf16[1040,256]{1,0:T(8,128)(2,1)S(1)} %collective-permute-done.4), channel_id=1, source_target_pairs={{316,68},{317,69},{318,70},{319,71},{256,0},{257,1},{258,2},{259,3... | collective-permute-start | bytes 1597448 | tf_op jit(solution)/shard_map/ppermute | solution.py:16
  27.5 21.7 %collective-permute-start.26 = (bf16[1040,256]{1,0:T(8,128)(2,1)S(1)}, bf16[1040,256]{1,0:T(8,128)(2,1)S(1)}, u32[]{:S(2)}, u32[]{:S(2)}) collective-permute-start(bf16[1040,256]{1,0:T(8,128)(2,1)S(1)} %collective-permute-done.15), channel_id=1, source_target_pairs={{379,67},{380,68},{381,69},{382,70},{383,71},{320,0},{321,1},{322,... | collective-permute-start | bytes 1597448 | tf_op jit(solution)/shard_map/ppermute | solution.py:16
  30.0 15.9 %collective-permute-start.17 = (bf16[4,256,256]{2,1,0:T(8,128)(2,1)S(1)}, bf16[4,256,256]{2,1,0:T(8,128)(2,1)S(1)}, u32[]{:S(2)}, u32[]{:S(2)}) collective-permute-start(bf16[4,256,256]{2,1,0:T(8,128)(2,1)S(1)} %get-tuple-element.88), channel_id=1, source_target_pairs={{65,66},{66,65},{67,68},{68,67},{69,70},{70,69},{71,0},{0,71},{1,2... | collective-permute-start | bytes 1572872 | tf_op jit(solution)/shard_map/ppermute | solution.py:16
  30.7 15.9 %collective-permute-start.18 = (bf16[4,256,256]{2,1,0:T(8,128)(2,1)S(1)}, bf16[4,256,256]{2,1,0:T(8,128)(2,1)S(1)}, u32[]{:S(2)}, u32[]{:S(2)}) collective-permute-start(bf16[4,256,256]{2,1,0:T(8,128)(2,1)S(1)} %get-tuple-element.89), channel_id=1, source_target_pairs={{64,65},{65,64},{66,67},{67,66},{68,69},{69,68},{70,71},{71,70},{0... | collective-permute-start | bytes 1572872 | tf_op jit(solution)/shard_map/ppermute | solution.py:16
  32.9 17.0 %collective-permute-start.22 = (bf16[4,256,256]{2,1,0:T(8,128)(2,1)S(1)}, bf16[4,256,256]{2,1,0:T(8,128)(2,1)S(1)}, u32[]{:S(2)}, u32[]{:S(2)}) collective-permute-start(bf16[4,256,256]{2,1,0:T(8,128)(2,1)S(1)} %collective-permute-done.21), channel_id=1, source_target_pairs={{190,128},{191,129},{128,130},{129,131},{130,132},{131,133},{132,1... | collective-permute-start | bytes 1572872 | tf_op jit(solution)/shard_map/ppermute | solution.py:16
  33.7 23.1 %collective-permute-start.3 = (bf16[1040,256]{1,0:T(8,128)(2,1)S(1)}, bf16[1040,256]{1,0:T(8,128)(2,1)S(1)}, u32[]{:S(2)}, u32[]{:S(2)}) collective-permute-start(bf16[1040,256]{1,0:T(8,128)(2,1)S(1)} %pad_maximum_fusion), channel_id=1, source_target_pairs={{448,505},{449,506},{450,507},{451,508},{452,509},{453,510},{454,5... | collective-permute-start | bytes 1597448 | tf_op jit(solution)/shard_map/ppermute | solution.py:16
  46.6 69.8 %collective-permute-start.25 = (bf16[1040,256]{1,0:T(8,128)(2,1)S(1)}, bf16[1040,256]{1,0:T(8,128)(2,1)S(1)}, u32[]{:S(2)}, u32[]{:S(2)}) collective-permute-start(bf16[1040,256]{1,0:T(8,128)(2,1)S(1)} %collective-permute-done.19), channel_id=1, source_target_pairs={{442,66},{443,67},{444,68},{445,69},{446,70},{447,71},{384,0},{385... | collective-permute-start | bytes 1597448 | tf_op jit(solution)/shard_map/ppermute | solution.py:16
  49.2 8.3 %collective-permute-start.27 = (bf16[4,256,256]{2,1,0:T(8,128)(2,1)S(1)}, bf16[4,256,256]{2,1,0:T(8,128)(2,1)S(1)}, u32[]{:S(2)}, u32[]{:S(2)}) collective-permute-start(bf16[4,256,256]{2,1,0:T(8,128)(2,1)S(1)} %get-tuple-element.102), channel_id=1, source_target_pairs={{65,66},{66,65},{67,68},{68,67},{69,70},{70,69},{71,0},{0,71},{1,2... | collective-permute-start | bytes 1572872 | tf_op jit(solution)/shard_map/ppermute | solution.py:16
  49.9 64.0 %collective-permute-start.28 = (bf16[4,256,256]{2,1,0:T(8,128)(2,1)S(1)}, bf16[4,256,256]{2,1,0:T(8,128)(2,1)S(1)}, u32[]{:S(2)}, u32[]{:S(2)}) collective-permute-start(bf16[4,256,256]{2,1,0:T(8,128)(2,1)S(1)} %get-tuple-element.103), channel_id=1, source_target_pairs={{64,65},{65,64},{66,67},{67,66},{68,69},{69,68},{70,71},{71,70},{0... | collective-permute-start | bytes 1572872 | tf_op jit(solution)/shard_map/ppermute | solution.py:16
  52.2 67.2 %collective-permute-start.32 = (bf16[4,256,256]{2,1,0:T(8,128)(2,1)S(1)}, bf16[4,256,256]{2,1,0:T(8,128)(2,1)S(1)}, u32[]{:S(2)}, u32[]{:S(2)}) collective-permute-start(bf16[4,256,256]{2,1,0:T(8,128)(2,1)S(1)} %get-tuple-element.95.env_ref), channel_id=1, source_target_pairs={{68,316},{69,317},{70,318},{71,319},{0,256},{1,257},{2,258},{3,259... | collective-permute-start | bytes 1572872 | tf_op jit(solution)/shard_map/ppermute | solution.py:16
  56.8 61.9 %collective-permute-start.31 = (bf16[4,256,256]{2,1,0:T(8,128)(2,1)S(1)}, bf16[4,256,256]{2,1,0:T(8,128)(2,1)S(1)}, u32[]{:S(2)}, u32[]{:S(2)}) collective-permute-start(bf16[4,256,256]{2,1,0:T(8,128)(2,1)S(1)} %collective-permute-done.23), channel_id=1, source_target_pairs={{253,192},{254,193},{255,194},{192,195},{193,196},{194,197},{195,1... | collective-permute-start | bytes 1572872 | tf_op jit(solution)/shard_map/ppermute | solution.py:16
  57.5 67.6 %collective-permute-start.24 = (bf16[1040,256]{1,0:T(8,128)(2,1)S(1)}, bf16[1040,256]{1,0:T(8,128)(2,1)S(1)}, u32[]{:S(2)}, u32[]{:S(2)}) collective-permute-start(bf16[1040,256]{1,0:T(8,128)(2,1)S(1)} %collective-permute-done.3), channel_id=1, source_target_pairs={{505,65},{506,66},{507,67},{508,68},{509,69},{510,70},{511,71},{44... | collective-permute-start | bytes 1597448 | tf_op jit(solution)/shard_map/ppermute | solution.py:16
  118.7 8.7 %collective-permute-start.36 = (bf16[4,256,256]{2,1,0:T(8,128)(2,1)S(1)}, bf16[4,256,256]{2,1,0:T(8,128)(2,1)S(1)}, u32[]{:S(2)}, u32[]{:S(2)}) collective-permute-start(bf16[4,256,256]{2,1,0:T(8,128)(2,1)S(1)} %get-tuple-element.107.env_ref), channel_id=1, source_target_pairs={{67,379},{68,380},{69,381},{70,382},{71,383},{0,320},{1,321},{2,32... | collective-permute-start | bytes 1572872 | tf_op jit(solution)/shard_map/ppermute | solution.py:16
  119.4 8.0 %collective-permute-start.35 = (bf16[4,256,256]{2,1,0:T(8,128)(2,1)S(1)}, bf16[4,256,256]{2,1,0:T(8,128)(2,1)S(1)}, u32[]{:S(2)}, u32[]{:S(2)}) collective-permute-start(bf16[4,256,256]{2,1,0:T(8,128)(2,1)S(1)} %collective-permute-done.32), channel_id=1, source_target_pairs={{316,256},{317,257},{318,258},{319,259},{256,260},{257,261},{258,2... | collective-permute-start | bytes 1572872 | tf_op jit(solution)/shard_map/ppermute | solution.py:16
  125.1 9.0 %collective-permute-start.39 = (bf16[4,256,256]{2,1,0:T(8,128)(2,1)S(1)}, bf16[4,256,256]{2,1,0:T(8,128)(2,1)S(1)}, u32[]{:S(2)}, u32[]{:S(2)}) collective-permute-start(bf16[4,256,256]{2,1,0:T(8,128)(2,1)S(1)} %get-tuple-element.113.env_ref), channel_id=1, source_target_pairs={{66,442},{67,443},{68,444},{69,445},{70,446},{71,447},{0,384},{1,3... | collective-permute-start | bytes 1572872 | tf_op jit(solution)/shard_map/ppermute | solution.py:16
  130.6 67.6 %collective-permute-start.43 = (bf16[4,256,256]{2,1,0:T(8,128)(2,1)S(1)}, bf16[4,256,256]{2,1,0:T(8,128)(2,1)S(1)}, u32[]{:S(2)}, u32[]{:S(2)}) collective-permute-start(bf16[4,256,256]{2,1,0:T(8,128)(2,1)S(1)} %get-tuple-element.119.env_ref), channel_id=1, source_target_pairs={{65,505},{66,506},{67,507},{68,508},{69,509},{70,510},{71,511},{0,... | collective-permute-start | bytes 1572872 | tf_op jit(solution)/shard_map/ppermute | solution.py:16
  131.9 68.2 %collective-permute-start.41 = (bf16[4,256,256]{2,1,0:T(8,128)(2,1)S(1)}, bf16[4,256,256]{2,1,0:T(8,128)(2,1)S(1)}, u32[]{:S(2)}, u32[]{:S(2)}) collective-permute-start(bf16[4,256,256]{2,1,0:T(8,128)(2,1)S(1)} %collective-permute-done.36), channel_id=1, source_target_pairs={{379,320},{380,321},{381,322},{382,323},{383,324},{320,325},{321,3... | collective-permute-start | bytes 1572872 | tf_op jit(solution)/shard_map/ppermute | solution.py:16
  134.1 66.0 %collective-permute-start.42 = (bf16[4,256,256]{2,1,0:T(8,128)(2,1)S(1)}, bf16[4,256,256]{2,1,0:T(8,128)(2,1)S(1)}, u32[]{:S(2)}, u32[]{:S(2)}) collective-permute-start(bf16[4,256,256]{2,1,0:T(8,128)(2,1)S(1)} %collective-permute-done.39), channel_id=1, source_target_pairs={{442,384},{443,385},{444,386},{445,387},{446,388},{447,389},{384,3... | collective-permute-start | bytes 1572872 | tf_op jit(solution)/shard_map/ppermute | solution.py:16
  135.1 65.1 %collective-permute-start.40 = (bf16[4,256,256]{2,1,0:T(8,128)(2,1)S(1)}, bf16[4,256,256]{2,1,0:T(8,128)(2,1)S(1)}, u32[]{:S(2)}, u32[]{:S(2)}) collective-permute-start(bf16[4,256,256]{2,1,0:T(8,128)(2,1)S(1)} %last.1), channel_id=1, source_target_pairs={{64,0},{65,1},{66,2},{67,3},{68,4},{69,5},{70,6},{71,7},{0,8},{1,9... | collective-permute-start | bytes 1572872 | tf_op jit(solution)/shard_map/ppermute | solution.py:16
  198.2 17.6 %collective-permute-start.44 = (bf16[4,256,256]{2,1,0:T(8,128)(2,1)S(1)}, bf16[4,256,256]{2,1,0:T(8,128)(2,1)S(1)}, u32[]{:S(2)}, u32[]{:S(2)}) collective-permute-start(bf16[4,256,256]{2,1,0:T(8,128)(2,1)S(1)} %collective-permute-done.43), channel_id=1, source_target_pairs={{505,448},{506,449},{507,450},{508,451},{509,452},{510,453},{511,4... | collective-permute-start | bytes 1572872 | tf_op jit(solution)/shard_map/ppermute | solution.py:16
  (25 other events, 117.5 us)

commit v8 on v2

--- a/solution.py
+++ b/solution.py
@@ -285,8 +285,9 @@
         functools.partial(pick_kernel, 3),
         out_shape=block_shape,
         in_specs=[SMEM, VMEM, ANY, ANY],
-        out_specs=ANY,
+        out_specs=VMEM,
         scratch_shapes=[pltpu.SemaphoreType.DMA],
+        compiler_params=PARAMS,
         name="pick",
     )(
         jnp.stack([jnp.where(row == 1, 1, jnp.where(row == late, 2, 0))]),

time: 207 us -> 193 us (0.932)
  the two profiles are of different devices: /device:TPU:10 before, /device:TPU:50 now
where the time goes in v8:
time: 193 us; the launch traced here: 192 us
  waiting for transfers between devices  79.7 us (41%)
  starting transfers between devices  78.4 us (41%)
  Pallas kernels  28.1 us (15%)
  local copies, waits for them, and re-layouts  3.09 us (2%)
  other arithmetic  2.16 us (1%)
    ppermute x34, waiting for transfers between devices, moved(): return lax.ppermute(x, AXES, flat)  79.7 us
    ppermute x34, starting transfers between devices, moved(): return lax.ppermute(x, AXES, flat)  78.4 us
    pallas_call x8, Pallas kernels, local(): pl.pallas_call(stay_kernel, out_shape=block_shape, in_specs=[SMEM, VMEM,...  12.3 us
    pallas_call x7, Pallas kernels, local(): pl.pallas_call(lead_kernel, out_shape=(block_shape,) * 3, in_specs=[SMEM,...  12.3 us
  transfers between devices with their start and end apart: 34, of which 4 were waited for; matrix products, arithmetic and copies ran while one was open for 0% of the time, Pallas kernels for 14%

profile of v8, /device:TPU:50, one launch (start us, length us, event | category | flops | bytes accessed | tf_op | source)
XLA Modules:
  0.0 192.4 jit_solution(11999293429270341224)
XLA Ops:
  6.5 2.0 %first.1 = (bf16[4,256,256]{2,1,0:T(8,128)(2,1)}, bf16[4,256,256]{2,1,0:T(8,128)(2,1)S(1)}) custom-call(s32[2]{0:T(128)S(1)} %pad_add_fusion.3.p_ref, f32[64]{0:T(128)S(1)} %reshape.15.w_ref, bf16[4,256,256]{2,1,0:T(8,128)(2,1)S(1)} %bitcast.44, bf16[1024,256]{1,0:T(8,128)(2,1)S(1)} %bitcast.41), custom_call_target="tpu_custom_call" | custom-call | flops 536870912 | bytes 2097152 | tf_op jit(solution)/shard_map/first/pallas_call | solution.py:212
  10.1 1.5 stay.8.stay_ref
  13.0 11.9 %collective-permute-start.1 = (bf16[1040,256]{1,0:T(8,128)(2,1)S(1)}, bf16[1040,256]{1,0:T(8,128)(2,1)S(1)}, u32[]{:S(2)}, u32[]{:S(2)}) collective-permute-start(bf16[1040,256]{1,0:T(8,128)(2,1)S(1)} %pad_maximum_fusion), channel_id=1, source_target_pairs={{192,253},{193,254},{194,255},{195,192},{196,193},{197,194},{198,1... | collective-permute-start | bytes 1597448 | tf_op jit(solution)/shard_map/ppermute | solution.py:17
  24.9 1.7 lead.7
  28.1 1.5 stay.9.stay_ref
  29.6 6.6 %collective-permute-done.1 = bf16[1040,256]{1,0:T(8,128)(2,1)S(1)} collective-permute-done((bf16[1040,256]{1,0:T(8,128)(2,1)S(1)}, bf16[1040,256]{1,0:T(8,128)(2,1)S(1)}, u32[]{:S(2)}, u32[]{:S(2)}) %collective-permute-start.1) | collective-permute-done | bytes 532512 | tf_op jit(solution)/shard_map/ppermute | solution.py:17
  37.7 1.7 lead.8
  41.5 1.5 stay.10.stay_ref
  43.8 1.7 lead.9
  47.0 1.5 stay.11.stay_ref
  50.0 1.9 lead.10
  53.3 1.5 stay.12.stay_ref
  55.6 42.6 %collective-permute-start.22 = (bf16[1040,256]{1,0:T(8,128)(2,1)S(1)}, bf16[1040,256]{1,0:T(8,128)(2,1)S(1)}, u32[]{:S(2)}, u32[]{:S(2)}) collective-permute-start(bf16[1040,256]{1,0:T(8,128)(2,1)S(1)} %collective-permute-done.1), channel_id=1, source_target_pairs={{442,66},{443,67},{444,68},{445,69},{446,70},{447,71},{384,0},{385... | collective-permute-start | bytes 1597448 | tf_op jit(solution)/shard_map/ppermute | solution.py:17
  98.2 1.7 lead.11
  101.4 1.5 stay.13.stay_ref
  103.6 3.3 %collective-permute-done.22.a_ref = bf16[1040,256]{1,0:T(8,128)(2,1)S(1)} collective-permute-done((bf16[1040,256]{1,0:T(8,128)(2,1)S(1)}, bf16[1040,256]{1,0:T(8,128)(2,1)S(1)}, u32[]{:S(2)}, u32[]{:S(2)}) %collective-permute-start.22) | collective-permute-done | bytes 532512 | tf_op jit(solution)/shard_map/ppermute | solution.py:17
  107.7 1.7 lead.12
  110.8 1.5 stay.14.stay_ref
  112.4 1.3 collective-permute-start.30
  113.7 1.7 lead.13
  117.6 1.5 stay.15.stay_ref
  119.1 54.1 %collective-permute-done.30.refs_4_ = bf16[4,256,256]{2,1,0:T(8,128)(2,1)S(1)} collective-permute-done((bf16[4,256,256]{2,1,0:T(8,128)(2,1)S(1)}, bf16[4,256,256]{2,1,0:T(8,128)(2,1)S(1)}, u32[]{:S(2)}, u32[]{:S(2)}) %collective-permute-start.30) | collective-permute-done | bytes 524320 | tf_op jit(solution)/shard_map/ppermute | solution.py:17
  173.9 1.9 collective-permute-start.31
  175.8 15.6 %collective-permute-done.31.refs_0_ = bf16[4,256,256]{2,1,0:T(8,128)(2,1)S(1)} collective-permute-done((bf16[4,256,256]{2,1,0:T(8,128)(2,1)S(1)}, bf16[4,256,256]{2,1,0:T(8,128)(2,1)S(1)}, u32[]{:S(2)}, u32[]{:S(2)}) %collective-permute-start.31) | collective-permute-done | bytes 524320 | tf_op jit(solution)/shard_map/ppermute | solution.py:17
  (98 shorter events, 27.5 us)
Async XLA Ops:
  1.6 10.6 %collective-permute-start = (f32[64]{0:T(128)S(1)}, f32[64]{0:T(128)S(1)}, u32[]{:S(2)}, u32[]{:S(2)}) collective-permute-start(f32[64]{0:T(128)S(1)} %reshape.15.w_ref), channel_id=1, source_target_pairs={{64,71},{65,0},{66,1},{67,2},{68,3},{69,4},{70,5},{71,6},{72,7},{7... | collective-permute-start | bytes 776 | tf_op jit(solution)/shard_map/ppermute | solution.py:17
  2.3 34.7 %collective-permute-start.6 = (f32[64]{0:T(128)S(1)}, f32[64]{0:T(128)S(1)}, u32[]{:S(2)}, u32[]{:S(2)}) collective-permute-start(f32[64]{0:T(128)S(1)} %reshape.15.w_ref), channel_id=1, source_target_pairs={{128,70},{129,71},{130,0},{131,1},{132,2},{133,3},{134,4},{135,5},... | collective-permute-start | bytes 776 | tf_op jit(solution)/shard_map/ppermute | solution.py:17
  2.9 22.0 %collective-permute-start.4 = (bf16[1024,256]{1,0:T(8,128)(2,1)}, bf16[1024,256]{1,0:T(8,128)(2,1)S(1)}, u32[]{:S(2)}, u32[]{:S(2)}) collective-permute-start(bf16[1024,256]{1,0:T(8,128)(2,1)} %bitcast.39), channel_id=1, source_target_pairs={{64,71},{65,0},{66,1},{67,2},{68,3},{69,4},{70,5},{71,6},{72,7},{7... | collective-permute-start | bytes 1572872 | tf_op jit(solution)/shard_map/ppermute | solution.py:17
  3.6 34.0 %collective-permute-start.9 = (bf16[1024,256]{1,0:T(8,128)(2,1)}, bf16[1024,256]{1,0:T(8,128)(2,1)S(1)}, u32[]{:S(2)}, u32[]{:S(2)}) collective-permute-start(bf16[1024,256]{1,0:T(8,128)(2,1)} %bitcast.40), channel_id=1, source_target_pairs={{128,70},{129,71},{130,0},{131,1},{132,2},{133,3},{134,4},{135,5},... | collective-permute-start | bytes 1572872 | tf_op jit(solution)/shard_map/ppermute | solution.py:17
  12.2 12.7 %collective-permute-start.3 = (bf16[4,256,256]{2,1,0:T(8,128)(2,1)}, bf16[4,256,256]{2,1,0:T(8,128)(2,1)S(1)}, u32[]{:S(2)}, u32[]{:S(2)}) collective-permute-start(bf16[4,256,256]{2,1,0:T(8,128)(2,1)} %copy-done.4), channel_id=1, source_target_pairs={{0,1},{1,0},{2,3},{3,2},{4,5},{5,4},{6,7},{7,6},{8,9},{9,8},{10,11... | collective-permute-start | bytes 1572872 | tf_op jit(solution)/shard_map/ppermute | solution.py:17
  13.0 23.2 %collective-permute-start.1 = (bf16[1040,256]{1,0:T(8,128)(2,1)S(1)}, bf16[1040,256]{1,0:T(8,128)(2,1)S(1)}, u32[]{:S(2)}, u32[]{:S(2)}) collective-permute-start(bf16[1040,256]{1,0:T(8,128)(2,1)S(1)} %pad_maximum_fusion), channel_id=1, source_target_pairs={{192,253},{193,254},{194,255},{195,192},{196,193},{197,194},{198,1... | collective-permute-start | bytes 1597448 | tf_op jit(solution)/shard_map/ppermute | solution.py:17
  26.7 11.0 %collective-permute-start.7 = (bf16[4,256,256]{2,1,0:T(8,128)(2,1)S(1)}, bf16[4,256,256]{2,1,0:T(8,128)(2,1)S(1)}, u32[]{:S(2)}, u32[]{:S(2)}) collective-permute-start(bf16[4,256,256]{2,1,0:T(8,128)(2,1)S(1)} %get-tuple-element.56), channel_id=1, source_target_pairs={{71,0},{0,71},{1,2},{2,1},{3,4},{4,3},{5,6},{6,5},{7,8},{8,7},{9,1... | collective-permute-start | bytes 1572872 | tf_op jit(solution)/shard_map/ppermute | solution.py:17
  27.4 10.3 %collective-permute-start.8 = (bf16[4,256,256]{2,1,0:T(8,128)(2,1)S(1)}, bf16[4,256,256]{2,1,0:T(8,128)(2,1)S(1)}, u32[]{:S(2)}, u32[]{:S(2)}) collective-permute-start(bf16[4,256,256]{2,1,0:T(8,128)(2,1)S(1)} %get-tuple-element.57), channel_id=1, source_target_pairs={{71,70},{0,1},{1,0},{2,3},{3,2},{4,5},{5,4},{6,7},{7,6},{8,9},{9,8... | collective-permute-start | bytes 1572872 | tf_op jit(solution)/shard_map/ppermute | solution.py:17
  36.2 139.6 %collective-permute-start.32 = (bf16[4,256,256]{2,1,0:T(8,128)(2,1)S(1)}, bf16[4,256,256]{2,1,0:T(8,128)(2,1)S(1)}, u32[]{:S(2)}, u32[]{:S(2)}) collective-permute-start(bf16[4,256,256]{2,1,0:T(8,128)(2,1)S(1)} %get-tuple-element.54.env_ref), channel_id=1, source_target_pairs={{71,64},{0,65},{1,66},{2,67},{3,68},{4,69},{5,70},{6,71},{7,72},{8... | collective-permute-start | bytes 1572872 | tf_op jit(solution)/shard_map/ppermute | solution.py:17
  40.8 7.7 %collective-permute-start.12 = (bf16[4,256,256]{2,1,0:T(8,128)(2,1)S(1)}, bf16[4,256,256]{2,1,0:T(8,128)(2,1)S(1)}, u32[]{:S(2)}, u32[]{:S(2)}) collective-permute-start(bf16[4,256,256]{2,1,0:T(8,128)(2,1)S(1)} %get-tuple-element.61.env_ref), channel_id=1, source_target_pairs={{70,190},{71,191},{0,128},{1,129},{2,130},{3,131},{4,132},{5,133},... | collective-permute-start | bytes 1572872 | tf_op jit(solution)/shard_map/ppermute | solution.py:17
  48.5 6.3 %collective-permute-start.19 = (bf16[4,256,256]{2,1,0:T(8,128)(2,1)S(1)}, bf16[4,256,256]{2,1,0:T(8,128)(2,1)S(1)}, u32[]{:S(2)}, u32[]{:S(2)}) collective-permute-start(bf16[4,256,256]{2,1,0:T(8,128)(2,1)S(1)} %get-tuple-element.63.env_ref), channel_id=1, source_target_pairs={{69,253},{70,254},{71,255},{0,192},{1,193},{2,194},{3,195},{4,196}... | collective-permute-start | bytes 1572872 | tf_op jit(solution)/shard_map/ppermute | solution.py:17
  51.9 46.3 %collective-permute-start.17 = (bf16[4,256,256]{2,1,0:T(8,128)(2,1)S(1)}, bf16[4,256,256]{2,1,0:T(8,128)(2,1)S(1)}, u32[]{:S(2)}, u32[]{:S(2)}) collective-permute-start(bf16[4,256,256]{2,1,0:T(8,128)(2,1)S(1)} %get-tuple-element.70), channel_id=1, source_target_pairs={{68,67},{69,70},{70,69},{71,0},{0,71},{1,2},{2,1},{3,4},{4,3},{5,6... | collective-permute-start | bytes 1572872 | tf_op jit(solution)/shard_map/ppermute | solution.py:17
  52.6 45.6 %collective-permute-start.18 = (bf16[4,256,256]{2,1,0:T(8,128)(2,1)S(1)}, bf16[4,256,256]{2,1,0:T(8,128)(2,1)S(1)}, u32[]{:S(2)}, u32[]{:S(2)}) collective-permute-start(bf16[4,256,256]{2,1,0:T(8,128)(2,1)S(1)} %get-tuple-element.71), channel_id=1, source_target_pairs={{68,69},{69,68},{70,71},{71,70},{0,1},{1,0},{2,3},{3,2},{4,5},{5,4... | collective-permute-start | bytes 1572872 | tf_op jit(solution)/shard_map/ppermute | solution.py:17
  54.9 48.1 %collective-permute-start.20 = (bf16[4,256,256]{2,1,0:T(8,128)(2,1)S(1)}, bf16[4,256,256]{2,1,0:T(8,128)(2,1)S(1)}, u32[]{:S(2)}, u32[]{:S(2)}) collective-permute-start(bf16[4,256,256]{2,1,0:T(8,128)(2,1)S(1)} %get-tuple-element.72.env_ref), channel_id=1, source_target_pairs={{68,316},{69,317},{70,318},{71,319},{0,256},{1,257},{2,258},{3,259... | collective-permute-start | bytes 1572872 | tf_op jit(solution)/shard_map/ppermute | solution.py:17
  55.6 51.4 %collective-permute-start.22 = (bf16[1040,256]{1,0:T(8,128)(2,1)S(1)}, bf16[1040,256]{1,0:T(8,128)(2,1)S(1)}, u32[]{:S(2)}, u32[]{:S(2)}) collective-permute-start(bf16[1040,256]{1,0:T(8,128)(2,1)S(1)} %collective-permute-done.1), channel_id=1, source_target_pairs={{442,66},{443,67},{444,68},{445,69},{446,70},{447,71},{384,0},{385... | collective-permute-start | bytes 1597448 | tf_op jit(solution)/shard_map/ppermute | solution.py:17
  99.9 7.7 %collective-permute-start.23 = (bf16[4,256,256]{2,1,0:T(8,128)(2,1)S(1)}, bf16[4,256,256]{2,1,0:T(8,128)(2,1)S(1)}, u32[]{:S(2)}, u32[]{:S(2)}) collective-permute-start(bf16[4,256,256]{2,1,0:T(8,128)(2,1)S(1)} %get-tuple-element.79), channel_id=1, source_target_pairs={{67,68},{68,67},{69,70},{70,69},{71,0},{0,71},{1,2},{2,1},{3,4},{4... | collective-permute-start | bytes 1572872 | tf_op jit(solution)/shard_map/ppermute | solution.py:17
  100.7 7.0 %collective-permute-start.24 = (bf16[4,256,256]{2,1,0:T(8,128)(2,1)S(1)}, bf16[4,256,256]{2,1,0:T(8,128)(2,1)S(1)}, u32[]{:S(2)}, u32[]{:S(2)}) collective-permute-start(bf16[4,256,256]{2,1,0:T(8,128)(2,1)S(1)} %get-tuple-element.80), channel_id=1, source_target_pairs={{67,66},{68,69},{69,68},{70,71},{71,70},{0,1},{1,0},{2,3},{3,2},{4... | collective-permute-start | bytes 1572872 | tf_op jit(solution)/shard_map/ppermute | solution.py:17
  102.9 9.5 %collective-permute-start.27 = (bf16[4,256,256]{2,1,0:T(8,128)(2,1)S(1)}, bf16[4,256,256]{2,1,0:T(8,128)(2,1)S(1)}, u32[]{:S(2)}, u32[]{:S(2)}) collective-permute-start(bf16[4,256,256]{2,1,0:T(8,128)(2,1)S(1)} %get-tuple-element.75.env_ref), channel_id=1, source_target_pairs={{67,379},{68,380},{69,381},{70,382},{71,383},{0,320},{1,321},{2,32... | collective-permute-start | bytes 1572872 | tf_op jit(solution)/shard_map/ppermute | solution.py:17
  107.0 6.7 %collective-permute-start.21 = (bf16[1040,256]{1,0:T(8,128)(2,1)S(1)}, bf16[1040,256]{1,0:T(8,128)(2,1)S(1)}, u32[]{:S(2)}, u32[]{:S(2)}) collective-permute-start(bf16[1040,256]{1,0:T(8,128)(2,1)S(1)} %collective-permute-done.1), channel_id=1, source_target_pairs={{505,65},{506,66},{507,67},{508,68},{509,69},{510,70},{511,71},{44... | collective-permute-start | bytes 1597448 | tf_op jit(solution)/shard_map/ppermute | solution.py:17
  112.4 60.8 %collective-permute-start.30 = (bf16[4,256,256]{2,1,0:T(8,128)(2,1)S(1)}, bf16[4,256,256]{2,1,0:T(8,128)(2,1)S(1)}, u32[]{:S(2)}, u32[]{:S(2)}) collective-permute-start(bf16[4,256,256]{2,1,0:T(8,128)(2,1)S(1)} %get-tuple-element.84.env_ref), channel_id=1, source_target_pairs={{66,442},{67,443},{68,444},{69,445},{70,446},{71,447},{0,384},{1,3... | collective-permute-start | bytes 1572872 | tf_op jit(solution)/shard_map/ppermute | solution.py:17
  115.5 57.7 %collective-permute-start.28 = (bf16[4,256,256]{2,1,0:T(8,128)(2,1)S(1)}, bf16[4,256,256]{2,1,0:T(8,128)(2,1)S(1)}, u32[]{:S(2)}, u32[]{:S(2)}) collective-permute-start(bf16[4,256,256]{2,1,0:T(8,128)(2,1)S(1)} %get-tuple-element.86), channel_id=1, source_target_pairs={{65,66},{66,65},{67,68},{68,67},{69,70},{70,69},{71,0},{0,71},{1,2... | collective-permute-start | bytes 1572872 | tf_op jit(solution)/shard_map/ppermute | solution.py:17
  116.2 57.0 %collective-permute-start.29 = (bf16[4,256,256]{2,1,0:T(8,128)(2,1)S(1)}, bf16[4,256,256]{2,1,0:T(8,128)(2,1)S(1)}, u32[]{:S(2)}, u32[]{:S(2)}) collective-permute-start(bf16[4,256,256]{2,1,0:T(8,128)(2,1)S(1)} %get-tuple-element.87), channel_id=1, source_target_pairs={{65,64},{66,67},{67,66},{68,69},{69,68},{70,71},{71,70},{0,1},{1,0... | collective-permute-start | bytes 1572872 | tf_op jit(solution)/shard_map/ppermute | solution.py:17
  116.9 58.9 %collective-permute-start.33 = (bf16[4,256,256]{2,1,0:T(8,128)(2,1)S(1)}, bf16[4,256,256]{2,1,0:T(8,128)(2,1)S(1)}, u32[]{:S(2)}, u32[]{:S(2)}) collective-permute-start(bf16[4,256,256]{2,1,0:T(8,128)(2,1)S(1)} %get-tuple-element.88.env_ref), channel_id=1, source_target_pairs={{65,448},{66,449},{67,450},{68,451},{69,452},{70,453},{71,454},{0,... | collective-permute-start | bytes 1572872 | tf_op jit(solution)/shard_map/ppermute | solution.py:17
  173.9 17.6 %collective-permute-start.31 = (bf16[4,256,256]{2,1,0:T(8,128)(2,1)S(1)}, bf16[4,256,256]{2,1,0:T(8,128)(2,1)S(1)}, u32[]{:S(2)}, u32[]{:S(2)}) collective-permute-start(bf16[4,256,256]{2,1,0:T(8,128)(2,1)S(1)} %last.1), channel_id=1, source_target_pairs={{64,0},{65,1},{66,2},{67,3},{68,4},{69,5},{70,6},{71,7},{0,8},{1,9... | collective-permute-start | bytes 1572872 | tf_op jit(solution)/shard_map/ppermute | solution.py:17
  (15 other events, 56.3 us)

commit v9 on v8

--- a/solution.py
+++ b/solution.py
@@ -261,40 +261,43 @@
         if early <= ahead < sites:
             parcels[ahead], stay = fetch(ahead, stay)
 
-    resting = [raised[r] for r in range(2, late)]
     ended = pl.pallas_call(
-        functools.partial(last_kernel, len(resting)),
+        functools.partial(last_kernel, 0),
         out_shape=block_shape,
-        in_specs=[SMEM] + [VMEM] * 3 + [ANY] * len(resting),
+        in_specs=[SMEM] + [VMEM] * 3,
         out_specs=VMEM,
         scratch_shapes=[pltpu.SemaphoreType.DMA],
         compiler_params=PARAMS,
         name="last",
-    )(
-        jnp.stack([jnp.maximum(row - 1, 0), fresh_of(sites - 1)]),
-        cross,
-        swap,
-        stay,
-        *resting,
+    )(jnp.stack([jnp.zeros_like(row), fresh_of(sites - 1)]), cross, swap, stay)
+    home = moved(ended, [(device(t - sites), (0, t)) for t in range(sectors)], sectors)
+    raised[late - 1], home, direct[1], direct[late] = lax.optimization_barrier(
+        (raised[late - 1], home, direct[1], direct[late])
     )
-    pairs = [(device(t - sites), (0, t)) for t in range(sectors)]
+    resting = [raised[r] for r in range(2, late)]
+    picked = pl.pallas_call(
+        functools.partial(pick_kernel, len(resting)),
+        out_shape=block_shape,
+        in_specs=[SMEM] + [ANY] * len(resting),
+        out_specs=VMEM,
+        scratch_shapes=[pltpu.SemaphoreType.DMA],
+        compiler_params=PARAMS,
+        name="choose",
+    )(jnp.stack([row - 2]), *resting)
+    pairs = []
     for r in range(2, late):
         pairs += [((r, (t - r) % sectors), (r, t)) for t in range(sectors)]
-    home = moved(ended, pairs, sectors)
+    homeward = moved(picked, pairs, sectors)
+    kind = jnp.where(row == 0, 0, jnp.where(row == 1, 1, jnp.where(row == late, 2, 3)))
     out = pl.pallas_call(
-        functools.partial(pick_kernel, 3),
+        functools.partial(pick_kernel, 4),
         out_shape=block_shape,
-        in_specs=[SMEM, VMEM, ANY, ANY],
+        in_specs=[SMEM, VMEM, ANY, ANY, ANY],
         out_specs=VMEM,
         scratch_shapes=[pltpu.SemaphoreType.DMA],
         compiler_params=PARAMS,
         name="pick",
-    )(
-        jnp.stack([jnp.where(row == 1, 1, jnp.where(row == late, 2, 0))]),
-        home,
-        direct[1],
-        direct[late],
-    )
+    )(jnp.stack([kind]), home, direct[1], direct[late], homeward)
     return out[None, None]
 
 

time: 193 us -> 193 us (level)
  waiting for transfers between devices: 79.7 us -> 71.2 us
  Pallas kernels: 28.1 us -> 33.4 us
  starting transfers between devices: 78.4 us -> 80.9 us
    ppermute x34 -> x35, waiting for transfers between devices: 79.7 us -> 71.2 us  [moved(): return lax.ppermute(x, AXES, flat)]
    ppermute x34 -> x35, starting transfers between devices: 78.4 us -> 80.9 us  [moved(): return lax.ppermute(x, AXES, flat)]
    pallas_call x2 -> x3, Pallas kernels: 1.49 us -> 3.68 us  [the longest x1 1.88 us: local(): pl.pallas_call(functools.partial(pick_kernel, 4), out_shape=block_shape,...]
  transfers between devices with their start and end apart: 34 -> 35, of which waited for: 4 -> 4; matrix products, arithmetic and copies ran while one was open for 0% -> 1% of each run, Pallas kernels for 14% -> 16%
where the time goes in v9:
time: 193 us; the launch traced here: 192 us
  starting transfers between devices  80.9 us (42%)
  waiting for transfers between devices  71.2 us (37%)
  Pallas kernels  33.4 us (17%)
  local copies, waits for them, and re-layouts  3.09 us (2%)
  other arithmetic  2.16 us (1%)
    ppermute x35, starting transfers between devices, moved(): return lax.ppermute(x, AXES, flat)  80.9 us
    ppermute x35, waiting for transfers between devices, moved(): return lax.ppermute(x, AXES, flat)  71.2 us
    pallas_call x8, Pallas kernels, local(): pl.pallas_call(stay_kernel, out_shape=block_shape, in_specs=[SMEM, VMEM,...  13.9 us
    pallas_call x7, Pallas kernels, local(): pl.pallas_call(lead_kernel, out_shape=(block_shape,) * 3, in_specs=[SMEM,...  13.8 us
  transfers between devices with their start and end apart: 35, of which 4 were waited for; matrix products, arithmetic and copies ran while one was open for 1% of the time, Pallas kernels for 16%

profile of v9, /device:TPU:50, one launch (start us, length us, event | category | flops | bytes accessed | tf_op | source)
XLA Modules:
  0.0 191.7 jit_solution(9334955059448332251)
XLA Ops:
  6.5 2.0 %first.1 = (bf16[4,256,256]{2,1,0:T(8,128)(2,1)}, bf16[4,256,256]{2,1,0:T(8,128)(2,1)S(1)}) custom-call(s32[2]{0:T(128)S(1)} %pad_add_fusion.3.p_ref, f32[64]{0:T(128)S(1)} %reshape.15.w_ref, bf16[4,256,256]{2,1,0:T(8,128)(2,1)S(1)} %bitcast.44, bf16[1024,256]{1,0:T(8,128)(2,1)S(1)} %bitcast.41), custom_call_target="tpu_custom_call" | custom-call | flops 536870912 | bytes 2097152 | tf_op jit(solution)/shard_map/first/pallas_call | solution.py:212
  10.1 1.5 stay.8.stay_ref
  13.0 11.9 %collective-permute-start.1 = (bf16[1040,256]{1,0:T(8,128)(2,1)S(1)}, bf16[1040,256]{1,0:T(8,128)(2,1)S(1)}, u32[]{:S(2)}, u32[]{:S(2)}) collective-permute-start(bf16[1040,256]{1,0:T(8,128)(2,1)S(1)} %pad_maximum_fusion), channel_id=1, source_target_pairs={{192,253},{193,254},{194,255},{195,192},{196,193},{197,194},{198,1... | collective-permute-start | bytes 1597448 | tf_op jit(solution)/shard_map/ppermute | solution.py:17
  24.9 2.2 %lead.7 = (bf16[4,256,256]{2,1,0:T(8,128)(2,1)}, bf16[4,256,256]{2,1,0:T(8,128)(2,1)S(1)}, bf16[4,256,256]{2,1,0:T(8,128)(2,1)S(1)}) custom-call(s32[2]{0:T(128)S(1)} %pad_add_fusion.2.p_ref, f32[64]{0:T(128)S(1)} %collective-permute-done.w_ref, bf16[4,256,256]{2,1,0:T(8,128)(2,1)S(1)} %collective-permute-done.3.cross_ref, ...), custom_call_target="tpu_custom_call" | custom-call | flops 536870912 | bytes 3145728 | tf_op jit(solution)/shard_map/lead/pallas_call | solution.py:225
  28.5 2.1 %stay.9.stay_ref = bf16[4,256,256]{2,1,0:T(8,128)(2,1)S(1)} custom-call(f32[64]{0:T(128)S(1)} %collective-permute-done.w_ref, bf16[4,256,256]{2,1,0:T(8,128)(2,1)} %get-tuple-element.60.env_ref, bf16[1024,256]{1,0:T(8,128)(2,1)S(1)} %collective-permute-done.5.a_ref), custom_call_target="tpu_custom_call" | custom-call | flops 10737418240 | bytes 2097152 | tf_op jit(solution)/shard_map/stay/pallas_call | solution.py:240
  30.6 5.6 %collective-permute-done.1 = bf16[1040,256]{1,0:T(8,128)(2,1)S(1)} collective-permute-done((bf16[1040,256]{1,0:T(8,128)(2,1)S(1)}, bf16[1040,256]{1,0:T(8,128)(2,1)S(1)}, u32[]{:S(2)}, u32[]{:S(2)}) %collective-permute-start.1) | collective-permute-done | bytes 532512 | tf_op jit(solution)/shard_map/ppermute | solution.py:17
  37.6 1.7 lead.8
  41.5 1.5 stay.10.stay_ref
  43.8 1.7 lead.9
  46.9 1.5 stay.11.stay_ref
  50.0 1.9 lead.10
  53.3 1.5 stay.12.stay_ref
  55.6 42.9 %collective-permute-start.17 = (bf16[1040,256]{1,0:T(8,128)(2,1)S(1)}, bf16[1040,256]{1,0:T(8,128)(2,1)S(1)}, u32[]{:S(2)}, u32[]{:S(2)}) collective-permute-start(bf16[1040,256]{1,0:T(8,128)(2,1)S(1)} %collective-permute-done.1), channel_id=1, source_target_pairs={{442,66},{443,67},{444,68},{445,69},{446,70},{447,71},{384,0},{385... | collective-permute-start | bytes 1597448 | tf_op jit(solution)/shard_map/ppermute | solution.py:17
  98.5 1.7 lead.11
  101.7 1.5 stay.13.stay_ref
  103.9 3.3 %collective-permute-done.17.a_ref = bf16[1040,256]{1,0:T(8,128)(2,1)S(1)} collective-permute-done((bf16[1040,256]{1,0:T(8,128)(2,1)S(1)}, bf16[1040,256]{1,0:T(8,128)(2,1)S(1)}, u32[]{:S(2)}, u32[]{:S(2)}) %collective-permute-start.17) | collective-permute-done | bytes 532512 | tf_op jit(solution)/shard_map/ppermute | solution.py:17
  108.0 2.2 %lead.12 = (bf16[4,256,256]{2,1,0:T(8,128)(2,1)}, bf16[4,256,256]{2,1,0:T(8,128)(2,1)S(1)}, bf16[4,256,256]{2,1,0:T(8,128)(2,1)S(1)}) custom-call(s32[2]{0:T(128)S(1)} %pad_add_fusion.p_ref, f32[64]{0:T(128)S(1)} %add_bitcast_fusion.2.w_ref, bf16[4,256,256]{2,1,0:T(8,128)(2,1)S(1)} %collective-permute-done.21.cross_ref, ...), custom_call_target="tpu_custom_call" | custom-call | flops 536870912 | bytes 3145728 | tf_op jit(solution)/shard_map/lead/pallas_call | solution.py:225
  111.6 2.1 %stay.14.stay_ref = bf16[4,256,256]{2,1,0:T(8,128)(2,1)S(1)} custom-call(f32[64]{0:T(128)S(1)} %add_bitcast_fusion.2.w_ref, bf16[4,256,256]{2,1,0:T(8,128)(2,1)} %get-tuple-element.85.env_ref, bf16[1040,256]{1,0:T(8,128)(2,1)S(1)} %collective-permute-done.17.a_ref), custom_call_target="tpu_custom_call" | custom-call | flops 10737418240 | bytes 2097152 | tf_op jit(solution)/shard_map/stay/pallas_call | solution.py:240
  115.0 2.2 %lead.13 = (bf16[4,256,256]{2,1,0:T(8,128)(2,1)}, bf16[4,256,256]{2,1,0:T(8,128)(2,1)S(1)}, bf16[4,256,256]{2,1,0:T(8,128)(2,1)S(1)}) custom-call(s32[2]{0:T(128)S(1)} %pad_add_fusion.7.p_ref, f32[64]{0:T(128)S(1)} %add_bitcast_fusion.w_ref, bf16[4,256,256]{2,1,0:T(8,128)(2,1)S(1)} %collective-permute-done.26.cross_ref, ...), custom_call_target="tpu_custom_call" | custom-call | flops 536870912 | bytes 3145728 | tf_op jit(solution)/shard_map/lead/pallas_call | solution.py:225
  120.2 2.0 %stay.15.stay_ref = bf16[4,256,256]{2,1,0:T(8,128)(2,1)S(1)} custom-call(f32[64]{0:T(128)S(1)} %add_bitcast_fusion.w_ref, bf16[4,256,256]{2,1,0:T(8,128)(2,1)} %get-tuple-element.92.env_ref, bf16[1040,256]{1,0:T(8,128)(2,1)S(1)} %collective-permute-done.25.a_ref), custom_call_target="tpu_custom_call" | custom-call | flops 10737418240 | bytes 2097152 | tf_op jit(solution)/shard_map/stay/pallas_call | solution.py:240
  124.5 46.5 %collective-permute-done.24.refs_4_ = bf16[4,256,256]{2,1,0:T(8,128)(2,1)} collective-permute-done((bf16[4,256,256]{2,1,0:T(8,128)(2,1)}, bf16[4,256,256]{2,1,0:T(8,128)(2,1)}, u32[]{:S(2)}, u32[]{:S(2)}) %collective-permute-start.24) | collective-permute-done | bytes 524320 | tf_op jit(solution)/shard_map/ppermute | solution.py:17
  172.1 1.9 %collective-permute-start.34 = (bf16[4,256,256]{2,1,0:T(8,128)(2,1)S(1)}, bf16[4,256,256]{2,1,0:T(8,128)(2,1)S(1)}, u32[]{:S(2)}, u32[]{:S(2)}) collective-permute-start(bf16[4,256,256]{2,1,0:T(8,128)(2,1)S(1)} %choose.1), channel_id=1, source_target_pairs={{190,128},{191,129},{128,130},{129,131},{130,132},{131,133},{132,1... | collective-permute-start | bytes 1572872 | tf_op jit(solution)/shard_map/ppermute | solution.py:17
  174.0 15.6 %collective-permute-done.34.refs_3_ = bf16[4,256,256]{2,1,0:T(8,128)(2,1)S(1)} collective-permute-done((bf16[4,256,256]{2,1,0:T(8,128)(2,1)S(1)}, bf16[4,256,256]{2,1,0:T(8,128)(2,1)S(1)}, u32[]{:S(2)}, u32[]{:S(2)}) %collective-permute-start.34) | collective-permute-done | bytes 524320 | tf_op jit(solution)/shard_map/ppermute | solution.py:17
  189.6 1.9 pick.1
  (101 shorter events, 31.4 us)
Async XLA Ops:
  0.0 24.9 %collective-permute-start.5 = (bf16[1024,256]{1,0:T(8,128)(2,1)}, bf16[1024,256]{1,0:T(8,128)(2,1)S(1)}, u32[]{:S(2)}, u32[]{:S(2)}) collective-permute-start(bf16[1024,256]{1,0:T(8,128)(2,1)} %bitcast.39), channel_id=1, source_target_pairs={{64,71},{65,0},{66,1},{67,2},{68,3},{69,4},{70,5},{71,6},{72,7},{7... | collective-permute-start | bytes 1572872 | tf_op jit(solution)/shard_map/ppermute | solution.py:17
  0.7 36.9 %collective-permute-start.8 = (bf16[1024,256]{1,0:T(8,128)(2,1)}, bf16[1024,256]{1,0:T(8,128)(2,1)S(1)}, u32[]{:S(2)}, u32[]{:S(2)}) collective-permute-start(bf16[1024,256]{1,0:T(8,128)(2,1)} %bitcast.40), channel_id=1, source_target_pairs={{128,70},{129,71},{130,0},{131,1},{132,2},{133,3},{134,4},{135,5},... | collective-permute-start | bytes 1572872 | tf_op jit(solution)/shard_map/ppermute | solution.py:17
  3.0 9.2 %collective-permute-start = (f32[64]{0:T(128)S(1)}, f32[64]{0:T(128)S(1)}, u32[]{:S(2)}, u32[]{:S(2)}) collective-permute-start(f32[64]{0:T(128)S(1)} %reshape.15.w_ref), channel_id=1, source_target_pairs={{64,71},{65,0},{66,1},{67,2},{68,3},{69,4},{70,5},{71,6},{72,7},{7... | collective-permute-start | bytes 776 | tf_op jit(solution)/shard_map/ppermute | solution.py:17
  3.6 33.3 %collective-permute-start.2 = (f32[64]{0:T(128)S(1)}, f32[64]{0:T(128)S(1)}, u32[]{:S(2)}, u32[]{:S(2)}) collective-permute-start(f32[64]{0:T(128)S(1)} %reshape.15.w_ref), channel_id=1, source_target_pairs={{128,70},{129,71},{130,0},{131,1},{132,2},{133,3},{134,4},{135,5},... | collective-permute-start | bytes 776 | tf_op jit(solution)/shard_map/ppermute | solution.py:17
  12.2 12.7 %collective-permute-start.4 = (bf16[4,256,256]{2,1,0:T(8,128)(2,1)}, bf16[4,256,256]{2,1,0:T(8,128)(2,1)S(1)}, u32[]{:S(2)}, u32[]{:S(2)}) collective-permute-start(bf16[4,256,256]{2,1,0:T(8,128)(2,1)} %copy-done.4), channel_id=1, source_target_pairs={{0,1},{1,0},{2,3},{3,2},{4,5},{5,4},{6,7},{7,6},{8,9},{9,8},{10,11... | collective-permute-start | bytes 1572872 | tf_op jit(solution)/shard_map/ppermute | solution.py:17
  13.0 23.2 %collective-permute-start.1 = (bf16[1040,256]{1,0:T(8,128)(2,1)S(1)}, bf16[1040,256]{1,0:T(8,128)(2,1)S(1)}, u32[]{:S(2)}, u32[]{:S(2)}) collective-permute-start(bf16[1040,256]{1,0:T(8,128)(2,1)S(1)} %pad_maximum_fusion), channel_id=1, source_target_pairs={{192,253},{193,254},{194,255},{195,192},{196,193},{197,194},{198,1... | collective-permute-start | bytes 1597448 | tf_op jit(solution)/shard_map/ppermute | solution.py:17
  27.1 10.5 %collective-permute-start.6 = (bf16[4,256,256]{2,1,0:T(8,128)(2,1)S(1)}, bf16[4,256,256]{2,1,0:T(8,128)(2,1)S(1)}, u32[]{:S(2)}, u32[]{:S(2)}) collective-permute-start(bf16[4,256,256]{2,1,0:T(8,128)(2,1)S(1)} %get-tuple-element.58), channel_id=1, source_target_pairs={{71,0},{0,71},{1,2},{2,1},{3,4},{4,3},{5,6},{6,5},{7,8},{8,7},{9,1... | collective-permute-start | bytes 1572872 | tf_op jit(solution)/shard_map/ppermute | solution.py:17
  27.8 9.8 %collective-permute-start.7 = (bf16[4,256,256]{2,1,0:T(8,128)(2,1)S(1)}, bf16[4,256,256]{2,1,0:T(8,128)(2,1)S(1)}, u32[]{:S(2)}, u32[]{:S(2)}) collective-permute-start(bf16[4,256,256]{2,1,0:T(8,128)(2,1)S(1)} %get-tuple-element.59), channel_id=1, source_target_pairs={{71,70},{0,1},{1,0},{2,3},{3,2},{4,5},{5,4},{6,7},{7,6},{8,9},{9,8... | collective-permute-start | bytes 1572872 | tf_op jit(solution)/shard_map/ppermute | solution.py:17
  36.2 88.3 %collective-permute-start.32 = (bf16[4,256,256]{2,1,0:T(8,128)(2,1)}, bf16[4,256,256]{2,1,0:T(8,128)(2,1)S(1)}, u32[]{:S(2)}, u32[]{:S(2)}) collective-permute-start(bf16[4,256,256]{2,1,0:T(8,128)(2,1)} %get-tuple-element.60.env_ref), channel_id=1, source_target_pairs={{71,64},{0,65},{1,66},{2,67},{3,68},{4,69},{5,70},{6,71},{7,72},{8... | collective-permute-start | bytes 1572872 | tf_op jit(solution)/shard_map/ppermute | solution.py:17
  40.8 7.7 %collective-permute-start.15 = (bf16[4,256,256]{2,1,0:T(8,128)(2,1)S(1)}, bf16[4,256,256]{2,1,0:T(8,128)(2,1)S(1)}, u32[]{:S(2)}, u32[]{:S(2)}) collective-permute-start(bf16[4,256,256]{2,1,0:T(8,128)(2,1)S(1)} %get-tuple-element.62.env_ref), channel_id=1, source_target_pairs={{70,190},{71,191},{0,128},{1,129},{2,130},{3,131},{4,132},{5,133},... | collective-permute-start | bytes 1572872 | tf_op jit(solution)/shard_map/ppermute | solution.py:17
  48.5 6.3 %collective-permute-start.16 = (bf16[4,256,256]{2,1,0:T(8,128)(2,1)S(1)}, bf16[4,256,256]{2,1,0:T(8,128)(2,1)S(1)}, u32[]{:S(2)}, u32[]{:S(2)}) collective-permute-start(bf16[4,256,256]{2,1,0:T(8,128)(2,1)S(1)} %get-tuple-element.70.env_ref), channel_id=1, source_target_pairs={{69,253},{70,254},{71,255},{0,192},{1,193},{2,194},{3,195},{4,196}... | collective-permute-start | bytes 1572872 | tf_op jit(solution)/shard_map/ppermute | solution.py:17
  49.2 6.3 %collective-permute-start.18 = (bf16[1040,256]{1,0:T(8,128)(2,1)S(1)}, bf16[1040,256]{1,0:T(8,128)(2,1)S(1)}, u32[]{:S(2)}, u32[]{:S(2)}) collective-permute-start(bf16[1040,256]{1,0:T(8,128)(2,1)S(1)} %collective-permute-done.1), channel_id=1, source_target_pairs={{379,67},{380,68},{381,69},{382,70},{383,71},{320,0},{321,1},{322,... | collective-permute-start | bytes 1597448 | tf_op jit(solution)/shard_map/ppermute | solution.py:17
  51.9 46.6 %collective-permute-start.19 = (bf16[4,256,256]{2,1,0:T(8,128)(2,1)S(1)}, bf16[4,256,256]{2,1,0:T(8,128)(2,1)S(1)}, u32[]{:S(2)}, u32[]{:S(2)}) collective-permute-start(bf16[4,256,256]{2,1,0:T(8,128)(2,1)S(1)} %get-tuple-element.77), channel_id=1, source_target_pairs={{68,67},{69,70},{70,69},{71,0},{0,71},{1,2},{2,1},{3,4},{4,3},{5,6... | collective-permute-start | bytes 1572872 | tf_op jit(solution)/shard_map/ppermute | solution.py:17
  52.6 45.9 %collective-permute-start.20 = (bf16[4,256,256]{2,1,0:T(8,128)(2,1)S(1)}, bf16[4,256,256]{2,1,0:T(8,128)(2,1)S(1)}, u32[]{:S(2)}, u32[]{:S(2)}) collective-permute-start(bf16[4,256,256]{2,1,0:T(8,128)(2,1)S(1)} %get-tuple-element.78), channel_id=1, source_target_pairs={{68,69},{69,68},{70,71},{71,70},{0,1},{1,0},{2,3},{3,2},{4,5},{5,4... | collective-permute-start | bytes 1572872 | tf_op jit(solution)/shard_map/ppermute | solution.py:17
  54.8 48.4 %collective-permute-start.23 = (bf16[4,256,256]{2,1,0:T(8,128)(2,1)S(1)}, bf16[4,256,256]{2,1,0:T(8,128)(2,1)S(1)}, u32[]{:S(2)}, u32[]{:S(2)}) collective-permute-start(bf16[4,256,256]{2,1,0:T(8,128)(2,1)S(1)} %get-tuple-element.73.env_ref), channel_id=1, source_target_pairs={{68,316},{69,317},{70,318},{71,319},{0,256},{1,257},{2,258},{3,259... | collective-permute-start | bytes 1572872 | tf_op jit(solution)/shard_map/ppermute | solution.py:17
  55.6 51.7 %collective-permute-start.17 = (bf16[1040,256]{1,0:T(8,128)(2,1)S(1)}, bf16[1040,256]{1,0:T(8,128)(2,1)S(1)}, u32[]{:S(2)}, u32[]{:S(2)}) collective-permute-start(bf16[1040,256]{1,0:T(8,128)(2,1)S(1)} %collective-permute-done.1), channel_id=1, source_target_pairs={{442,66},{443,67},{444,68},{445,69},{446,70},{447,71},{384,0},{385... | collective-permute-start | bytes 1597448 | tf_op jit(solution)/shard_map/ppermute | solution.py:17
  100.2 7.7 %collective-permute-start.21 = (bf16[4,256,256]{2,1,0:T(8,128)(2,1)S(1)}, bf16[4,256,256]{2,1,0:T(8,128)(2,1)S(1)}, u32[]{:S(2)}, u32[]{:S(2)}) collective-permute-start(bf16[4,256,256]{2,1,0:T(8,128)(2,1)S(1)} %get-tuple-element.80), channel_id=1, source_target_pairs={{67,68},{68,67},{69,70},{70,69},{71,0},{0,71},{1,2},{2,1},{3,4},{4... | collective-permute-start | bytes 1572872 | tf_op jit(solution)/shard_map/ppermute | solution.py:17
  100.9 7.0 %collective-permute-start.22 = (bf16[4,256,256]{2,1,0:T(8,128)(2,1)S(1)}, bf16[4,256,256]{2,1,0:T(8,128)(2,1)S(1)}, u32[]{:S(2)}, u32[]{:S(2)}) collective-permute-start(bf16[4,256,256]{2,1,0:T(8,128)(2,1)S(1)} %get-tuple-element.81), channel_id=1, source_target_pairs={{67,66},{68,69},{69,68},{70,71},{71,70},{0,1},{1,0},{2,3},{3,2},{4... | collective-permute-start | bytes 1572872 | tf_op jit(solution)/shard_map/ppermute | solution.py:17
  103.2 10.5 %collective-permute-start.28 = (bf16[4,256,256]{2,1,0:T(8,128)(2,1)S(1)}, bf16[4,256,256]{2,1,0:T(8,128)(2,1)S(1)}, u32[]{:S(2)}, u32[]{:S(2)}) collective-permute-start(bf16[4,256,256]{2,1,0:T(8,128)(2,1)S(1)} %get-tuple-element.82.env_ref), channel_id=1, source_target_pairs={{67,379},{68,380},{69,381},{70,382},{71,383},{0,320},{1,321},{2,32... | collective-permute-start | bytes 1572872 | tf_op jit(solution)/shard_map/ppermute | solution.py:17
  107.2 7.7 %collective-permute-start.25 = (bf16[1040,256]{1,0:T(8,128)(2,1)S(1)}, bf16[1040,256]{1,0:T(8,128)(2,1)S(1)}, u32[]{:S(2)}, u32[]{:S(2)}) collective-permute-start(bf16[1040,256]{1,0:T(8,128)(2,1)S(1)} %collective-permute-done.1), channel_id=1, source_target_pairs={{505,65},{506,66},{507,67},{508,68},{509,69},{510,70},{511,71},{44... | collective-permute-start | bytes 1597448 | tf_op jit(solution)/shard_map/ppermute | solution.py:17
  113.7 57.3 %collective-permute-start.24 = (bf16[4,256,256]{2,1,0:T(8,128)(2,1)}, bf16[4,256,256]{2,1,0:T(8,128)(2,1)}, u32[]{:S(2)}, u32[]{:S(2)}) collective-permute-start(bf16[4,256,256]{2,1,0:T(8,128)(2,1)} %get-tuple-element.85.env_ref), channel_id=1, source_target_pairs={{66,442},{67,443},{68,444},{69,445},{70,446},{71,447},{0,384},{1,3... | collective-permute-start | bytes 1572872 | tf_op jit(solution)/shard_map/ppermute | solution.py:17
  118.7 52.3 %collective-permute-start.33 = (bf16[4,256,256]{2,1,0:T(8,128)(2,1)}, bf16[4,256,256]{2,1,0:T(8,128)(2,1)}, u32[]{:S(2)}, u32[]{:S(2)}) collective-permute-start(bf16[4,256,256]{2,1,0:T(8,128)(2,1)} %get-tuple-element.92.env_ref), channel_id=1, source_target_pairs={{65,448},{66,449},{67,450},{68,451},{69,452},{70,453},{71,454},{0,... | collective-permute-start | bytes 1572872 | tf_op jit(solution)/shard_map/ppermute | solution.py:17
  123.0 48.0 %collective-permute-start.31 = (bf16[4,256,256]{2,1,0:T(8,128)(2,1)S(1)}, bf16[4,256,256]{2,1,0:T(8,128)(2,1)}, u32[]{:S(2)}, u32[]{:S(2)}) collective-permute-start(bf16[4,256,256]{2,1,0:T(8,128)(2,1)S(1)} %last.1), channel_id=1, source_target_pairs={{64,0},{65,1},{66,2},{67,3},{68,4},{69,5},{70,6},{71,7},{0,8},{1,9... | collective-permute-start | bytes 1572872 | tf_op jit(solution)/shard_map/ppermute | solution.py:17
  172.1 17.6 %collective-permute-start.34 = (bf16[4,256,256]{2,1,0:T(8,128)(2,1)S(1)}, bf16[4,256,256]{2,1,0:T(8,128)(2,1)S(1)}, u32[]{:S(2)}, u32[]{:S(2)}) collective-permute-start(bf16[4,256,256]{2,1,0:T(8,128)(2,1)S(1)} %choose.1), channel_id=1, source_target_pairs={{190,128},{191,129},{128,130},{129,131},{130,132},{131,133},{132,1... | collective-permute-start | bytes 1572872 | tf_op jit(solution)/shard_map/ppermute | solution.py:17
  (16 other events, 60.2 us)
